TPU v7x, 256 devices: a whole 4x4x8 slice. The times are simulated.
256 devices in a mesh: roll: 8 (over z), pipe: 2 (over core), tp: 16 (over y, x).
Axes of the slice: x: 4, y: 4, z: 8, core: 2. Of those that a mesh axis runs over, the one named last changes fastest.
Arguments:
- ssm_state: bfloat16 [2, 128, 128, 64, 128], P('pipe', 'roll', 'tp'), may hold values from -6 to 6
- conv_window: bfloat16 [2, 128, 3, 8192], P('pipe', 'roll', None, 'tp'), may hold values from -6 to 6
- x_in: bfloat16 [4, 128, 8192], P(None, 'roll', 'tp'), may hold values from -6 to 6
- z_gate: bfloat16 [2, 4, 128, 8192], P('pipe', None, 'roll', 'tp'), may hold values from -6 to 6
- dt_raw: float32 [2, 4, 128, 128], P('pipe', None, 'roll', 'tp'), may hold values from -3 to 3
- b_in: bfloat16 [2, 4, 128, 128], P('pipe', None, 'roll'), may hold values from -6 to 6
- c_in: bfloat16 [2, 4, 128, 128], P('pipe', None, 'roll'), may hold values from -0.5 to 0.5
- conv_weight: bfloat16 [2, 4, 8192], P('pipe', None, 'tp'), may hold values from -3 to 3
- a_log: float32 [2, 128], P('pipe', 'tp'), may hold values from 0 to 2.8
- dt_bias: float32 [2, 128], P('pipe', 'tp'), may hold values from -4 to -1
- skip_d: float32 [2, 128], P('pipe', 'tp'), may hold values from 0.5 to 1.5
- norm_gain: float32 [2, 8192], P('pipe', 'tp'), may hold values from 0.5 to 1.5
- parent: int32 [128], replicated, may hold values from 0 to 127, as said below
Outputs:
- layer_out: bfloat16 [2, 4, 128, 8192], P('pipe', None, 'roll', 'tp')
Inputs may be any that keep to these rules, and one draw needn't show every extreme that they name: Slot s's parent lies in the same aligned block of 16 slots as s or in the block just before; every block but the first has exactly 1 slot whose parent lies in the block before, the first has none.
All inputs are finite; a program needn't handle non-finite values.
Results may differ from a plain program's by a relative error of at most 0.003.
Values may be sent and summed in bfloat16 or wider, within the bound.
No kernel may reach another device: no remote copies, remote signals or barrier semaphores. Data moves between devices by JAX's collectives and lax.ppermute only.
A program may use at most 64 MiB of HBM per device.

v0:
```python
import jax
import jax.numpy as jnp
from jax import lax
from jax.sharding import PartitionSpec as P


def passed_along(value, axis, steps):
    count = lax.axis_size(axis)
    initial, last = (max(0, -steps), min(count, count - steps))
    return lax.ppermute(value, axis, [(source, source + steps) for source in range(initial, last)])


def recurrence(hstate, window, x_row, step, layer_data):
    z_all, dt_all, b_all, c_all, taps, a_log, dt_bias, skip_d, gain = layer_data
    z_row = lax.dynamic_index_in_dim(z_all, step, 0, keepdims=False)
    dt_row = lax.dynamic_index_in_dim(dt_all, step, 0, keepdims=False)
    b_row = lax.dynamic_index_in_dim(b_all, step, 0, keepdims=False).astype(jnp.float32)
    c_row = lax.dynamic_index_in_dim(c_all, step, 0, keepdims=False).astype(jnp.float32)
    slots, heads = dt_row.shape
    stacked = jnp.concatenate([window, x_row[:, None, :]], axis=1).astype(jnp.float32)
    xc = jax.nn.silu(jnp.sum(stacked * taps.astype(jnp.float32)[None], axis=1))
    delta = jax.nn.softplus(dt_row + dt_bias[None, :])
    decay = jnp.exp(-delta * jnp.exp(a_log)[None, :])
    x_heads = xc.reshape(slots, heads, -1)
    hstate = (
        decay[:, :, None, None] * hstate
        + (delta[:, :, None] * x_heads)[:, :, :, None] * b_row[:, None, None, :]
    )
    y_heads = (
        jnp.einsum("shpn,sn->shp", hstate, c_row, precision=lax.Precision.HIGHEST)
        + skip_d[None, :, None] * x_heads
    )
    gated = y_heads.reshape(slots, -1) * jax.nn.silu(z_row.astype(jnp.float32))
    window = jnp.concatenate([window[:, 1:], x_row[:, None, :]], axis=1)
    return (hstate, window, gated)


def normalize(gated, totals, gain):
    mean_sq = totals / (gated.shape[-1] * lax.axis_size("tp"))
    return (gated * lax.rsqrt(mean_sq + 1e-05)[..., None] * gain).astype(jnp.bfloat16)


def decode_step(hstate, window, x_row, step, layer_data):
    hstate, window, gated = recurrence(hstate, window, x_row, step, layer_data)
    totals = lax.psum(jnp.sum(gated * gated, axis=1), "tp")
    output = normalize(gated, totals, layer_data[8][None, :])
    return (hstate, window, output)


def body(
    ssm_state,
    conv_window,
    x_in,
    z_gate,
    dt_raw,
    b_in,
    c_in,
    conv_weight,
    a_log,
    dt_bias,
    skip_d,
    norm_gain,
    parent,
):
    slots = ssm_state.shape[1]
    base = lax.axis_index("roll") * slots
    own_state = ssm_state[0]
    own_window = conv_window[0]
    own_parent = lax.dynamic_slice_in_dim(parent, base, slots)
    local = own_parent - base
    from_own_state = jnp.take(own_state, jnp.clip(local, 0, slots - 1), axis=0)
    from_own_window = jnp.take(own_window, jnp.clip(local, 0, slots - 1), axis=0)
    prev_state, prev_window = passed_along((own_state, own_window), "roll", 1)
    prev_index = jnp.clip(local + slots, 0, slots - 1)
    outside = local < 0
    start_state = jnp.where(
        outside[:, None, None, None], jnp.take(prev_state, prev_index, axis=0), from_own_state
    )
    start_window = jnp.where(
        outside[:, None, None], jnp.take(prev_window, prev_index, axis=0), from_own_window
    )
    hstart = start_state.astype(jnp.float32)
    layer_data = (
        z_gate[0],
        dt_raw[0],
        b_in[0],
        c_in[0],
        conv_weight[0],
        a_log[0],
        dt_bias[0],
        skip_d[0],
        norm_gain[0],
    )
    section = lax.axis_index("pipe")
    steps = x_in.shape[0]

    def run_layer(inputs):
        hstate, window = (hstart, start_window)
        results = []
        for step in range(steps):
            hstate, window, output = decode_step(hstate, window, inputs[step], step, layer_data)
            results.append(output)
        return jnp.stack(results)

    first = run_layer(x_in)
    arrived = passed_along(first, "pipe", 1)
    second = run_layer(arrived)
    result = jnp.where(section == 0, first, second)
    return result[None]


def solution(mesh):
    in_specs = (
        P("pipe", "roll", "tp", None, None),
        P("pipe", "roll", None, "tp"),
        P(None, "roll", "tp"),
        P("pipe", None, "roll", "tp"),
        P("pipe", None, "roll", "tp"),
        P("pipe", None, "roll", None),
        P("pipe", None, "roll", None),
        P("pipe", None, "tp"),
        P("pipe", "tp"),
        P("pipe", "tp"),
        P("pipe", "tp"),
        P("pipe", "tp"),
        P(),
    )
    out_specs = P("pipe", None, "roll", "tp")
    return jax.shard_map(body, mesh=mesh, in_specs=in_specs, out_specs=out_specs, check_vma=False)
```

profile of v0, /device:TPU:98, one launch (start us, length us, event | category | flops | bytes accessed | tf_op | source)
XLA Modules:
  0.0 209.4 jit_solution(13504139270830162561)
XLA Ops:
  0.0 0.8 copy.168
  0.8 5.0 %collective-permute-start.1 = (bf16[16,3,512]{2,1,0:T(4,128)(2,1)S(1)}, bf16[16,3,512]{2,1,0:T(4,128)(2,1)S(1)}, u32[]{:S(2)}, u32[]{:S(2)}) collective-permute-start(bf16[16,3,512]{2,1,0:T(4,128)(2,1)S(1)} %bitcast.178), channel_id=1, source_target_pairs={{0,32},{32,64},{64,96},{96,128},{128,160},{160,192},{192,224},{1,3... | collective-permute-start | bytes 147464 | tf_op jit(solution)/shard_map/ppermute | solution.py:10
  5.9 2.9 %collective-permute-start = (bf16[16,8,64,128]{3,2,1,0:T(8,128)(2,1)}, bf16[16,8,64,128]{3,2,1,0:T(8,128)(2,1)}, u32[]{:S(2)}, u32[]{:S(2)}) collective-permute-start(bf16[16,8,64,128]{3,2,1,0:T(8,128)(2,1)} %bitcast.176), channel_id=1, source_target_pairs={{0,32},{32,64},{64,96},{96,128},{128,160},{160,192},{192,224},{1,3... | collective-permute-start | bytes 6291464 | tf_op jit(solution)/shard_map/ppermute | solution.py:10
  10.2 0.7 bitcast_convert_fusion.3
  10.9 0.7 slice_bitcast_fusion.11
  11.7 0.7 broadcast_compare_fusion
  12.4 0.8 multiply_exponential_fusion.3
  13.3 0.8 slice_bitcast_fusion.5
  14.0 0.8 slice_convert_fusion.3
  15.5 2.5 %gather_fusion.1 = bf16[16,8,64,128]{3,2,1,0:T(8,128)(2,1)S(1)} fusion(bf16[16,8,64,128]{3,2,1,0:T(8,128)(2,1)} %bitcast.177, s32[1024]{0:T(1024)S(1)} %get-tuple-element.109), kind=kCustom, calls=%fused_computation.2.clone | custom fusion | bytes 4194368 | tf_op jit(solution)/shard_map/jit(_take)/gather | solution.py:71
  21.3 33.9 %collective-permute-done = bf16[16,8,64,128]{3,2,1,0:T(8,128)(2,1)} collective-permute-done((bf16[16,8,64,128]{3,2,1,0:T(8,128)(2,1)}, bf16[16,8,64,128]{3,2,1,0:T(8,128)(2,1)}, u32[]{:S(2)}, u32[]{:S(2)}) %collective-permute-start) | collective-permute-done | bytes 2097184 | tf_op jit(solution)/shard_map/ppermute | solution.py:10
  55.2 3.7 %gather_fusion = bf16[16,8,64,128]{3,2,1,0:T(8,128)(2,1)} fusion(bf16[16,8,64,128]{3,2,1,0:T(8,128)(2,1)} %collective-permute-done, s32[1024]{0:T(1024)S(1)} %get-tuple-element.110), kind=kCustom, calls=%fused_computation.clone | custom fusion | bytes 4194368 | tf_op jit(solution)/shard_map/jit(_take)/gather | solution.py:77
  58.9 2.0 select_select_fusion
  60.9 5.7 %fusion.8 = f32[16,1,8,64]{3,1,2,0:T(1,128)S(1)} fusion(bf16[16,8,64,128]{3,2,1,0:T(8,128)(2,1)S(1)} %select_select_fusion, f32[16,128]{1,0:T(8,128)S(1)} %get-tuple-element.91, f32[16,8,64]{2,1,0:T(8,128)S(1)} %broadcast_multiply_fusion.7, f32[16,8]{1,0:T(8,128)S(1)} %copy.112, bf16[16,128,1,1]{1,0,2,3:T(8,128)(2,1)S(1)} %get-tuple-element.87), kind=kOutput, calls=%fused_computation.19 | convolution fusion | flops 16777216 | bytes 2175488 | tf_op jit(solution)/shard_map/shpn,sn->shp/dot_general | solution.py:30
  66.6 7.2 %fusion.10 = f32[16,1,8,64]{3,1,2,0:T(1,128)S(1)} fusion(bf16[16,8,64,128]{3,2,1,0:T(8,128)(2,1)S(1)} %select_select_fusion, f32[16,128]{1,0:T(8,128)S(1)} %get-tuple-element.92, f32[16,8,64]{2,1,0:T(8,128)S(1)} %broadcast_multiply_fusion.5, f32[16,8]{1,0:T(8,128)S(1)} %copy.116, f32[16,128]{1,0:T(8,128)S(1)} %get-tuple-element.91, ...), kind=kOutput, calls=%fused_computation.21 | convolution fusion | flops 19922944 | bytes 2216960 | tf_op jit(solution)/shard_map/shpn,sn->shp/dot_general | solution.py:30
  73.8 8.4 %fusion.12 = f32[16,1,8,64]{3,1,2,0:T(1,128)S(1)} fusion(bf16[16,8,64,128]{3,2,1,0:T(8,128)(2,1)S(1)} %select_select_fusion, f32[16,128]{1,0:T(8,128)S(1)} %get-tuple-element.94, f32[16,8,64]{2,1,0:T(8,128)S(1)} %broadcast_multiply_fusion.3, f32[16,8]{1,0:T(8,128)S(1)} %copy.120, f32[16,128]{1,0:T(8,128)S(1)} %get-tuple-element.92, ...), kind=kOutput, calls=%fused_computation.23 | convolution fusion | flops 23068672 | bytes 2258432 | tf_op jit(solution)/shard_map/shpn,sn->shp/dot_general | solution.py:30
  82.3 11.4 %fusion.4 = f32[16,1,8,64]{3,1,2,0:T(1,128)S(1)} fusion(bf16[16,8,64,128]{3,2,1,0:T(8,128)(2,1)S(1)} %select_select_fusion, f32[16,128]{1,0:T(8,128)S(1)} %get-tuple-element.93, f32[16,8,64]{2,1,0:T(8,128)S(1)} %broadcast_multiply_fusion.1, f32[16,8]{1,0:T(8,128)S(1)} %copy.125, f32[16,128]{1,0:T(8,128)S(1)} %get-tuple-element.94, ...), kind=kOutput, calls=%fused_computation.11 | convolution fusion | flops 26214400 | bytes 2299904 | tf_op jit(solution)/shard_map/shpn,sn->shp/dot_general | solution.py:30
  94.1 36.8 %all-reduce.1 = (f32[16]{0:T(128)S(1)}, f32[16]{0:T(128)S(1)}, f32[16]{0:T(128)S(1)}, f32[16]{0:T(128)S(1)}) all-reduce(f32[16]{0:T(128)S(1)} %get-tuple-element.105, f32[16]{0:T(128)S(1)} %get-tuple-element.103, f32[16]{0:T(128)S(1)} %get-tuple-element.101, ...), channel_id=1, replica_groups=mesh['roll'=8,'pipe'=2,'tp'=16] {'tp'}, use_global_device_ids=true, to_apply=%region_11.14 | all-reduce | flops 64 | bytes 512 | tf_op jit(solution)/shard_map/psum | solution.py:45
  131.3 1.3 collective-permute-start.2
  135.2 5.7 %fusion.9 = f32[16,1,8,64]{3,1,2,0:T(1,128)S(1)} fusion(bf16[16,8,64,128]{3,2,1,0:T(8,128)(2,1)S(1)} %copy-done.1, f32[16,8,64]{2,1,0:T(8,128)S(1)} %broadcast_multiply_fusion.6, f32[16,128]{1,0:T(8,128)S(1)} %get-tuple-element.91, f32[16,8]{1,0:T(8,128)S(1)} %copy.112, bf16[16,128,1,1]{1,0,2,3:T(8,128)(2,1)S(1)} %get-tuple-element.87), kind=kOutput, calls=%fused_computation.20 | convolution fusion | flops 16777216 | bytes 2175488 | tf_op jit(solution)/shard_map/shpn,sn->shp/dot_general | solution.py:30
  140.8 7.2 %fusion.11 = f32[16,1,8,64]{3,1,2,0:T(1,128)S(1)} fusion(bf16[16,8,64,128]{3,2,1,0:T(8,128)(2,1)S(1)} %copy-done.1, f32[16,8,64]{2,1,0:T(8,128)S(1)} %broadcast_multiply_fusion.4, f32[16,8,64]{2,1,0:T(8,128)S(1)} %broadcast_multiply_fusion.6, f32[16,128]{1,0:T(8,128)S(1)} %get-tuple-element.92, f32[16,8]{1,0:T(8,128)S(1)} %copy.116, ...), kind=kOutput, calls=%fused_computation.22 | convolution fusion | flops 19922944 | bytes 2216960 | tf_op jit(solution)/shard_map/shpn,sn->shp/dot_general | solution.py:30
  148.1 8.4 %fusion.13 = f32[16,1,8,64]{3,1,2,0:T(1,128)S(1)} fusion(bf16[16,8,64,128]{3,2,1,0:T(8,128)(2,1)S(1)} %copy-done.1, f32[16,8,64]{2,1,0:T(8,128)S(1)} %broadcast_multiply_fusion.2, f32[16,8,64]{2,1,0:T(8,128)S(1)} %broadcast_multiply_fusion.4, f32[16,8,64]{2,1,0:T(8,128)S(1)} %broadcast_multiply_fusion.6, f32[16,128]{1,0:T(8,128)S(1)} %get-tuple-element.94, ...), kind=kOutput, calls=%fused_computation.24 | convolution fusion | flops 23068672 | bytes 2258432 | tf_op jit(solution)/shard_map/shpn,sn->shp/dot_general | solution.py:30
  156.5 11.4 %fusion = f32[16,1,8,64]{3,1,2,0:T(1,128)S(1)} fusion(bf16[16,8,64,128]{3,2,1,0:T(8,128)(2,1)S(1)} %copy-done.1, f32[16,8,64]{2,1,0:T(8,128)S(1)} %broadcast_multiply_fusion, f32[16,8,64]{2,1,0:T(8,128)S(1)} %broadcast_multiply_fusion.2, f32[16,8,64]{2,1,0:T(8,128)S(1)} %broadcast_multiply_fusion.4, f32[16,8,64]{2,1,0:T(8,128)S(1)} %broadcast_multiply_fusion.6, ...), kind=kOutput, calls=%fused_computation.4 | convolution fusion | flops 26214400 | bytes 2299904 | tf_op jit(solution)/shard_map/shpn,sn->shp/dot_general | solution.py:30
  168.3 40.0 %all-reduce = (f32[16]{0:T(128)S(1)}, f32[16]{0:T(128)S(1)}, f32[16]{0:T(128)S(1)}, f32[16]{0:T(128)S(1)}) all-reduce(f32[16]{0:T(128)S(1)} %get-tuple-element.99, f32[16]{0:T(128)S(1)} %get-tuple-element.97, f32[16]{0:T(128)S(1)} %get-tuple-element.95, f32[16]{0:T(128)S(1)} %get-tuple-element.27), channel_id=1, replica_groups=mesh['roll'=8,'pipe'=2,'tp'=16] {'tp'}, use_global_device_ids=true, to_apply=%region_23.26 | all-reduce | flops 64 | bytes 512 | tf_op jit(solution)/shard_map/psum | solution.py:45
  (88 shorter events, 10.0 us)
Async XLA Ops:
  0.8 18.2 %collective-permute-start.1 = (bf16[16,3,512]{2,1,0:T(4,128)(2,1)S(1)}, bf16[16,3,512]{2,1,0:T(4,128)(2,1)S(1)}, u32[]{:S(2)}, u32[]{:S(2)}) collective-permute-start(bf16[16,3,512]{2,1,0:T(4,128)(2,1)S(1)} %bitcast.178), channel_id=1, source_target_pairs={{0,32},{32,64},{64,96},{96,128},{128,160},{160,192},{192,224},{1,3... | collective-permute-start | bytes 147464 | tf_op jit(solution)/shard_map/ppermute | solution.py:10
  5.9 49.3 %collective-permute-start = (bf16[16,8,64,128]{3,2,1,0:T(8,128)(2,1)}, bf16[16,8,64,128]{3,2,1,0:T(8,128)(2,1)}, u32[]{:S(2)}, u32[]{:S(2)}) collective-permute-start(bf16[16,8,64,128]{3,2,1,0:T(8,128)(2,1)} %bitcast.176), channel_id=1, source_target_pairs={{0,32},{32,64},{64,96},{96,128},{128,160},{160,192},{192,224},{1,3... | collective-permute-start | bytes 6291464 | tf_op jit(solution)/shard_map/ppermute | solution.py:10
  60.9 21.4 %copy-start = (bf16[16,8,64,128]{3,2,1,0:T(8,128)(2,1)}, bf16[16,8,64,128]{3,2,1,0:T(8,128)(2,1)S(1)}, u32[]{:S(2)}) copy-start(bf16[16,8,64,128]{3,2,1,0:T(8,128)(2,1)S(1)} %select_select_fusion) | copy-start | bytes 6291460
  82.3 11.5 %copy-start.4 = (f32[1,8]{1,0:T(1,128)S(1)}, f32[1,8]{1,0:T(1,128)}, u32[]{:S(2)}) copy-start(f32[1,8]{1,0:T(1,128)} %param.27) | copy-start | bytes 100
  82.3 49.0 %copy-start.2 = (bf16[1,4,16,512]{3,2,1,0:T(8,128)(2,1)S(1)}, bf16[1,4,16,512]{3,2,1,0:T(8,128)(2,1)}, u32[]{:S(2)}) copy-start(bf16[1,4,16,512]{3,2,1,0:T(8,128)(2,1)} %param.20) | copy-start | bytes 196612
  82.3 49.0 %copy-start.3 = (f32[1,512]{1,0:T(1,128)S(1)}, f32[1,512]{1,0:T(1,128)}, u32[]{:S(2)}) copy-start(f32[1,512]{1,0:T(1,128)} %param.28) | copy-start | bytes 6148
  93.7 41.4 %copy-start.1 = (bf16[16,8,64,128]{3,2,1,0:T(8,128)(2,1)S(1)}, bf16[16,8,64,128]{3,2,1,0:T(8,128)(2,1)}, u32[]{:S(2)}) copy-start(bf16[16,8,64,128]{3,2,1,0:T(8,128)(2,1)} %copy-done) | copy-start | bytes 6291460
  131.3 2.2 %collective-permute-start.2 = (bf16[4,16,512]{2,1,0:T(8,128)(2,1)S(1)}, bf16[4,16,512]{2,1,0:T(8,128)(2,1)S(1)}, u32[]{:S(2)}, u32[]{:S(2)}) collective-permute-start(bf16[4,16,512]{2,1,0:T(8,128)(2,1)S(1)} %pad_maximum_fusion.4), channel_id=1, source_target_pairs={{0,16},{1,17},{2,18},{3,19},{4,20},{5,21},{6,22},{7,23},{8,24},{9,... | collective-permute-start | bytes 196616 | tf_op jit(solution)/shard_map/ppermute | solution.py:10
where the time goes:
time: 210 us; the launch traced here: 209 us
  blocking collectives  76.8 us (37%)
  matrix products  65.5 us (31%)
  waiting for transfers between devices  34.4 us (16%)
  local copies, waits for them, and re-layouts  13.2 us (6%)
  other arithmetic  9.88 us (5%)
  starting transfers between devices  9.26 us (4%)
    psum x2, blocking collectives, decode_step(): totals = lax.psum(jnp.sum(gated * gated, axis=1), 'tp')  76.8 us
    dot_general x8, matrix products, recurrence(): jnp.einsum('shpn,sn->shp', hstate, c_row, precision=lax.Precision.HIGHEST)  65.5 us
    ppermute x3, waiting for transfers between devices, passed_along(): lax.ppermute(value, axis, [(source, source + steps) for source in range(i...  34.4 us
    ppermute x3, starting transfers between devices, passed_along(): lax.ppermute(value, axis, [(source, source + steps) for source in range(i...  9.26 us
  transfers between devices with their start and end apart: 3, of which 2 were waited for; matrix products, arithmetic and copies ran while one was open for 6% of the time, Pallas kernels for 0%

commit v1 on v0

v1 whole, which is shorter than its diff:
```python
import jax
import jax.numpy as jnp
from jax import lax
from jax.experimental import pallas as pl
from jax.experimental.pallas import tpu as pltpu
from jax.sharding import PartitionSpec as P

F32 = jnp.float32
BF16 = jnp.bfloat16
VMEM = pl.BlockSpec(memory_space=pltpu.VMEM)
SMEM = pl.BlockSpec(memory_space=pltpu.SMEM)
ANY = pl.BlockSpec(memory_space=pl.ANY)
NT = (((1,), (1,)), ((), ()))
EPS = 1e-05
PARAMS = pltpu.CompilerParams(vmem_limit_bytes=24 * 1024 * 1024)


def silu(value):
    return value / (1.0 + jnp.exp(-value))


def pairs(steps):
    return [(t, r) for t in range(steps) for r in range(t + 1)]


def crossing_kernel(parent, state, window, out, sem):
    slots = window.shape[1]
    nrows = state.shape[1]
    count = lax.axis_size("roll")
    following = lax.rem(lax.axis_index("roll") + 1, count)
    begin = following * slots

    def look(s, found):
        row = parent[begin + s] - begin + slots
        return jnp.where(row < slots, row, found)

    row = lax.fori_loop(0, slots, look, jnp.int32(0), unroll=True)
    row = jnp.clip(row, 0, slots - 1)
    copy = pltpu.make_async_copy(state.at[row], out.at[pl.ds(0, nrows)], sem)
    copy.start()
    taps, _, width = window.shape
    groups = width // 128
    pick = lax.broadcasted_iota(jnp.int32, (slots, 1), 0) == row
    place = lax.broadcasted_iota(jnp.int32, (out.shape[0] - nrows, 128), 0)
    packed = jnp.zeros(place.shape, F32)
    for k in range(taps):
        chosen = jnp.sum(jnp.where(pick, window[k].astype(F32), 0.0), axis=0, keepdims=True)
        for j in range(groups):
            packed = jnp.where(place == k * groups + j, chosen[:, j * 128:(j + 1) * 128], packed)
    out[pl.ds(nrows, place.shape[0])] = packed.astype(BF16)
    copy.wait()


def local_kernel(
    parent, state, window, c_in, b_in, dt_raw, z_gate, conv, a_log, dt_bias, skip_d,
    base_out, reach_out, mix_out, conv_out, cmask_out, wmask_out,
    held, sems,
):
    steps, slots, width = z_gate.shape
    heads = dt_raw.shape[1]
    taps = window.shape[0]
    nstate = c_in.shape[2]
    first = lax.axis_index("roll") * slots
    local = []
    copies = []
    for s in range(slots):
        row = parent[first + s] - first
        local.append(row)
        copy = pltpu.make_async_copy(state.at[jnp.clip(row, 0, slots - 1)], held.at[s], sems.at[s])
        copy.start()
        copies.append(copy)

    slot_col = lax.broadcasted_iota(jnp.int32, (slots, slots), 0)
    slot_row = lax.broadcasted_iota(jnp.int32, (slots, slots), 1)
    choose = jnp.zeros((slots, slots), F32)
    slot_lane = lax.broadcasted_iota(jnp.int32, (slots, 128), 0)
    inside = jnp.zeros((slots, 128), F32)
    for s in range(slots):
        choose = jnp.where((slot_col == s) & (slot_row == local[s]), 1.0, choose)
        inside = jnp.where((slot_lane == s) & (local[s] >= 0), 1.0, inside)
    outside = 1.0 - inside
    wmask_out[...] = outside
    choose = choose.astype(BF16)

    taken = [jnp.dot(choose, window[k], preferred_element_type=F32) for k in range(taps)]
    weight = [conv[pl.ds(k, 1), :].astype(F32) for k in range(taps + 1)]
    for t in range(taps):
        part = weight[0] * taken[t]
        for k in range(1, taps - t):
            part = part + weight[k] * taken[t + k]
        conv_out[t] = part

    rate = jnp.exp(a_log[...])
    delta, decay = [], []
    for t in range(steps):
        raw = jnp.transpose(dt_raw[t]) + dt_bias[...]
        delta.append(jnp.maximum(raw, 0.0) + jnp.log1p(jnp.exp(-jnp.abs(raw))))
        decay.append(jnp.exp(-delta[t] * rate))
    c_rows = [c_in[t].astype(F32) for t in range(steps)]
    b_rows = [b_in[t].astype(F32) for t in range(steps)]
    coefs = []
    running = None
    for t in range(steps):
        running = decay[t] if running is None else running * decay[t]
        coefs.append(running)
    for t, r in pairs(steps):
        dot = jnp.sum(c_rows[t] * b_rows[r], axis=1, keepdims=True)
        coef = delta[r] * dot
        for j in range(r + 1, t + 1):
            coef = coef * decay[j]
        if t == r:
            coef = coef + skip_d[...]
        coefs.append(coef)
    stacked = jnp.concatenate(coefs, axis=0)
    head = lax.broadcasted_iota(jnp.int32, (heads, width), 0)
    lane_head = lax.broadcasted_iota(jnp.int32, (heads, width), 1) // (width // heads)
    expand = jnp.where(head == lane_head, 1.0, 0.0).astype(BF16)
    high = stacked.astype(BF16)
    low = (stacked - high.astype(F32)).astype(BF16)
    spread = jnp.dot(high, expand, preferred_element_type=F32) + jnp.dot(low, expand, preferred_element_type=F32)
    gate = [silu(z_gate[t].astype(F32)) for t in range(steps)]
    reach = []
    for t in range(steps):
        reach.append(spread[t * slots:(t + 1) * slots] * gate[t])
        reach_out[t] = reach[t]
    for i, (t, _) in enumerate(pairs(steps)):
        mix_out[i] = spread[(steps + i) * slots:(steps + i + 1) * slots] * gate[t]

    c_all = jnp.concatenate(c_rows, axis=0)
    slot_of = lax.rem(lax.broadcasted_iota(jnp.int32, (steps * slots, nstate), 0), slots)
    all_outside = jnp.concatenate([outside] * steps, axis=0)
    all_inside = 1.0 - all_outside
    cmask_out[...] = (c_all * all_outside).astype(BF16)
    c_inside = c_all * all_inside
    total = None
    for s in range(0, slots, 2):
        copies[s].wait()
        copies[s + 1].wait()
        lhs = jnp.concatenate(
            [jnp.where(slot_of == s + i, c_inside, 0.0).astype(BF16) for i in range(2)], axis=1
        )
        rhs = jnp.concatenate([held[s], held[s + 1]], axis=1)
        part = lax.dot_general(lhs, rhs, NT, preferred_element_type=F32)
        total = part if total is None else total + part
    for t in range(steps):
        base_out[t] = total[t * slots:(t + 1) * slots] * reach[t]


def gated_rows(pre, base, mix, steps):
    inner = [silu(value) for value in pre]
    rows = list(base)
    for i, (t, r) in enumerate(pairs(steps)):
        rows[t] = rows[t] + mix[i] * inner[r]
    return rows


def square_sums(rows):
    squares = []
    for row in rows:
        sq = row * row
        part = sq[:, :128]
        for j in range(1, sq.shape[1] // 128):
            part = part + sq[:, j * 128:(j + 1) * 128]
        squares.append(part)
    flat = jnp.concatenate(squares, axis=0)
    flat = jnp.concatenate([flat, jnp.zeros((128 - flat.shape[0], 128), F32)], axis=0)
    return jnp.sum(jnp.transpose(flat), axis=0, keepdims=True)


def row_scales(parts, channels, rows):
    totals = jnp.sum(parts, axis=0)[:1]
    scale = lax.rsqrt(totals * (1.0 / channels) + EPS)
    return jnp.transpose(jnp.broadcast_to(scale, (128, 128)))[:rows]


def scaled(row, scale):
    return jnp.concatenate(
        [row[:, j * 128:(j + 1) * 128] * scale for j in range(row.shape[1] // 128)], axis=1
    )


def first_kernel(arrived, base, reach, mix, conv_part, cmask, wmask, conv, x_in, gain,
                 base_out, conv_out, send_out, sums_out):
    steps, slots, width = x_in.shape
    taps = conv_part.shape[0]
    nrows = arrived.shape[0] - 16
    groups = width // 128
    extra = lax.dot_general(cmask[...], arrived[pl.ds(0, nrows)], NT, preferred_element_type=F32)
    start = []
    for t in range(steps):
        start.append(base[t] + extra[t * slots:(t + 1) * slots] * reach[t])
        base_out[t] = start[t]
    packed = arrived[pl.ds(nrows, 16)].astype(F32)
    rows = [
        jnp.concatenate([packed[k * groups + j:k * groups + j + 1] for j in range(groups)], axis=1)
        for k in range(taps)
    ]
    weight = [conv[pl.ds(k, 1), :].astype(F32) for k in range(taps + 1)]
    mask = wmask[:, :1]
    pre = []
    for t in range(taps):
        part = weight[0] * rows[t]
        for k in range(1, taps - t):
            part = part + weight[k] * rows[t + k]
        pre.append(conv_part[t] + mask * part)
        conv_out[t] = pre[t]
    x_rows = [x_in[t].astype(F32) for t in range(steps)]
    pre = with_inputs(pre, weight, x_rows)
    gated = gated_rows(pre, start, [mix[i] for i in range(mix.shape[0])], steps)
    for t in range(steps):
        send_out[t] = gated[t] * gain[...]
    sums_out[...] = jnp.broadcast_to(square_sums(gated)[None], sums_out.shape)


def with_inputs(window_part, weight, x_rows):
    taps = len(window_part)
    pre = []
    for t in range(len(x_rows)):
        part = window_part[t] if t < taps else None
        for k in range(max(0, taps - t), taps + 1):
            term = weight[k] * x_rows[t + k - taps]
            part = term if part is None else part + term
        pre.append(part)
    return pre


def second_kernel(sums, own, other, base, mix, conv_part, conv, channels, norm_out, gated_out, sums_out):
    steps, slots, width = own.shape
    taps = conv_part.shape[0]
    scale = row_scales(sums[...], channels, steps * slots)
    first = lax.axis_index("pipe") == 0
    rows = []
    for t in range(steps):
        row = jnp.where(first, own[t], other[t])
        row = scaled(row, scale[t * slots:(t + 1) * slots]).astype(BF16)
        norm_out[t] = row
        rows.append(row.astype(F32))
    weight = [conv[pl.ds(k, 1), :].astype(F32) for k in range(taps + 1)]
    pre = with_inputs([conv_part[t] for t in range(taps)], weight, rows)
    gated = gated_rows(pre, [base[t] for t in range(steps)], [mix[i] for i in range(mix.shape[0])], steps)
    for t in range(steps):
        gated_out[t] = gated[t]
    sums_out[...] = jnp.broadcast_to(square_sums(gated)[None], sums_out.shape)


def last_kernel(sums, norm, gated, gain, channels, out):
    steps, slots, width = gated.shape
    scale = row_scales(sums[...], channels, steps * slots)
    first = lax.axis_index("pipe") == 0
    for t in range(steps):
        row = scaled(gated[t], scale[t * slots:(t + 1) * slots]) * gain[...]
        out[t] = jnp.where(first, norm[t].astype(F32), row).astype(BF16)


def body(ssm_state, conv_window, x_in, z_gate, dt_raw, b_in, c_in, conv_weight, a_log, dt_bias, skip_d, norm_gain, parent):
    _, slots, heads, head_dim, nstate = ssm_state.shape
    steps, _, width = x_in.shape
    taps = conv_window.shape[2]
    rows = heads * head_dim
    tp = lax.axis_size("tp")
    pipes = lax.axis_size("pipe")
    count = lax.axis_size("roll")
    channels = width * tp
    npairs = len(pairs(steps))
    state = ssm_state.reshape(slots, rows, nstate)
    window = jnp.transpose(conv_window[0], (1, 0, 2))
    raw = jnp.transpose(dt_raw[0], (0, 2, 1))
    shape = jax.ShapeDtypeStruct

    leaving = pl.pallas_call(
        crossing_kernel,
        out_shape=shape((rows + 16, nstate), BF16),
        in_specs=[SMEM, ANY, VMEM],
        out_specs=VMEM,
        scratch_shapes=[pltpu.SemaphoreType.DMA],
        compiler_params=PARAMS,
        name="crossing",
    )(parent, state, window)
    arrived = lax.ppermute(leaving, "roll", [(i, (i + 1) % count) for i in range(count)])

    base, reach, mix, conv_part, cmask, wmask = pl.pallas_call(
        local_kernel,
        out_shape=(
            shape((steps, slots, width), F32),
            shape((steps, slots, width), F32),
            shape((npairs, slots, width), F32),
            shape((taps, slots, width), F32),
            shape((steps * slots, nstate), BF16),
            shape((slots, 128), F32),
        ),
        in_specs=[SMEM, ANY] + [VMEM] * 9,
        out_specs=(VMEM,) * 6,
        scratch_shapes=[
            pltpu.VMEM((slots, rows, nstate), BF16),
            pltpu.SemaphoreType.DMA((slots,)),
        ],
        compiler_params=PARAMS,
        cost_estimate=pl.CostEstimate(flops=20_000_000, bytes_accessed=4_000_000, transcendentals=0),
        name="local",
    )(parent, state, window, c_in[0], b_in[0], raw, z_gate[0], conv_weight[0], a_log, dt_bias, skip_d)

    base, conv_part, own, sums = pl.pallas_call(
        first_kernel,
        out_shape=(
            shape((steps, slots, width), F32),
            shape((taps, slots, width), F32),
            shape((steps, slots, width), F32),
            shape((pipes * tp, 8, 128), F32),
        ),
        in_specs=[VMEM] * 10,
        out_specs=(VMEM,) * 4,
        compiler_params=PARAMS,
        name="first",
    )(arrived, base, reach, mix, conv_part, cmask, wmask, conv_weight[0], x_in, norm_gain)
    other = lax.ppermute(own, "pipe", [(i, (i + 1) % pipes) for i in range(pipes)])
    sums = lax.all_to_all(sums, ("pipe", "tp"), 0, 0)

    norm, gated, sums = pl.pallas_call(
        lambda sums, *refs: second_kernel(sums.at[pl.ds(0, tp)], *refs[:6], channels, *refs[6:]),
        out_shape=(
            shape((steps, slots, width), BF16),
            shape((steps, slots, width), F32),
            shape((tp, 8, 128), F32),
        ),
        in_specs=[VMEM] * 7,
        out_specs=(VMEM,) * 3,
        compiler_params=PARAMS,
        name="second",
    )(sums, own, other, base, mix, conv_part, conv_weight[0])
    sums = lax.all_to_all(sums, "tp", 0, 0)

    result = pl.pallas_call(
        lambda sums, norm, gated, gain, out: last_kernel(sums, norm, gated, gain, channels, out),
        out_shape=shape((steps, slots, width), BF16),
        in_specs=[VMEM] * 4,
        out_specs=VMEM,
        compiler_params=PARAMS,
        name="last",
    )(sums, norm, gated, norm_gain)
    return result[None]


def solution(mesh):
    in_specs = (
        P("pipe", "roll", "tp", None, None),
        P("pipe", "roll", None, "tp"),
        P(None, "roll", "tp"),
        P("pipe", None, "roll", "tp"),
        P("pipe", None, "roll", "tp"),
        P("pipe", None, "roll", None),
        P("pipe", None, "roll", None),
        P("pipe", None, "tp"),
        P("pipe", "tp"),
        P("pipe", "tp"),
        P("pipe", "tp"),
        P("pipe", "tp"),
        P(),
    )
    out_specs = P("pipe", None, "roll", "tp")
    return jax.shard_map(body, mesh=mesh, in_specs=in_specs, out_specs=out_specs, check_vma=False)
```

time: 210 us -> 40.6 us (0.19)
  the two profiles are of different devices: /device:TPU:98 before, /device:TPU:1 now
where the time goes in v1:
time: 40.6 us; the launch traced here: 40.4 us
  blocking collectives  24 us (59%)
  Pallas kernels  6.9 us (17%)
  starting transfers between devices  3.86 us (10%)
  local copies, waits for them, and re-layouts  3.11 us (8%)
  waiting for transfers between devices  2.43 us (6%)
    all_to_all x1, blocking collectives, body(): sums = lax.all_to_all(sums, ('pipe', 'tp'), 0, 0)  14.5 us
    all_to_all x1, blocking collectives, body(): sums = lax.all_to_all(sums, 'tp', 0, 0)  9.48 us
    pallas_call x1, Pallas kernels, body(): pl.pallas_call(local_kernel, out_shape=(shape((steps, slots, width), F32)...  4.77 us
    unnamed x26, local copies, waits for them, and re-layouts  3.11 us
    ppermute x1, starting transfers between devices, body(): lax.ppermute(leaving, 'roll', [(i, (i + 1) % count) for i in range(count)])  2.54 us
    ppermute x1, waiting for transfers between devices, body(): lax.ppermute(leaving, 'roll', [(i, (i + 1) % count) for i in range(count)])  2.42 us
    ppermute x1, starting transfers between devices, body(): lax.ppermute(own, 'pipe', [(i, (i + 1) % pipes) for i in range(pipes)])  1.32 us
  transfers between devices with their start and end apart: 2, of which 1 were waited for; matrix products, arithmetic and copies ran while one was open for 0% of the time, Pallas kernels for 12%

profile of v1, /device:TPU:1, one launch (start us, length us, event | category | flops | bytes accessed | tf_op | source)
XLA Modules:
  0.0 40.4 jit_solution(17628399369143745811)
XLA Ops:
  0.0 0.0 copy-start
  0.0 1.6 %copy-done = bf16[1,16,8,64,128]{4,3,2,1,0:T(8,128)(2,1)S(1)} copy-done((bf16[1,16,8,64,128]{4,3,2,1,0:T(8,128)(2,1)S(1)}, bf16[1,16,8,64,128]{4,3,2,1,0:T(8,128)(2,1)}, u32[]{:S(2)}) %copy-start) | copy-done | bytes 2097176
  1.6 0.8 %copy-done.1 = bf16[1,16,3,512]{3,1,2,0:T(8,128)(2,1)S(1)} copy-done((bf16[1,16,3,512]{3,1,2,0:T(8,128)(2,1)S(1)}, bf16[1,16,3,512]{3,1,2,0:T(8,128)(2,1)}, u32[]{:S(2)}) %copy-start.1) | copy-done | bytes 49176
  2.4 0.7 %copy-done.9 = s32[128]{0:T(128)S(1)} copy-done((s32[128]{0:T(128)S(1)}, s32[128]{0:T(128)}, u32[]{:S(2)}) %copy-start.9) | copy-done | bytes 536
  3.1 0.0 copy-start.7
  3.1 0.0 copy-start.2
  3.1 0.0 copy-start.8
  3.1 0.8 %crossing.1 = bf16[528,128]{1,0:T(8,128)(2,1)S(1)} custom-call(s32[128]{0:T(128)S(1)} %copy-done.9, bf16[16,512,128]{2,1,0:T(8,128)(2,1)S(1)} %bitcast.12, bf16[3,16,512]{2,1,0:T(8,128)(2,1)S(1)} %bitcast.14), custom_call_target="tpu_custom_call" | custom-call | tf_op jit(solution)/shard_map/crossing/pallas_call | solution.py:270
  3.9 2.5 %collective-permute-start = (bf16[528,128]{1,0:T(8,128)(2,1)S(1)}, bf16[528,128]{1,0:T(8,128)(2,1)S(1)}, u32[]{:S(2)}, u32[]{:S(2)}) collective-permute-start(bf16[528,128]{1,0:T(8,128)(2,1)S(1)} %crossing.1), channel_id=1, source_target_pairs={{0,32},{32,64},{64,96},{96,128},{128,160},{160,192},{192,224},{224... | collective-permute-start | bytes 405512 | tf_op jit(solution)/shard_map/ppermute | solution.py:279
  6.5 0.0 copy-done.12
  6.5 0.0 copy-done.11
  6.5 0.0 copy-done.10
  6.5 0.0 copy-done.3
  6.5 0.0 copy-done.4
  6.5 0.0 copy-done.5
  6.5 4.8 %local.1 = (f32[4,16,512]{2,1,0:T(8,128)S(1)}, f32[4,16,512]{2,1,0:T(8,128)S(1)}, f32[10,16,512]{2,1,0:T(8,128)S(1)}, f32[3,16,512]{2,1,0:T(8,128)S(1)}, bf16[64...) custom-call(s32[128]{0:T(128)S(1)} %copy-done.9, bf16[16,512,128]{2,1,0:T(8,128)(2,1)S(1)} %bitcast.13, ...), custom_call_target="tpu_custom_call" | custom-call | flops 20000000 | bytes 4000000 | tf_op jit(solution)/shard_map/local/pallas_call | solution.py:281
  11.3 2.4 %collective-permute-done.arrived = bf16[528,128]{1,0:T(8,128)(2,1)S(1)} collective-permute-done((bf16[528,128]{1,0:T(8,128)(2,1)S(1)}, bf16[528,128]{1,0:T(8,128)(2,1)S(1)}, u32[]{:S(2)}, u32[]{:S(2)}) %collective-permute-start) | collective-permute-done | bytes 135200 | tf_op jit(solution)/shard_map/ppermute | solution.py:279
  13.7 0.3 first.1
  14.0 1.3 %collective-permute-start.1 = (f32[4,16,512]{2,1,0:T(8,128)S(1)}, f32[4,16,512]{2,1,0:T(8,128)S(1)}, u32[]{:S(2)}, u32[]{:S(2)}) collective-permute-start(f32[4,16,512]{2,1,0:T(8,128)S(1)} %get-tuple-element.25.refs_0_), channel_id=1, source_target_pairs={{0,16},{16,0},{1,17},{17,1},{2,18},{18,2},{3,19},{19,3},{4,20},{20... | collective-permute-start | bytes 393224 | tf_op jit(solution)/shard_map/ppermute | solution.py:315
  15.4 14.5 %all_to_all.10.sums = f32[32,8,128]{2,1,0:T(8,128)S(1)} all-to-all(f32[32,8,128]{2,1,0:T(8,128)S(1)} %get-tuple-element.24), channel_id=1, replica_groups=mesh['roll'=8,'pipe'=2,'tp'=16] {'pipe','tp'}, dimensions={0} | all-to-all | bytes 262144 | tf_op jit(solution)/shard_map/all_to_all | solution.py:316
  29.9 0.0 collective-permute-done.1.refs_1_
  29.9 0.3 second.1
  30.2 9.5 %all_to_all.11.sums = f32[16,8,128]{2,1,0:T(8,128)S(1)} all-to-all(f32[16,8,128]{2,1,0:T(8,128)S(1)} %get-tuple-element.28), channel_id=1, replica_groups=mesh['roll'=8,'pipe'=2,'tp'=16] {'tp'}, dimensions={0} | all-to-all | bytes 131072 | tf_op jit(solution)/shard_map/all_to_all | solution.py:330
  39.7 0.7 %last.1 = bf16[4,16,512]{2,1,0:T(8,128)(2,1)} custom-call(f32[16,8,128]{2,1,0:T(8,128)S(1)} %all_to_all.11.sums, bf16[4,16,512]{2,1,0:T(8,128)(2,1)S(1)} %get-tuple-element.29.norm, f32[4,16,512]{2,1,0:T(8,128)S(1)} %get-tuple-element.30.gated, f32[1,512]{1,0:T(1,128)S(1)} %copy-done.8), custom_call_target="tpu_custom_call" | custom-call | tf_op jit(solution)/shard_map/last/pallas_call | solution.py:332
  (13 shorter events, 0.0 us)
Async XLA Ops:
  0.0 6.5 %copy-start.12 = (f32[1,8]{1,0:T(1,128)S(1)}, f32[1,8]{1,0:T(1,128)}, u32[]{:S(2)}) copy-start(f32[1,8]{1,0:T(1,128)} %skip_d.1) | copy-start | bytes 100
  0.0 6.5 %copy-start.11 = (f32[1,8]{1,0:T(1,128)S(1)}, f32[1,8]{1,0:T(1,128)}, u32[]{:S(2)}) copy-start(f32[1,8]{1,0:T(1,128)} %dt_bias.1) | copy-start | bytes 100
  0.0 6.5 %copy-start.10 = (f32[1,8]{1,0:T(1,128)S(1)}, f32[1,8]{1,0:T(1,128)}, u32[]{:S(2)}) copy-start(f32[1,8]{1,0:T(1,128)} %a_log.1) | copy-start | bytes 100
  0.0 1.6 %copy-start = (bf16[1,16,8,64,128]{4,3,2,1,0:T(8,128)(2,1)S(1)}, bf16[1,16,8,64,128]{4,3,2,1,0:T(8,128)(2,1)}, u32[]{:S(2)}) copy-start(bf16[1,16,8,64,128]{4,3,2,1,0:T(8,128)(2,1)} %param.13) | copy-start | bytes 6291460
  1.6 0.8 %copy-start.1 = (bf16[1,16,3,512]{3,1,2,0:T(8,128)(2,1)S(1)}, bf16[1,16,3,512]{3,1,2,0:T(8,128)(2,1)}, u32[]{:S(2)}) copy-start(bf16[1,16,3,512]{3,1,2,0:T(8,128)(2,1)} %param.14) | copy-start | bytes 147460
  2.4 0.7 %copy-start.9 = (s32[128]{0:T(128)S(1)}, s32[128]{0:T(128)}, u32[]{:S(2)}) copy-start(s32[128]{0:T(128)} %parent.3) | copy-start | bytes 1540
  3.1 3.4 %copy-start.3 = (bf16[1,4,16,512]{3,2,1,0:T(8,128)(2,1)S(1)}, bf16[1,4,16,512]{3,2,1,0:T(8,128)(2,1)}, u32[]{:S(2)}) copy-start(bf16[1,4,16,512]{3,2,1,0:T(8,128)(2,1)} %param.16) | copy-start | bytes 196612
  3.1 3.4 %copy-start.4 = (bf16[1,4,512]{2,1,0:T(4,128)(2,1)S(1)}, bf16[1,4,512]{2,1,0:T(4,128)(2,1)}, u32[]{:S(2)}) copy-start(bf16[1,4,512]{2,1,0:T(4,128)(2,1)} %param.20) | copy-start | bytes 12292
  3.1 3.4 %copy-start.5 = (bf16[1,4,16,128]{3,2,1,0:T(8,128)(2,1)S(1)}, bf16[1,4,16,128]{3,2,1,0:T(8,128)(2,1)}, u32[]{:S(2)}) copy-start(bf16[1,4,16,128]{3,2,1,0:T(8,128)(2,1)} %param.19) | copy-start | bytes 49156
  3.1 3.4 %copy-start.6 = (bf16[1,4,16,128]{3,2,1,0:T(8,128)(2,1)S(1)}, bf16[1,4,16,128]{3,2,1,0:T(8,128)(2,1)}, u32[]{:S(2)}) copy-start(bf16[1,4,16,128]{3,2,1,0:T(8,128)(2,1)} %param.18) | copy-start | bytes 49156
  3.1 3.4 %copy-start.7 = (f32[1,4,16,8]{2,3,1,0:T(8,128)S(1)}, f32[1,4,16,8]{2,3,1,0:T(8,128)}, u32[]{:S(2)}) copy-start(f32[1,4,16,8]{2,3,1,0:T(8,128)} %param.17) | copy-start | bytes 6148
  3.1 10.6 %copy-start.2 = (bf16[4,16,512]{2,1,0:T(8,128)(2,1)S(1)}, bf16[4,16,512]{2,1,0:T(8,128)(2,1)}, u32[]{:S(2)}) copy-start(bf16[4,16,512]{2,1,0:T(8,128)(2,1)} %x_in.1) | copy-start | bytes 196612
  3.1 10.6 %copy-start.8 = (f32[1,512]{1,0:T(1,128)S(1)}, f32[1,512]{1,0:T(1,128)}, u32[]{:S(2)}) copy-start(f32[1,512]{1,0:T(1,128)} %gain.3) | copy-start | bytes 6148
  3.9 9.8 %collective-permute-start = (bf16[528,128]{1,0:T(8,128)(2,1)S(1)}, bf16[528,128]{1,0:T(8,128)(2,1)S(1)}, u32[]{:S(2)}, u32[]{:S(2)}) collective-permute-start(bf16[528,128]{1,0:T(8,128)(2,1)S(1)} %crossing.1), channel_id=1, source_target_pairs={{0,32},{32,64},{64,96},{96,128},{128,160},{160,192},{192,224},{224... | collective-permute-start | bytes 405512 | tf_op jit(solution)/shard_map/ppermute | solution.py:279
  14.0 15.8 %collective-permute-start.1 = (f32[4,16,512]{2,1,0:T(8,128)S(1)}, f32[4,16,512]{2,1,0:T(8,128)S(1)}, u32[]{:S(2)}, u32[]{:S(2)}) collective-permute-start(f32[4,16,512]{2,1,0:T(8,128)S(1)} %get-tuple-element.25.refs_0_), channel_id=1, source_target_pairs={{0,16},{16,0},{1,17},{17,1},{2,18},{18,2},{3,19},{19,3},{4,20},{20... | collective-permute-start | bytes 393224 | tf_op jit(solution)/shard_map/ppermute | solution.py:315

commit v2 on v1

--- a/solution.py
+++ b/solution.py
@@ -9,7 +9,7 @@
 BF16 = jnp.bfloat16
 VMEM = pl.BlockSpec(memory_space=pltpu.VMEM)
 SMEM = pl.BlockSpec(memory_space=pltpu.SMEM)
-ANY = pl.BlockSpec(memory_space=pl.ANY)
+HBM = pl.BlockSpec(memory_space=pltpu.HBM)
 NT = (((1,), (1,)), ((), ()))
 EPS = 1e-05
 PARAMS = pltpu.CompilerParams(vmem_limit_bytes=24 * 1024 * 1024)
@@ -23,26 +23,31 @@
     return [(t, r) for t in range(steps) for r in range(t + 1)]
 
 
-def crossing_kernel(parent, state, window, out, sem):
+def crossing_kernel(parent_hbm, state, window_hbm, out, parent, window, sems):
+    get_parent = pltpu.make_async_copy(parent_hbm, parent, sems.at[0])
+    get_parent.start()
+    get_window = pltpu.make_async_copy(window_hbm, window, sems.at[1])
+    get_window.start()
     slots = window.shape[1]
     nrows = state.shape[1]
     count = lax.axis_size("roll")
     following = lax.rem(lax.axis_index("roll") + 1, count)
     begin = following * slots
-
-    def look(s, found):
-        row = parent[begin + s] - begin + slots
-        return jnp.where(row < slots, row, found)
-
-    row = lax.fori_loop(0, slots, look, jnp.int32(0), unroll=True)
+    get_parent.wait()
+
+    row = jnp.int32(0)
+    for s in range(slots):
+        found = parent[begin + s] - begin + slots
+        row = jnp.where(found < slots, found, row)
     row = jnp.clip(row, 0, slots - 1)
-    copy = pltpu.make_async_copy(state.at[row], out.at[pl.ds(0, nrows)], sem)
+    copy = pltpu.make_async_copy(state.at[row], out.at[pl.ds(0, nrows)], sems.at[2])
     copy.start()
     taps, _, width = window.shape
     groups = width // 128
     pick = lax.broadcasted_iota(jnp.int32, (slots, 1), 0) == row
     place = lax.broadcasted_iota(jnp.int32, (out.shape[0] - nrows, 128), 0)
     packed = jnp.zeros(place.shape, F32)
+    get_window.wait()
     for k in range(taps):
         chosen = jnp.sum(jnp.where(pick, window[k].astype(F32), 0.0), axis=0, keepdims=True)
         for j in range(groups):
@@ -54,21 +59,14 @@
 def local_kernel(
     parent, state, window, c_in, b_in, dt_raw, z_gate, conv, a_log, dt_bias, skip_d,
     base_out, reach_out, mix_out, conv_out, cmask_out, wmask_out,
-    held, sems,
 ):
     steps, slots, width = z_gate.shape
     heads = dt_raw.shape[1]
     taps = window.shape[0]
     nstate = c_in.shape[2]
     first = lax.axis_index("roll") * slots
-    local = []
-    copies = []
-    for s in range(slots):
-        row = parent[first + s] - first
-        local.append(row)
-        copy = pltpu.make_async_copy(state.at[jnp.clip(row, 0, slots - 1)], held.at[s], sems.at[s])
-        copy.start()
-        copies.append(copy)
+    local = [parent[first + s] - first for s in range(slots)]
+    held = [jnp.clip(row, 0, slots - 1) for row in local]
 
     slot_col = lax.broadcasted_iota(jnp.int32, (slots, slots), 0)
     slot_row = lax.broadcasted_iota(jnp.int32, (slots, slots), 1)
@@ -134,12 +132,10 @@
     c_inside = c_all * all_inside
     total = None
     for s in range(0, slots, 2):
-        copies[s].wait()
-        copies[s + 1].wait()
         lhs = jnp.concatenate(
             [jnp.where(slot_of == s + i, c_inside, 0.0).astype(BF16) for i in range(2)], axis=1
         )
-        rhs = jnp.concatenate([held[s], held[s + 1]], axis=1)
+        rhs = jnp.concatenate([state[held[s]], state[held[s + 1]]], axis=1)
         part = lax.dot_general(lhs, rhs, NT, preferred_element_type=F32)
         total = part if total is None else total + part
     for t in range(steps):
@@ -270,12 +266,16 @@
     leaving = pl.pallas_call(
         crossing_kernel,
         out_shape=shape((rows + 16, nstate), BF16),
-        in_specs=[SMEM, ANY, VMEM],
+        in_specs=[HBM, HBM, HBM],
         out_specs=VMEM,
-        scratch_shapes=[pltpu.SemaphoreType.DMA],
+        scratch_shapes=[
+            pltpu.SMEM(parent.shape, jnp.int32),
+            pltpu.VMEM(window.shape, BF16),
+            pltpu.SemaphoreType.DMA((3,)),
+        ],
         compiler_params=PARAMS,
         name="crossing",
-    )(parent, state, window)
+    )(*[pltpu.with_memory_space_constraint(value, pltpu.HBM) for value in (parent, state, window)])
     arrived = lax.ppermute(leaving, "roll", [(i, (i + 1) % count) for i in range(count)])
 
     base, reach, mix, conv_part, cmask, wmask = pl.pallas_call(
@@ -288,12 +288,8 @@
             shape((steps * slots, nstate), BF16),
             shape((slots, 128), F32),
         ),
-        in_specs=[SMEM, ANY] + [VMEM] * 9,
+        in_specs=[SMEM] + [VMEM] * 10,
         out_specs=(VMEM,) * 6,
-        scratch_shapes=[
-            pltpu.VMEM((slots, rows, nstate), BF16),
-            pltpu.SemaphoreType.DMA((slots,)),
-        ],
         compiler_params=PARAMS,
         cost_estimate=pl.CostEstimate(flops=20_000_000, bytes_accessed=4_000_000, transcendentals=0),
         name="local",

time: 40.6 us -> 38.5 us (0.948)
  waiting for transfers between devices: 2.43 us -> 5.68 us
  local copies, waits for them, and re-layouts: 3.11 us -> 0.05 us
  Pallas kernels: 6.9 us -> 4.59 us
    pallas_call x1, Pallas kernels: 4.77 us -> 1.49 us  [body(): pl.pallas_call(local_kernel, out_shape=(shape((steps, slots, width), F32)...]
    ppermute x1, waiting for transfers between devices: 2.42 us -> 5.68 us  [body(): lax.ppermute(leaving, 'roll', [(i, (i + 1) % count) for i in range(count)])]
    unnamed x26, local copies, waits for them, and re-layouts: 3.11 us -> 0.05 us
    pallas_call x1, Pallas kernels: 0.79 us -> 1.76 us  [body(): pl.pallas_call(crossing_kernel, out_shape=shape((rows + 16, nstate), BF16...]
  transfers between devices with their start and end apart: 2 -> 2, of which waited for: 1 -> 1; matrix products, arithmetic and copies ran while one was open for 0% -> 0% of each run, Pallas kernels for 12% -> 4%
where the time goes in v2:
time: 38.5 us; the launch traced here: 38.4 us
  blocking collectives  24 us (62%)
  waiting for transfers between devices  5.68 us (15%)
  Pallas kernels  4.59 us (12%)
  starting transfers between devices  3.86 us (10%)
    all_to_all x1, blocking collectives, body(): sums = lax.all_to_all(sums, ('pipe', 'tp'), 0, 0)  14.5 us
    all_to_all x1, blocking collectives, body(): sums = lax.all_to_all(sums, 'tp', 0, 0)  9.48 us
    ppermute x1, waiting for transfers between devices, body(): lax.ppermute(leaving, 'roll', [(i, (i + 1) % count) for i in range(count)])  5.68 us
    ppermute x1, starting transfers between devices, body(): lax.ppermute(leaving, 'roll', [(i, (i + 1) % count) for i in range(count)])  2.54 us
    pallas_call x1, Pallas kernels, body(): pl.pallas_call(crossing_kernel, out_shape=shape((rows + 16, nstate), BF16...  1.76 us
    pallas_call x1, Pallas kernels, body(): pl.pallas_call(local_kernel, out_shape=(shape((steps, slots, width), F32)...  1.49 us
    ppermute x1, starting transfers between devices, body(): lax.ppermute(own, 'pipe', [(i, (i + 1) % pipes) for i in range(pipes)])  1.32 us
  transfers between devices with their start and end apart: 2, of which 1 were waited for; matrix products, arithmetic and copies ran while one was open for 0% of the time, Pallas kernels for 4%

profile of v2, /device:TPU:1, one launch (start us, length us, event | category | flops | bytes accessed | tf_op | source)
XLA Modules:
  0.0 38.4 jit_solution(14362444288995273292)
XLA Ops:
  0.0 0.0 copy-start.12
  0.0 0.0 copy-start.11
  0.0 0.0 copy-start.10
  0.0 0.0 copy-start.4
  0.0 0.0 copy-start.5
  0.1 0.0 copy-start.6
  0.1 0.0 copy-start.7
  0.1 0.0 copy-start.3
  0.1 0.0 copy-start.2
  0.1 0.0 copy-start.8
  0.1 1.8 %crossing.1 = bf16[528,128]{1,0:T(8,128)(2,1)S(1)} custom-call(s32[128]{0:T(128)} %parent.1, bf16[16,512,128]{2,1,0:T(8,128)(2,1)} %bitcast.12, bf16[3,16,512]{2,1,0:T(8,128)(2,1)} %bitcast.14), custom_call_target="tpu_custom_call" | custom-call | tf_op jit(solution)/shard_map/crossing/pallas_call | solution.py:266
  1.9 2.5 %collective-permute-start = (bf16[528,128]{1,0:T(8,128)(2,1)S(1)}, bf16[528,128]{1,0:T(8,128)(2,1)S(1)}, u32[]{:S(2)}, u32[]{:S(2)}) collective-permute-start(bf16[528,128]{1,0:T(8,128)(2,1)S(1)} %crossing.1), channel_id=1, source_target_pairs={{0,32},{32,64},{64,96},{96,128},{128,160},{160,192},{192,224},{224... | collective-permute-start | bytes 405512 | tf_op jit(solution)/shard_map/ppermute | solution.py:279
  4.4 0.0 copy-done.9
  4.4 0.0 copy-done.1
  4.5 1.5 %local.1 = (f32[4,16,512]{2,1,0:T(8,128)S(1)}, f32[4,16,512]{2,1,0:T(8,128)S(1)}, f32[10,16,512]{2,1,0:T(8,128)S(1)}, f32[3,16,512]{2,1,0:T(8,128)S(1)}, bf16[64...) custom-call(s32[128]{0:T(128)S(1)} %copy-done.9, bf16[16,512,128]{2,1,0:T(8,128)(2,1)S(1)} %bitcast.13, ...), custom_call_target="tpu_custom_call" | custom-call | flops 20000000 | bytes 4000000 | tf_op jit(solution)/shard_map/local/pallas_call | solution.py:281
  6.0 5.7 %collective-permute-done.arrived = bf16[528,128]{1,0:T(8,128)(2,1)S(1)} collective-permute-done((bf16[528,128]{1,0:T(8,128)(2,1)S(1)}, bf16[528,128]{1,0:T(8,128)(2,1)S(1)}, u32[]{:S(2)}, u32[]{:S(2)}) %collective-permute-start) | collective-permute-done | bytes 135200 | tf_op jit(solution)/shard_map/ppermute | solution.py:279
  11.7 0.0 copy-done.8
  11.7 0.3 first.1
  12.0 1.3 %collective-permute-start.1 = (f32[4,16,512]{2,1,0:T(8,128)S(1)}, f32[4,16,512]{2,1,0:T(8,128)S(1)}, u32[]{:S(2)}, u32[]{:S(2)}) collective-permute-start(f32[4,16,512]{2,1,0:T(8,128)S(1)} %get-tuple-element.25.refs_0_), channel_id=1, source_target_pairs={{0,16},{16,0},{1,17},{17,1},{2,18},{18,2},{3,19},{19,3},{4,20},{20... | collective-permute-start | bytes 393224 | tf_op jit(solution)/shard_map/ppermute | solution.py:311
  13.3 14.5 %all_to_all.10.sums = f32[32,8,128]{2,1,0:T(8,128)S(1)} all-to-all(f32[32,8,128]{2,1,0:T(8,128)S(1)} %get-tuple-element.24), channel_id=1, replica_groups=mesh['roll'=8,'pipe'=2,'tp'=16] {'pipe','tp'}, dimensions={0} | all-to-all | bytes 262144 | tf_op jit(solution)/shard_map/all_to_all | solution.py:312
  27.8 0.0 collective-permute-done.1.refs_1_
  27.8 0.3 second.1
  28.1 9.5 %all_to_all.11.sums = f32[16,8,128]{2,1,0:T(8,128)S(1)} all-to-all(f32[16,8,128]{2,1,0:T(8,128)S(1)} %get-tuple-element.28), channel_id=1, replica_groups=mesh['roll'=8,'pipe'=2,'tp'=16] {'tp'}, dimensions={0} | all-to-all | bytes 131072 | tf_op jit(solution)/shard_map/all_to_all | solution.py:326
  37.6 0.7 %last.1 = bf16[4,16,512]{2,1,0:T(8,128)(2,1)} custom-call(f32[16,8,128]{2,1,0:T(8,128)S(1)} %all_to_all.11.sums, bf16[4,16,512]{2,1,0:T(8,128)(2,1)S(1)} %get-tuple-element.29.norm, f32[4,16,512]{2,1,0:T(8,128)S(1)} %get-tuple-element.30.gated, f32[1,512]{1,0:T(1,128)S(1)} %copy-done.8), custom_call_target="tpu_custom_call" | custom-call | tf_op jit(solution)/shard_map/last/pallas_call | solution.py:328
  (13 shorter events, 0.0 us)
Async XLA Ops:
  0.0 4.4 %copy-start.9 = (s32[128]{0:T(128)S(1)}, s32[128]{0:T(128)}, u32[]{:S(2)}) copy-start(s32[128]{0:T(128)} %parent.1) | copy-start | bytes 1540
  0.0 4.4 %copy-start.1 = (bf16[1,16,3,512]{3,1,2,0:T(8,128)(2,1)S(1)}, bf16[1,16,3,512]{3,1,2,0:T(8,128)(2,1)}, u32[]{:S(2)}) copy-start(bf16[1,16,3,512]{3,1,2,0:T(8,128)(2,1)} %param.14) | copy-start | bytes 147460
  0.0 4.4 %copy-start = (bf16[1,16,8,64,128]{4,3,2,1,0:T(8,128)(2,1)S(1)}, bf16[1,16,8,64,128]{4,3,2,1,0:T(8,128)(2,1)}, u32[]{:S(2)}) copy-start(bf16[1,16,8,64,128]{4,3,2,1,0:T(8,128)(2,1)} %param.13) | copy-start | bytes 6291460
  0.0 4.4 %copy-start.12 = (f32[1,8]{1,0:T(1,128)S(1)}, f32[1,8]{1,0:T(1,128)}, u32[]{:S(2)}) copy-start(f32[1,8]{1,0:T(1,128)} %skip_d.1) | copy-start | bytes 100
  0.0 4.4 %copy-start.11 = (f32[1,8]{1,0:T(1,128)S(1)}, f32[1,8]{1,0:T(1,128)}, u32[]{:S(2)}) copy-start(f32[1,8]{1,0:T(1,128)} %dt_bias.1) | copy-start | bytes 100
  0.0 4.4 %copy-start.10 = (f32[1,8]{1,0:T(1,128)S(1)}, f32[1,8]{1,0:T(1,128)}, u32[]{:S(2)}) copy-start(f32[1,8]{1,0:T(1,128)} %a_log.1) | copy-start | bytes 100
  0.0 4.4 %copy-start.4 = (bf16[1,4,512]{2,1,0:T(4,128)(2,1)S(1)}, bf16[1,4,512]{2,1,0:T(4,128)(2,1)}, u32[]{:S(2)}) copy-start(bf16[1,4,512]{2,1,0:T(4,128)(2,1)} %param.20) | copy-start | bytes 12292
  0.0 4.4 %copy-start.5 = (bf16[1,4,16,128]{3,2,1,0:T(8,128)(2,1)S(1)}, bf16[1,4,16,128]{3,2,1,0:T(8,128)(2,1)}, u32[]{:S(2)}) copy-start(bf16[1,4,16,128]{3,2,1,0:T(8,128)(2,1)} %param.19) | copy-start | bytes 49156
  0.1 4.4 %copy-start.6 = (bf16[1,4,16,128]{3,2,1,0:T(8,128)(2,1)S(1)}, bf16[1,4,16,128]{3,2,1,0:T(8,128)(2,1)}, u32[]{:S(2)}) copy-start(bf16[1,4,16,128]{3,2,1,0:T(8,128)(2,1)} %param.18) | copy-start | bytes 49156
  0.1 4.4 %copy-start.7 = (f32[1,4,16,8]{2,3,1,0:T(8,128)S(1)}, f32[1,4,16,8]{2,3,1,0:T(8,128)}, u32[]{:S(2)}) copy-start(f32[1,4,16,8]{2,3,1,0:T(8,128)} %param.17) | copy-start | bytes 6148
  0.1 4.4 %copy-start.3 = (bf16[1,4,16,512]{3,2,1,0:T(8,128)(2,1)S(1)}, bf16[1,4,16,512]{3,2,1,0:T(8,128)(2,1)}, u32[]{:S(2)}) copy-start(bf16[1,4,16,512]{3,2,1,0:T(8,128)(2,1)} %param.16) | copy-start | bytes 196612
  0.1 11.6 %copy-start.2 = (bf16[4,16,512]{2,1,0:T(8,128)(2,1)S(1)}, bf16[4,16,512]{2,1,0:T(8,128)(2,1)}, u32[]{:S(2)}) copy-start(bf16[4,16,512]{2,1,0:T(8,128)(2,1)} %x_in.1) | copy-start | bytes 196612
  0.1 11.6 %copy-start.8 = (f32[1,512]{1,0:T(1,128)S(1)}, f32[1,512]{1,0:T(1,128)}, u32[]{:S(2)}) copy-start(f32[1,512]{1,0:T(1,128)} %gain.3) | copy-start | bytes 6148
  1.9 9.8 %collective-permute-start = (bf16[528,128]{1,0:T(8,128)(2,1)S(1)}, bf16[528,128]{1,0:T(8,128)(2,1)S(1)}, u32[]{:S(2)}, u32[]{:S(2)}) collective-permute-start(bf16[528,128]{1,0:T(8,128)(2,1)S(1)} %crossing.1), channel_id=1, source_target_pairs={{0,32},{32,64},{64,96},{96,128},{128,160},{160,192},{192,224},{224... | collective-permute-start | bytes 405512 | tf_op jit(solution)/shard_map/ppermute | solution.py:279
  12.0 15.8 %collective-permute-start.1 = (f32[4,16,512]{2,1,0:T(8,128)S(1)}, f32[4,16,512]{2,1,0:T(8,128)S(1)}, u32[]{:S(2)}, u32[]{:S(2)}) collective-permute-start(f32[4,16,512]{2,1,0:T(8,128)S(1)} %get-tuple-element.25.refs_0_), channel_id=1, source_target_pairs={{0,16},{16,0},{1,17},{17,1},{2,18},{18,2},{3,19},{19,3},{4,20},{20... | collective-permute-start | bytes 393224 | tf_op jit(solution)/shard_map/ppermute | solution.py:311

commit v3 on v2

--- a/solution.py
+++ b/solution.py
@@ -24,36 +24,41 @@
 
 
 def crossing_kernel(parent_hbm, state, window_hbm, out, parent, window, sems):
-    get_parent = pltpu.make_async_copy(parent_hbm, parent, sems.at[0])
-    get_parent.start()
-    get_window = pltpu.make_async_copy(window_hbm, window, sems.at[1])
-    get_window.start()
     slots = window.shape[1]
     nrows = state.shape[1]
-    count = lax.axis_size("roll")
-    following = lax.rem(lax.axis_index("roll") + 1, count)
-    begin = following * slots
-    get_parent.wait()
-
-    row = jnp.int32(0)
-    for s in range(slots):
-        found = parent[begin + s] - begin + slots
-        row = jnp.where(found < slots, found, row)
-    row = jnp.clip(row, 0, slots - 1)
-    copy = pltpu.make_async_copy(state.at[row], out.at[pl.ds(0, nrows)], sems.at[2])
-    copy.start()
     taps, _, width = window.shape
     groups = width // 128
-    pick = lax.broadcasted_iota(jnp.int32, (slots, 1), 0) == row
-    place = lax.broadcasted_iota(jnp.int32, (out.shape[0] - nrows, 128), 0)
-    packed = jnp.zeros(place.shape, F32)
-    get_window.wait()
-    for k in range(taps):
-        chosen = jnp.sum(jnp.where(pick, window[k].astype(F32), 0.0), axis=0, keepdims=True)
-        for j in range(groups):
-            packed = jnp.where(place == k * groups + j, chosen[:, j * 128:(j + 1) * 128], packed)
-    out[pl.ds(nrows, place.shape[0])] = packed.astype(BF16)
-    copy.wait()
+    following = lax.axis_index("roll") + 1
+
+    @pl.when(following == lax.axis_size("roll"))
+    def _():
+        out[...] = jnp.zeros(out.shape, BF16)
+
+    @pl.when(following < lax.axis_size("roll"))
+    def _():
+        get_parent = pltpu.make_async_copy(parent_hbm, parent, sems.at[0])
+        get_parent.start()
+        get_window = pltpu.make_async_copy(window_hbm, window, sems.at[1])
+        get_window.start()
+        begin = following * slots
+        get_parent.wait()
+        row = jnp.int32(0)
+        for s in range(slots):
+            found = parent[begin + s] - begin + slots
+            row = jnp.where(found < slots, found, row)
+        row = jnp.clip(row, 0, slots - 1)
+        copy = pltpu.make_async_copy(state.at[row], out.at[pl.ds(0, nrows)], sems.at[2])
+        copy.start()
+        pick = lax.broadcasted_iota(jnp.int32, (slots, 1), 0) == row
+        place = lax.broadcasted_iota(jnp.int32, (out.shape[0] - nrows, 128), 0)
+        packed = jnp.zeros(place.shape, F32)
+        get_window.wait()
+        for k in range(taps):
+            chosen = jnp.sum(jnp.where(pick, window[k].astype(F32), 0.0), axis=0, keepdims=True)
+            for j in range(groups):
+                packed = jnp.where(place == k * groups + j, chosen[:, j * 128:(j + 1) * 128], packed)
+        out[pl.ds(nrows, place.shape[0])] = packed.astype(BF16)
+        copy.wait()
 
 
 def local_kernel(

time: 38.5 us -> 36.8 us (0.956)
  waiting for transfers between devices: 5.68 us -> 3.06 us
  starting transfers between devices: 3.86 us -> 4.99 us
    ppermute x1, waiting for transfers between devices: 5.68 us -> 3.05 us  [body(): lax.ppermute(leaving, 'roll', [(i, (i + 1) % count) for i in range(count)])]
    ppermute x1, starting transfers between devices: 1.32 us -> 2.44 us  [body(): lax.ppermute(own, 'pipe', [(i, (i + 1) % pipes) for i in range(pipes)])]
where the time goes in v3:
time: 36.8 us; the launch traced here: 36.7 us
  blocking collectives  23.8 us (65%)
  starting transfers between devices  4.99 us (14%)
  Pallas kernels  4.6 us (12%)
  waiting for transfers between devices  3.06 us (8%)
    all_to_all x1, blocking collectives, body(): sums = lax.all_to_all(sums, ('pipe', 'tp'), 0, 0)  14.3 us
    all_to_all x1, blocking collectives, body(): sums = lax.all_to_all(sums, 'tp', 0, 0)  9.48 us
    ppermute x1, waiting for transfers between devices, body(): lax.ppermute(leaving, 'roll', [(i, (i + 1) % count) for i in range(count)])  3.05 us
    ppermute x1, starting transfers between devices, body(): lax.ppermute(leaving, 'roll', [(i, (i + 1) % count) for i in range(count)])  2.54 us
    ppermute x1, starting transfers between devices, body(): lax.ppermute(own, 'pipe', [(i, (i + 1) % pipes) for i in range(pipes)])  2.44 us
    pallas_call x1, Pallas kernels, body(): pl.pallas_call(crossing_kernel, out_shape=shape((rows + 16, nstate), BF16...  1.78 us
    pallas_call x1, Pallas kernels, body(): pl.pallas_call(local_kernel, out_shape=(shape((steps, slots, width), F32)...  1.49 us
    pallas_call x1, Pallas kernels, body(): pl.pallas_call(lambda sums, norm, gated, gain, out: last_kernel(sums, nor...  0.74 us
  transfers between devices with their start and end apart: 2, of which 1 were waited for; matrix products, arithmetic and copies ran while one was open for 0% of the time, Pallas kernels for 4%

profile of v3, /device:TPU:1, one launch (start us, length us, event | category | flops | bytes accessed | tf_op | source)
XLA Modules:
  0.0 36.7 jit_solution(12060315315917350897)
XLA Ops:
  0.0 0.0 copy-start.12
  0.0 0.0 copy-start.11
  0.0 0.0 copy-start.10
  0.0 0.0 copy-start.4
  0.0 0.0 copy-start.5
  0.1 0.0 copy-start.6
  0.1 0.0 copy-start.7
  0.1 0.0 copy-start.3
  0.1 0.0 copy-start.2
  0.1 0.0 copy-start.8
  0.1 1.8 %crossing.1 = bf16[528,128]{1,0:T(8,128)(2,1)S(1)} custom-call(s32[128]{0:T(128)} %parent.1, bf16[16,512,128]{2,1,0:T(8,128)(2,1)} %bitcast.12, bf16[3,16,512]{2,1,0:T(8,128)(2,1)} %bitcast.14), custom_call_target="tpu_custom_call" | custom-call | tf_op jit(solution)/shard_map/crossing/pallas_call | solution.py:271
  1.9 2.5 %collective-permute-start = (bf16[528,128]{1,0:T(8,128)(2,1)S(1)}, bf16[528,128]{1,0:T(8,128)(2,1)S(1)}, u32[]{:S(2)}, u32[]{:S(2)}) collective-permute-start(bf16[528,128]{1,0:T(8,128)(2,1)S(1)} %crossing.1), channel_id=1, source_target_pairs={{0,32},{32,64},{64,96},{96,128},{128,160},{160,192},{192,224},{224... | collective-permute-start | bytes 405512 | tf_op jit(solution)/shard_map/ppermute | solution.py:284
  4.4 0.0 copy-done.9
  4.4 0.0 copy-done.1
  4.4 0.0 copy-done
  4.5 1.5 %local.1 = (f32[4,16,512]{2,1,0:T(8,128)S(1)}, f32[4,16,512]{2,1,0:T(8,128)S(1)}, f32[10,16,512]{2,1,0:T(8,128)S(1)}, f32[3,16,512]{2,1,0:T(8,128)S(1)}, bf16[64...) custom-call(s32[128]{0:T(128)S(1)} %copy-done.9, bf16[16,512,128]{2,1,0:T(8,128)(2,1)S(1)} %bitcast.13, ...), custom_call_target="tpu_custom_call" | custom-call | flops 20000000 | bytes 4000000 | tf_op jit(solution)/shard_map/local/pallas_call | solution.py:286
  6.0 3.1 %collective-permute-done.arrived = bf16[528,128]{1,0:T(8,128)(2,1)S(1)} collective-permute-done((bf16[528,128]{1,0:T(8,128)(2,1)S(1)}, bf16[528,128]{1,0:T(8,128)(2,1)S(1)}, u32[]{:S(2)}, u32[]{:S(2)}) %collective-permute-start) | collective-permute-done | bytes 135200 | tf_op jit(solution)/shard_map/ppermute | solution.py:284
  9.1 0.3 first.1
  9.4 2.4 %collective-permute-start.1 = (f32[4,16,512]{2,1,0:T(8,128)S(1)}, f32[4,16,512]{2,1,0:T(8,128)S(1)}, u32[]{:S(2)}, u32[]{:S(2)}) collective-permute-start(f32[4,16,512]{2,1,0:T(8,128)S(1)} %get-tuple-element.25.refs_0_), channel_id=1, source_target_pairs={{0,16},{16,0},{1,17},{17,1},{2,18},{18,2},{3,19},{19,3},{4,20},{20... | collective-permute-start | bytes 393224 | tf_op jit(solution)/shard_map/ppermute | solution.py:316
  11.8 14.3 %all_to_all.10.sums = f32[32,8,128]{2,1,0:T(8,128)S(1)} all-to-all(f32[32,8,128]{2,1,0:T(8,128)S(1)} %get-tuple-element.24), channel_id=1, replica_groups=mesh['roll'=8,'pipe'=2,'tp'=16] {'pipe','tp'}, dimensions={0} | all-to-all | bytes 262144 | tf_op jit(solution)/shard_map/all_to_all | solution.py:317
  26.1 0.0 collective-permute-done.1.refs_1_
  26.1 0.3 second.1
  26.4 9.5 %all_to_all.11.sums = f32[16,8,128]{2,1,0:T(8,128)S(1)} all-to-all(f32[16,8,128]{2,1,0:T(8,128)S(1)} %get-tuple-element.28), channel_id=1, replica_groups=mesh['roll'=8,'pipe'=2,'tp'=16] {'tp'}, dimensions={0} | all-to-all | bytes 131072 | tf_op jit(solution)/shard_map/all_to_all | solution.py:331
  35.9 0.7 %last.1 = bf16[4,16,512]{2,1,0:T(8,128)(2,1)} custom-call(f32[16,8,128]{2,1,0:T(8,128)S(1)} %all_to_all.11.sums, bf16[4,16,512]{2,1,0:T(8,128)(2,1)S(1)} %get-tuple-element.29.norm, f32[4,16,512]{2,1,0:T(8,128)S(1)} %get-tuple-element.30.gated, f32[1,512]{1,0:T(1,128)S(1)} %copy-done.8), custom_call_target="tpu_custom_call" | custom-call | tf_op jit(solution)/shard_map/last/pallas_call | solution.py:333
  (13 shorter events, 0.0 us)
Async XLA Ops:
  0.0 4.4 %copy-start.9 = (s32[128]{0:T(128)S(1)}, s32[128]{0:T(128)}, u32[]{:S(2)}) copy-start(s32[128]{0:T(128)} %parent.1) | copy-start | bytes 1540
  0.0 4.4 %copy-start.1 = (bf16[1,16,3,512]{3,1,2,0:T(8,128)(2,1)S(1)}, bf16[1,16,3,512]{3,1,2,0:T(8,128)(2,1)}, u32[]{:S(2)}) copy-start(bf16[1,16,3,512]{3,1,2,0:T(8,128)(2,1)} %param.14) | copy-start | bytes 147460
  0.0 4.4 %copy-start = (bf16[1,16,8,64,128]{4,3,2,1,0:T(8,128)(2,1)S(1)}, bf16[1,16,8,64,128]{4,3,2,1,0:T(8,128)(2,1)}, u32[]{:S(2)}) copy-start(bf16[1,16,8,64,128]{4,3,2,1,0:T(8,128)(2,1)} %param.13) | copy-start | bytes 6291460
  0.0 4.4 %copy-start.12 = (f32[1,8]{1,0:T(1,128)S(1)}, f32[1,8]{1,0:T(1,128)}, u32[]{:S(2)}) copy-start(f32[1,8]{1,0:T(1,128)} %skip_d.1) | copy-start | bytes 100
  0.0 4.4 %copy-start.11 = (f32[1,8]{1,0:T(1,128)S(1)}, f32[1,8]{1,0:T(1,128)}, u32[]{:S(2)}) copy-start(f32[1,8]{1,0:T(1,128)} %dt_bias.1) | copy-start | bytes 100
  0.0 4.4 %copy-start.10 = (f32[1,8]{1,0:T(1,128)S(1)}, f32[1,8]{1,0:T(1,128)}, u32[]{:S(2)}) copy-start(f32[1,8]{1,0:T(1,128)} %a_log.1) | copy-start | bytes 100
  0.0 4.4 %copy-start.4 = (bf16[1,4,512]{2,1,0:T(4,128)(2,1)S(1)}, bf16[1,4,512]{2,1,0:T(4,128)(2,1)}, u32[]{:S(2)}) copy-start(bf16[1,4,512]{2,1,0:T(4,128)(2,1)} %param.20) | copy-start | bytes 12292
  0.0 4.4 %copy-start.5 = (bf16[1,4,16,128]{3,2,1,0:T(8,128)(2,1)S(1)}, bf16[1,4,16,128]{3,2,1,0:T(8,128)(2,1)}, u32[]{:S(2)}) copy-start(bf16[1,4,16,128]{3,2,1,0:T(8,128)(2,1)} %param.19) | copy-start | bytes 49156
  0.1 4.4 %copy-start.6 = (bf16[1,4,16,128]{3,2,1,0:T(8,128)(2,1)S(1)}, bf16[1,4,16,128]{3,2,1,0:T(8,128)(2,1)}, u32[]{:S(2)}) copy-start(bf16[1,4,16,128]{3,2,1,0:T(8,128)(2,1)} %param.18) | copy-start | bytes 49156
  0.1 4.4 %copy-start.7 = (f32[1,4,16,8]{2,3,1,0:T(8,128)S(1)}, f32[1,4,16,8]{2,3,1,0:T(8,128)}, u32[]{:S(2)}) copy-start(f32[1,4,16,8]{2,3,1,0:T(8,128)} %param.17) | copy-start | bytes 6148
  0.1 4.4 %copy-start.3 = (bf16[1,4,16,512]{3,2,1,0:T(8,128)(2,1)S(1)}, bf16[1,4,16,512]{3,2,1,0:T(8,128)(2,1)}, u32[]{:S(2)}) copy-start(bf16[1,4,16,512]{3,2,1,0:T(8,128)(2,1)} %param.16) | copy-start | bytes 196612
  0.1 9.0 %copy-start.2 = (bf16[4,16,512]{2,1,0:T(8,128)(2,1)S(1)}, bf16[4,16,512]{2,1,0:T(8,128)(2,1)}, u32[]{:S(2)}) copy-start(bf16[4,16,512]{2,1,0:T(8,128)(2,1)} %x_in.1) | copy-start | bytes 196612
  0.1 9.0 %copy-start.8 = (f32[1,512]{1,0:T(1,128)S(1)}, f32[1,512]{1,0:T(1,128)}, u32[]{:S(2)}) copy-start(f32[1,512]{1,0:T(1,128)} %gain.3) | copy-start | bytes 6148
  1.9 7.2 %collective-permute-start = (bf16[528,128]{1,0:T(8,128)(2,1)S(1)}, bf16[528,128]{1,0:T(8,128)(2,1)S(1)}, u32[]{:S(2)}, u32[]{:S(2)}) collective-permute-start(bf16[528,128]{1,0:T(8,128)(2,1)S(1)} %crossing.1), channel_id=1, source_target_pairs={{0,32},{32,64},{64,96},{96,128},{128,160},{160,192},{192,224},{224... | collective-permute-start | bytes 405512 | tf_op jit(solution)/shard_map/ppermute | solution.py:284
  9.4 16.7 %collective-permute-start.1 = (f32[4,16,512]{2,1,0:T(8,128)S(1)}, f32[4,16,512]{2,1,0:T(8,128)S(1)}, u32[]{:S(2)}, u32[]{:S(2)}) collective-permute-start(f32[4,16,512]{2,1,0:T(8,128)S(1)} %get-tuple-element.25.refs_0_), channel_id=1, source_target_pairs={{0,16},{16,0},{1,17},{17,1},{2,18},{18,2},{3,19},{19,3},{4,20},{20... | collective-permute-start | bytes 393224 | tf_op jit(solution)/shard_map/ppermute | solution.py:316

commit v4 on v3

--- a/solution.py
+++ b/solution.py
@@ -225,17 +225,21 @@
     return pre
 
 
-def second_kernel(sums, own, other, base, mix, conv_part, conv, channels, norm_out, gated_out, sums_out):
-    steps, slots, width = own.shape
+def finish_kernel(sums, own, channels, out):
+    steps, slots, _ = own.shape
+    scale = row_scales(sums[...], channels, steps * slots)
+    for t in range(steps):
+        out[t] = scaled(own[t], scale[t * slots:(t + 1) * slots]).astype(BF16)
+
+
+def second_kernel(sums, other, base, mix, conv_part, conv, channels, gated_out, sums_out):
+    steps, slots, width = other.shape
     taps = conv_part.shape[0]
     scale = row_scales(sums[...], channels, steps * slots)
-    first = lax.axis_index("pipe") == 0
     rows = []
     for t in range(steps):
-        row = jnp.where(first, own[t], other[t])
-        row = scaled(row, scale[t * slots:(t + 1) * slots]).astype(BF16)
-        norm_out[t] = row
-        rows.append(row.astype(F32))
+        row = scaled(other[t], scale[t * slots:(t + 1) * slots])
+        rows.append(row.astype(BF16).astype(F32))
     weight = [conv[pl.ds(k, 1), :].astype(F32) for k in range(taps + 1)]
     pre = with_inputs([conv_part[t] for t in range(taps)], weight, rows)
     gated = gated_rows(pre, [base[t] for t in range(steps)], [mix[i] for i in range(mix.shape[0])], steps)
@@ -244,13 +248,11 @@
     sums_out[...] = jnp.broadcast_to(square_sums(gated)[None], sums_out.shape)
 
 
-def last_kernel(sums, norm, gated, gain, channels, out):
+def last_kernel(sums, gated, gain, channels, out):
     steps, slots, width = gated.shape
     scale = row_scales(sums[...], channels, steps * slots)
-    first = lax.axis_index("pipe") == 0
-    for t in range(steps):
-        row = scaled(gated[t], scale[t * slots:(t + 1) * slots]) * gain[...]
-        out[t] = jnp.where(first, norm[t].astype(F32), row).astype(BF16)
+    for t in range(steps):
+        out[t] = (scaled(gated[t], scale[t * slots:(t + 1) * slots]) * gain[...]).astype(BF16)
 
 
 def body(ssm_state, conv_window, x_in, z_gate, dt_raw, b_in, c_in, conv_weight, a_log, dt_bias, skip_d, norm_gain, parent):
@@ -306,7 +308,7 @@
             shape((steps, slots, width), F32),
             shape((taps, slots, width), F32),
             shape((steps, slots, width), F32),
-            shape((pipes * tp, 8, 128), F32),
+            shape((pipes * tp, 1, 128), F32),
         ),
         in_specs=[VMEM] * 10,
         out_specs=(VMEM,) * 4,
@@ -314,30 +316,44 @@
         name="first",
     )(arrived, base, reach, mix, conv_part, cmask, wmask, conv_weight[0], x_in, norm_gain)
     other = lax.ppermute(own, "pipe", [(i, (i + 1) % pipes) for i in range(pipes)])
+    section = lax.axis_index("pipe")
+    sums, section = lax.optimization_barrier((sums, section))
     sums = lax.all_to_all(sums, ("pipe", "tp"), 0, 0)
-
-    norm, gated, sums = pl.pallas_call(
-        lambda sums, *refs: second_kernel(sums.at[pl.ds(0, tp)], *refs[:6], channels, *refs[6:]),
-        out_shape=(
-            shape((steps, slots, width), BF16),
-            shape((steps, slots, width), F32),
-            shape((tp, 8, 128), F32),
-        ),
-        in_specs=[VMEM] * 7,
-        out_specs=(VMEM,) * 3,
-        compiler_params=PARAMS,
-        name="second",
-    )(sums, own, other, base, mix, conv_part, conv_weight[0])
-    sums = lax.all_to_all(sums, "tp", 0, 0)
-
-    result = pl.pallas_call(
-        lambda sums, norm, gated, gain, out: last_kernel(sums, norm, gated, gain, channels, out),
-        out_shape=shape((steps, slots, width), BF16),
-        in_specs=[VMEM] * 4,
-        out_specs=VMEM,
-        compiler_params=PARAMS,
-        name="last",
-    )(sums, norm, gated, norm_gain)
+    sums, section = lax.optimization_barrier((sums, section))
+
+    def first_section(sums, own, other, base, mix, conv_part, conv, gain):
+        return pl.pallas_call(
+            lambda sums, own, out: finish_kernel(sums.at[pl.ds(0, tp)], own, channels, out),
+            out_shape=shape((steps, slots, width), BF16),
+            in_specs=[VMEM] * 2,
+            out_specs=VMEM,
+            compiler_params=PARAMS,
+            name="finish",
+        )(sums, own)
+
+    def second_section(sums, own, other, base, mix, conv_part, conv, gain):
+        gated, sums = pl.pallas_call(
+            lambda sums, *refs: second_kernel(sums.at[pl.ds(0, tp)], *refs[:5], channels, *refs[5:]),
+            out_shape=(shape((steps, slots, width), F32), shape((tp, 1, 128), F32)),
+            in_specs=[VMEM] * 6,
+            out_specs=(VMEM,) * 2,
+            compiler_params=PARAMS,
+            name="second",
+        )(sums, other, base, mix, conv_part, conv)
+        sums = lax.all_to_all(sums, "tp", 0, 0)
+        return pl.pallas_call(
+            lambda sums, gated, gain, out: last_kernel(sums, gated, gain, channels, out),
+            out_shape=shape((steps, slots, width), BF16),
+            in_specs=[VMEM] * 3,
+            out_specs=VMEM,
+            compiler_params=PARAMS,
+            name="last",
+        )(sums, gated, gain)
+
+    result = lax.cond(
+        section == 0, first_section, second_section,
+        sums, own, other, base, mix, conv_part, conv_weight[0], norm_gain,
+    )
     return result[None]
 
 

time: 36.8 us -> 35.8 us (0.973)
  blocking collectives: 23.8 us -> 22.8 us
  Pallas kernels: 4.6 us -> 3.96 us
  local copies, waits for them, and re-layouts: 0.05 us -> 0.68 us
    all_to_all x1, blocking collectives: 14.3 us -> 13.6 us  [body(): sums = lax.all_to_all(sums, ('pipe', 'tp'), 0, 0)]
    pallas_call x2, Pallas kernels: 1.04 us -> 0.39 us  [the longest x1 0.28 us: second_section(): pl.pallas_call(lambda sums, *refs: second_kernel(sums.at[pl.ds(0, tp)], *...]
    unnamed x26 -> x28, local copies, waits for them, and re-layouts: 0.05 us -> 0.68 us
where the time goes in v4:
time: 35.8 us; the launch traced here: 35.7 us
  blocking collectives  22.8 us (64%)
  starting transfers between devices  4.99 us (14%)
  Pallas kernels  3.96 us (11%)
  waiting for transfers between devices  3.05 us (9%)
  local copies, waits for them, and re-layouts  0.68 us (2%)
    all_to_all x1, blocking collectives, body(): sums = lax.all_to_all(sums, ('pipe', 'tp'), 0, 0)  13.6 us
    all_to_all x1, blocking collectives, second_section(): sums = lax.all_to_all(sums, 'tp', 0, 0)  9.15 us
    ppermute x1, waiting for transfers between devices, body(): lax.ppermute(leaving, 'roll', [(i, (i + 1) % count) for i in range(count)])  3.05 us
    ppermute x1, starting transfers between devices, body(): lax.ppermute(leaving, 'roll', [(i, (i + 1) % count) for i in range(count)])  2.54 us
    ppermute x1, starting transfers between devices, body(): lax.ppermute(own, 'pipe', [(i, (i + 1) % pipes) for i in range(pipes)])  2.44 us
    pallas_call x1, Pallas kernels, body(): pl.pallas_call(crossing_kernel, out_shape=shape((rows + 16, nstate), BF16...  1.78 us
    pallas_call x1, Pallas kernels, body(): pl.pallas_call(local_kernel, out_shape=(shape((steps, slots, width), F32)...  1.49 us
  transfers between devices with their start and end apart: 2, of which 1 were waited for; matrix products, arithmetic and copies ran while one was open for 0% of the time, Pallas kernels for 4%

profile of v4, /device:TPU:1, one launch (start us, length us, event | category | flops | bytes accessed | tf_op | source)
XLA Modules:
  0.0 35.7 jit_solution(6700426009957172745)
XLA Ops:
  0.0 0.0 copy-start.12
  0.0 0.0 copy-start.3
  0.0 0.0 copy-start.4
  0.0 0.0 copy-start.5
  0.0 0.0 copy-start.6
  0.1 0.0 copy-start.8
  0.1 0.0 copy-start.9
  0.1 0.0 copy-start.10
  0.1 0.0 copy-start.2
  0.1 0.0 copy-start.13
  0.1 1.8 %crossing.1 = bf16[528,128]{1,0:T(8,128)(2,1)S(1)} custom-call(s32[128]{0:T(128)} %parent.1, bf16[16,512,128]{2,1,0:T(8,128)(2,1)} %bitcast.13, bf16[3,16,512]{2,1,0:T(8,128)(2,1)} %bitcast.15), custom_call_target="tpu_custom_call" | custom-call | tf_op jit(solution)/shard_map/crossing/pallas_call | solution.py:273
  1.9 2.5 %collective-permute-start = (bf16[528,128]{1,0:T(8,128)(2,1)S(1)}, bf16[528,128]{1,0:T(8,128)(2,1)S(1)}, u32[]{:S(2)}, u32[]{:S(2)}) collective-permute-start(bf16[528,128]{1,0:T(8,128)(2,1)S(1)} %crossing.1), channel_id=1, source_target_pairs={{0,32},{32,64},{64,96},{96,128},{128,160},{160,192},{192,224},{224... | collective-permute-start | bytes 405512 | tf_op jit(solution)/shard_map/ppermute | solution.py:286
  4.5 1.5 %local.1 = (f32[4,16,512]{2,1,0:T(8,128)S(1)}, f32[4,16,512]{2,1,0:T(8,128)S(1)}, f32[10,16,512]{2,1,0:T(8,128)S(1)}, f32[3,16,512]{2,1,0:T(8,128)S(1)}, bf16[64...) custom-call(s32[128]{0:T(128)S(1)} %copy-done.7, bf16[16,512,128]{2,1,0:T(8,128)(2,1)S(1)} %bitcast.14, ...), custom_call_target="tpu_custom_call" | custom-call | flops 20000000 | bytes 4000000 | tf_op jit(solution)/shard_map/local/pallas_call | solution.py:288
  6.0 3.0 %collective-permute-done.arrived = bf16[528,128]{1,0:T(8,128)(2,1)S(1)} collective-permute-done((bf16[528,128]{1,0:T(8,128)(2,1)S(1)}, bf16[528,128]{1,0:T(8,128)(2,1)S(1)}, u32[]{:S(2)}, u32[]{:S(2)}) %collective-permute-start) | collective-permute-done | bytes 135200 | tf_op jit(solution)/shard_map/ppermute | solution.py:286
  9.1 0.3 first.1
  9.4 2.4 %collective-permute-start.1 = (f32[4,16,512]{2,1,0:T(8,128)S(1)}, f32[4,16,512]{2,1,0:T(8,128)S(1)}, u32[]{:S(2)}, u32[]{:S(2)}) collective-permute-start(f32[4,16,512]{2,1,0:T(8,128)S(1)} %get-tuple-element.63), channel_id=1, source_target_pairs={{0,16},{16,0},{1,17},{17,1},{2,18},{18,2},{3,19},{19,3},{4,20},{20... | collective-permute-start | bytes 393224 | tf_op jit(solution)/shard_map/ppermute | solution.py:318
  11.8 13.6 %all_to_all.10 = f32[32,1,128]{2,1,0:T(1,128)S(1)} all-to-all(f32[32,1,128]{2,1,0:T(1,128)S(1)} %get-tuple-element.59), channel_id=1, replica_groups=mesh['roll'=8,'pipe'=2,'tp'=16] {'pipe','tp'}, dimensions={0} | all-to-all | bytes 32768 | tf_op jit(solution)/shard_map/all_to_all | solution.py:321
  25.5 0.0 collective-permute-done.1
  25.5 9.6 %conditional.1 = (bf16[1,4,16,512]{3,2,1,0:T(8,128)(2,1)S(1)}) conditional(s32[]{:T(128)} %convert_element_type.3, (f32[32,1,128]{2,1,0:T(1,128)S(1)}, f32[4,16,512]{2,1,0:T(8,128)S(1)}, f32[4,16,512]{2,1,0:T(8,128)S(1)}, f32[10,16,512]{2,1,0:T(8,128)S(1)}, f32[3,16,512]{2,1,0:T(8,128)S(1)}, /*index=5*/bf16[4,512]{1,0:T(4,128)(2,1)S(1)}, ...), branch_computations={%region_0.0_spmd, %region_1.0_spmd} | conditional | bytes 16392 | solution.py:353
  25.5 0.3 second.1
  25.7 9.2 %all_to_all.9.sums = f32[16,1,128]{2,1,0:T(1,128)S(1)} all-to-all(f32[16,1,128]{2,1,0:T(1,128)S(1)} %get-tuple-element.33), channel_id=1, replica_groups=mesh['roll'=8,'pipe'=2,'tp'=16] {'tp'}, dimensions={0} | all-to-all | bytes 16384 | tf_op jit(solution)/shard_map/cond/branch_0_fun/all_to_all | solution.py:343
  34.9 0.1 last.1
  35.0 0.0 copy-start.11
  35.0 0.6 %copy-done.11 = bf16[1,4,16,512]{3,2,1,0:T(8,128)(2,1)} copy-done((bf16[1,4,16,512]{3,2,1,0:T(8,128)(2,1)}, bf16[1,4,16,512]{3,2,1,0:T(8,128)(2,1)S(1)}, u32[]{:S(2)}) %copy-start.11) | copy-done | bytes 65560
  (16 shorter events, 0.0 us)
Async XLA Ops:
  0.0 4.4 %copy-start = (bf16[1,16,8,64,128]{4,3,2,1,0:T(8,128)(2,1)S(1)}, bf16[1,16,8,64,128]{4,3,2,1,0:T(8,128)(2,1)}, u32[]{:S(2)}) copy-start(bf16[1,16,8,64,128]{4,3,2,1,0:T(8,128)(2,1)} %param.15) | copy-start | bytes 6291460
  0.0 4.4 %copy-start.1 = (bf16[1,16,3,512]{3,1,2,0:T(8,128)(2,1)S(1)}, bf16[1,16,3,512]{3,1,2,0:T(8,128)(2,1)}, u32[]{:S(2)}) copy-start(bf16[1,16,3,512]{3,1,2,0:T(8,128)(2,1)} %param.16) | copy-start | bytes 147460
  0.0 4.4 %copy-start.7 = (s32[128]{0:T(128)S(1)}, s32[128]{0:T(128)}, u32[]{:S(2)}) copy-start(s32[128]{0:T(128)} %parent.1) | copy-start | bytes 1540
  0.0 4.4 %copy-start.12 = (bf16[1,4,512]{2,1,0:T(4,128)(2,1)S(1)}, bf16[1,4,512]{2,1,0:T(4,128)(2,1)}, u32[]{:S(2)}) copy-start(bf16[1,4,512]{2,1,0:T(4,128)(2,1)} %param.22) | copy-start | bytes 12292
  0.0 4.4 %copy-start.3 = (bf16[1,4,16,512]{3,2,1,0:T(8,128)(2,1)S(1)}, bf16[1,4,16,512]{3,2,1,0:T(8,128)(2,1)}, u32[]{:S(2)}) copy-start(bf16[1,4,16,512]{3,2,1,0:T(8,128)(2,1)} %param.18) | copy-start | bytes 196612
  0.0 4.4 %copy-start.4 = (bf16[1,4,16,128]{3,2,1,0:T(8,128)(2,1)S(1)}, bf16[1,4,16,128]{3,2,1,0:T(8,128)(2,1)}, u32[]{:S(2)}) copy-start(bf16[1,4,16,128]{3,2,1,0:T(8,128)(2,1)} %param.21) | copy-start | bytes 49156
  0.0 4.4 %copy-start.5 = (bf16[1,4,16,128]{3,2,1,0:T(8,128)(2,1)S(1)}, bf16[1,4,16,128]{3,2,1,0:T(8,128)(2,1)}, u32[]{:S(2)}) copy-start(bf16[1,4,16,128]{3,2,1,0:T(8,128)(2,1)} %param.20) | copy-start | bytes 49156
  0.0 4.4 %copy-start.6 = (f32[1,4,16,8]{2,3,1,0:T(8,128)S(1)}, f32[1,4,16,8]{2,3,1,0:T(8,128)}, u32[]{:S(2)}) copy-start(f32[1,4,16,8]{2,3,1,0:T(8,128)} %param.19) | copy-start | bytes 6148
  0.1 4.4 %copy-start.8 = (f32[1,8]{1,0:T(1,128)S(1)}, f32[1,8]{1,0:T(1,128)}, u32[]{:S(2)}) copy-start(f32[1,8]{1,0:T(1,128)} %a_log.1) | copy-start | bytes 100
  0.1 4.4 %copy-start.9 = (f32[1,8]{1,0:T(1,128)S(1)}, f32[1,8]{1,0:T(1,128)}, u32[]{:S(2)}) copy-start(f32[1,8]{1,0:T(1,128)} %dt_bias.1) | copy-start | bytes 100
  0.1 4.4 %copy-start.10 = (f32[1,8]{1,0:T(1,128)S(1)}, f32[1,8]{1,0:T(1,128)}, u32[]{:S(2)}) copy-start(f32[1,8]{1,0:T(1,128)} %skip_d.1) | copy-start | bytes 100
  0.1 9.0 %copy-start.2 = (bf16[4,16,512]{2,1,0:T(8,128)(2,1)S(1)}, bf16[4,16,512]{2,1,0:T(8,128)(2,1)}, u32[]{:S(2)}) copy-start(bf16[4,16,512]{2,1,0:T(8,128)(2,1)} %x_in.1) | copy-start | bytes 196612
  0.1 9.0 %copy-start.13 = (f32[1,512]{1,0:T(1,128)S(1)}, f32[1,512]{1,0:T(1,128)}, u32[]{:S(2)}) copy-start(f32[1,512]{1,0:T(1,128)} %gain.1) | copy-start | bytes 6148
  1.9 7.2 %collective-permute-start = (bf16[528,128]{1,0:T(8,128)(2,1)S(1)}, bf16[528,128]{1,0:T(8,128)(2,1)S(1)}, u32[]{:S(2)}, u32[]{:S(2)}) collective-permute-start(bf16[528,128]{1,0:T(8,128)(2,1)S(1)} %crossing.1), channel_id=1, source_target_pairs={{0,32},{32,64},{64,96},{96,128},{128,160},{160,192},{192,224},{224... | collective-permute-start | bytes 405512 | tf_op jit(solution)/shard_map/ppermute | solution.py:286
  9.4 16.1 %collective-permute-start.1 = (f32[4,16,512]{2,1,0:T(8,128)S(1)}, f32[4,16,512]{2,1,0:T(8,128)S(1)}, u32[]{:S(2)}, u32[]{:S(2)}) collective-permute-start(f32[4,16,512]{2,1,0:T(8,128)S(1)} %get-tuple-element.63), channel_id=1, source_target_pairs={{0,16},{16,0},{1,17},{17,1},{2,18},{18,2},{3,19},{19,3},{4,20},{20... | collective-permute-start | bytes 393224 | tf_op jit(solution)/shard_map/ppermute | solution.py:318
  35.0 0.6 %copy-start.11 = (bf16[1,4,16,512]{3,2,1,0:T(8,128)(2,1)}, bf16[1,4,16,512]{3,2,1,0:T(8,128)(2,1)S(1)}, u32[]{:S(2)}) copy-start(bf16[1,4,16,512]{3,2,1,0:T(8,128)(2,1)S(1)} %get-tuple-element.73) | copy-start | bytes 196612

commit v5 on v4

--- a/solution.py
+++ b/solution.py
@@ -180,8 +180,8 @@
     )
 
 
-def first_kernel(arrived, base, reach, mix, conv_part, cmask, wmask, conv, x_in, gain,
-                 base_out, conv_out, send_out, sums_out):
+def first_kernel(arrived, base, reach, mix, conv_part, cmask, wmask, conv, x_in, gain, *outs):
+    base_out, conv_out, send_out, sums_out = outs
     steps, slots, width = x_in.shape
     taps = conv_part.shape[0]
     nrows = arrived.shape[0] - 16
@@ -205,8 +205,19 @@
             part = part + weight[k] * rows[t + k]
         pre.append(conv_part[t] + mask * part)
         conv_out[t] = pre[t]
-    x_rows = [x_in[t].astype(F32) for t in range(steps)]
-    pre = with_inputs(pre, weight, x_rows)
+    send_first(pre, weight, start, mix, x_in, gain, send_out, sums_out)
+
+
+def alone_kernel(base, mix, conv_part, conv, x_in, gain, send_out, sums_out):
+    taps = conv_part.shape[0]
+    weight = [conv[pl.ds(k, 1), :].astype(F32) for k in range(taps + 1)]
+    start = [base[t] for t in range(base.shape[0])]
+    send_first([conv_part[t] for t in range(taps)], weight, start, mix, x_in, gain, send_out, sums_out)
+
+
+def send_first(pre, weight, start, mix, x_in, gain, send_out, sums_out):
+    steps = x_in.shape[0]
+    pre = with_inputs(pre, weight, [x_in[t].astype(F32) for t in range(steps)])
     gated = gated_rows(pre, start, [mix[i] for i in range(mix.shape[0])], steps)
     for t in range(steps):
         send_out[t] = gated[t] * gain[...]
@@ -301,25 +312,6 @@
         cost_estimate=pl.CostEstimate(flops=20_000_000, bytes_accessed=4_000_000, transcendentals=0),
         name="local",
     )(parent, state, window, c_in[0], b_in[0], raw, z_gate[0], conv_weight[0], a_log, dt_bias, skip_d)
-
-    base, conv_part, own, sums = pl.pallas_call(
-        first_kernel,
-        out_shape=(
-            shape((steps, slots, width), F32),
-            shape((taps, slots, width), F32),
-            shape((steps, slots, width), F32),
-            shape((pipes * tp, 1, 128), F32),
-        ),
-        in_specs=[VMEM] * 10,
-        out_specs=(VMEM,) * 4,
-        compiler_params=PARAMS,
-        name="first",
-    )(arrived, base, reach, mix, conv_part, cmask, wmask, conv_weight[0], x_in, norm_gain)
-    other = lax.ppermute(own, "pipe", [(i, (i + 1) % pipes) for i in range(pipes)])
-    section = lax.axis_index("pipe")
-    sums, section = lax.optimization_barrier((sums, section))
-    sums = lax.all_to_all(sums, ("pipe", "tp"), 0, 0)
-    sums, section = lax.optimization_barrier((sums, section))
 
     def first_section(sums, own, other, base, mix, conv_part, conv, gain):
         return pl.pallas_call(
@@ -350,9 +342,50 @@
             name="last",
         )(sums, gated, gain)
 
+    def after_first(base, mix, conv_part, own, sums, conv, gain):
+        other = lax.ppermute(own, "pipe", [(i, (i + 1) % pipes) for i in range(pipes)])
+        section = lax.axis_index("pipe")
+        sums, section = lax.optimization_barrier((sums, section))
+        sums = lax.all_to_all(sums, ("pipe", "tp"), 0, 0)
+        sums, section = lax.optimization_barrier((sums, section))
+        return lax.cond(
+            section == 0, first_section, second_section,
+            sums, own, other, base, mix, conv_part, conv, gain,
+        )
+
+    sent = (shape((steps, slots, width), F32), shape((pipes * tp, 1, 128), F32))
+
+    def alone(base, mix, conv_part, conv, x_in, gain):
+        own, sums = pl.pallas_call(
+            alone_kernel,
+            out_shape=sent,
+            in_specs=[VMEM] * 6,
+            out_specs=(VMEM,) * 2,
+            compiler_params=PARAMS,
+            name="alone",
+        )(base, mix, conv_part, conv, x_in, gain)
+        return after_first(base, mix, conv_part, own, sums, conv, gain)
+
+    def joined(early, arrived, base, reach, mix, conv_part, cmask, wmask, conv, x_in, gain):
+        base, conv_part, own, sums = pl.pallas_call(
+            first_kernel,
+            out_shape=(shape((steps, slots, width), F32), shape((taps, slots, width), F32)) + sent,
+            in_specs=[VMEM] * 10,
+            out_specs=(VMEM,) * 4,
+            compiler_params=PARAMS,
+            name="first",
+        )(arrived, base, reach, mix, conv_part, cmask, wmask, conv, x_in, gain)
+        return after_first(base, mix, conv_part, own, sums, conv, gain)
+
+    conv = conv_weight[0]
+    lone = lax.axis_index("roll") == 0
+    early = lax.cond(
+        lone, alone, lambda base, mix, conv_part, conv, x_in, gain: x_in,
+        base, mix, conv_part, conv, x_in, norm_gain,
+    )
     result = lax.cond(
-        section == 0, first_section, second_section,
-        sums, own, other, base, mix, conv_part, conv_weight[0], norm_gain,
+        lone, lambda early, *others: early, joined,
+        early, arrived, base, reach, mix, conv_part, cmask, wmask, conv, x_in, norm_gain,
     )
     return result[None]
 

time: 35.8 us -> 33.8 us (0.944)
  the two profiles are of different devices: /device:TPU:1 before, /device:TPU:129 now
where the time goes in v5:
time: 33.8 us; the launch traced here: 33.6 us
  blocking collectives  23 us (68%)
  Pallas kernels  4.6 us (14%)
  waiting for transfers between devices  2.69 us (8%)
  starting transfers between devices  2.45 us (7%)
  local copies, waits for them, and re-layouts  0.69 us (2%)
    all_to_all x1, blocking collectives, after_first(): sums = lax.all_to_all(sums, ('pipe', 'tp'), 0, 0)  13.8 us
    all_to_all x1, blocking collectives, second_section(): sums = lax.all_to_all(sums, 'tp', 0, 0)  9.15 us
    ppermute x1, waiting for transfers between devices, body(): lax.ppermute(leaving, 'roll', [(i, (i + 1) % count) for i in range(count)])  2.69 us
    pallas_call x1, Pallas kernels, body(): pl.pallas_call(crossing_kernel, out_shape=shape((rows + 16, nstate), BF16...  1.78 us
    ppermute x1, starting transfers between devices, after_first(): lax.ppermute(own, 'pipe', [(i, (i + 1) % pipes) for i in range(pipes)])  1.63 us
    pallas_call x1, Pallas kernels, body(): pl.pallas_call(local_kernel, out_shape=(shape((steps, slots, width), F32)...  1.49 us
    ppermute x1, starting transfers between devices, body(): lax.ppermute(leaving, 'roll', [(i, (i + 1) % count) for i in range(count)])  0.82 us
    pallas_call x1, Pallas kernels, second_section(): pl.pallas_call(lambda sums, gated, gain, out: last_kernel(sums, gated, ga...  0.74 us
  transfers between devices with their start and end apart: 2, of which 1 were waited for; matrix products, arithmetic and copies ran while one was open for 2% of the time, Pallas kernels for 4%

profile of v5, /device:TPU:129, one launch (start us, length us, event | category | flops | bytes accessed | tf_op | source)
XLA Modules:
  0.0 33.6 jit_solution(9536583796017599148)
XLA Ops:
  0.0 0.0 copy-start.9
  0.0 0.0 copy-start.8
  0.0 0.0 copy-start.7
  0.0 0.0 copy-start.11
  0.0 0.0 copy-start.3
  0.1 0.0 copy-start.4
  0.1 1.8 %crossing.1 = bf16[528,128]{1,0:T(8,128)(2,1)S(1)} custom-call(s32[128]{0:T(128)} %parent.1, bf16[16,512,128]{2,1,0:T(8,128)(2,1)} %bitcast.14, bf16[3,16,512]{2,1,0:T(8,128)(2,1)} %bitcast.16), custom_call_target="tpu_custom_call" | custom-call | tf_op jit(solution)/shard_map/crossing/pallas_call | solution.py:284
  1.9 0.8 %collective-permute-start.2 = (bf16[528,128]{1,0:T(8,128)(2,1)S(1)}, bf16[528,128]{1,0:T(8,128)(2,1)S(1)}, u32[]{:S(2)}, u32[]{:S(2)}) collective-permute-start(bf16[528,128]{1,0:T(8,128)(2,1)S(1)} %crossing.1), channel_id=1, source_target_pairs={{0,32},{32,64},{64,96},{96,128},{128,160},{160,192},{192,224},{224... | collective-permute-start | bytes 405512 | tf_op jit(solution)/shard_map/ppermute | solution.py:297
  2.7 0.0 copy-done
  2.8 1.5 %local.1 = (f32[4,16,512]{2,1,0:T(8,128)S(1)}, f32[4,16,512]{2,1,0:T(8,128)S(1)}, f32[10,16,512]{2,1,0:T(8,128)S(1)}, f32[3,16,512]{2,1,0:T(8,128)S(1)}, bf16[64...) custom-call(s32[128]{0:T(128)S(1)} %copy-done.6, bf16[16,512,128]{2,1,0:T(8,128)(2,1)S(1)} %bitcast.15, ...), custom_call_target="tpu_custom_call" | custom-call | flops 20000000 | bytes 4000000 | tf_op jit(solution)/shard_map/local/pallas_call | solution.py:299
  4.3 0.0 copy-done.10
  4.3 0.0 copy-done.12
  4.3 0.6 %conditional.4 = (bf16[4,16,512]{2,1,0:T(8,128)(2,1)}) conditional(s32[]{:T(128)} %convert_element_type.10, bf16[4,16,512]{2,1,0:T(8,128)(2,1)S(1)} %copy-done.10, (f32[4,16,512]{2,1,0:T(8,128)S(1)}, f32[10,16,512]{2,1,0:T(8,128)S(1)}, f32[3,16,512]{2,1,0:T(8,128)S(1)}, bf16[4,512]{1,0:T(4,128)(2,1)S(1)}, bf16[4,16,512]{2,1,0:T(8,128)(2,1)S(1)}, ...), branch_computations={%region_0.0_spmd, %region_1.0_spmd} | conditional | flops 5 | bytes 573606 | solution.py:382
  4.3 0.6 %copy.20 = bf16[4,16,512]{2,1,0:T(8,128)(2,1)} copy(bf16[4,16,512]{2,1,0:T(8,128)(2,1)S(1)} %param) | data formatting | bytes 131072 | tf_op jit(solution)/shard_map/cond
  4.9 2.7 %collective-permute-done.2 = bf16[528,128]{1,0:T(8,128)(2,1)S(1)} collective-permute-done((bf16[528,128]{1,0:T(8,128)(2,1)S(1)}, bf16[528,128]{1,0:T(8,128)(2,1)S(1)}, u32[]{:S(2)}, u32[]{:S(2)}) %collective-permute-start.2) | collective-permute-done | bytes 135200 | tf_op jit(solution)/shard_map/ppermute | solution.py:297
  7.6 26.0 %conditional.5 = ((bf16[1,4,16,512]{3,2,1,0:T(8,128)(2,1)})) conditional(s32[]{:T(128)} %convert_element_type.10, (bf16[528,128]{1,0:T(8,128)(2,1)S(1)}, f32[4,16,512]{2,1,0:T(8,128)S(1)}, f32[4,16,512]{2,1,0:T(8,128)S(1)}, f32[10,16,512]{2,1,0:T(8,128)S(1)}, f32[3,16,512]{2,1,0:T(8,128)S(1)}, /*index=5*/bf16[64,128]{1,0:T(8,128)(2,1)S(1)}, ...), branch_computations={%region_4.0_spmd, %region_7.0_spmd} | conditional | flops 5 | bytes 573614 | solution.py:386
  7.6 0.3 first.1
  7.9 1.6 %collective-permute-start.1 = (f32[4,16,512]{2,1,0:T(8,128)S(1)}, f32[4,16,512]{2,1,0:T(8,128)S(1)}, u32[]{:S(2)}, u32[]{:S(2)}) collective-permute-start(f32[4,16,512]{2,1,0:T(8,128)S(1)} %get-tuple-element.139), channel_id=1, source_target_pairs={{0,16},{16,0},{1,17},{17,1},{2,18},{18,2},{3,19},{19,3},{4,20},{20... | collective-permute-start | bytes 393224 | tf_op jit(solution)/shard_map/cond/branch_0_fun/ppermute | solution.py:346
  9.6 13.8 %all_to_all.19 = f32[32,1,128]{2,1,0:T(1,128)S(1)} all-to-all(f32[32,1,128]{2,1,0:T(1,128)S(1)} %get-tuple-element.135), channel_id=1, replica_groups=mesh['roll'=8,'pipe'=2,'tp'=16] {'pipe','tp'}, dimensions={0} | all-to-all | bytes 32768 | tf_op jit(solution)/shard_map/cond/branch_0_fun/all_to_all | solution.py:349
  23.4 0.0 collective-permute-done.1
  23.4 10.2 %conditional.1 = (bf16[1,4,16,512]{3,2,1,0:T(8,128)(2,1)}) conditional(s32[]{:T(128)} %convert_element_type.8, (f32[32,1,128]{2,1,0:T(1,128)S(1)}, f32[4,16,512]{2,1,0:T(8,128)S(1)}, f32[4,16,512]{2,1,0:T(8,128)S(1)}, f32[10,16,512]{2,1,0:T(8,128)S(1)}, f32[3,16,512]{2,1,0:T(8,128)S(1)}, /*index=5*/bf16[4,512]{1,0:T(4,128)(2,1)S(1)}, ...), branch_computations={%region_5.0_spmd, %region_6.0_spmd} | conditional | bytes 16392 | solution.py:351
  23.4 0.3 second.3
  23.7 9.2 %all_to_all.18.sums = f32[16,1,128]{2,1,0:T(1,128)S(1)} all-to-all(f32[16,1,128]{2,1,0:T(1,128)S(1)} %get-tuple-element.119), channel_id=1, replica_groups=mesh['roll'=8,'pipe'=2,'tp'=16] {'tp'}, dimensions={0} | all-to-all | bytes 16384 | tf_op jit(solution)/shard_map/cond/branch_0_fun/cond/branch_0_fun/all_to_all | solution.py:335
  32.9 0.7 %last.3 = bf16[4,16,512]{2,1,0:T(8,128)(2,1)} custom-call(f32[16,1,128]{2,1,0:T(1,128)S(1)} %all_to_all.18.sums, f32[4,16,512]{2,1,0:T(8,128)S(1)} %get-tuple-element.120.gated, f32[1,512]{1,0:T(1,128)S(1)} %get-tuple-element.121.gain), custom_call_target="tpu_custom_call" | custom-call | tf_op jit(solution)/shard_map/cond/branch_0_fun/cond/branch_0_fun/last/pallas_call | solution.py:336
  (17 shorter events, 0.0 us)
Async XLA Ops:
  0.0 2.7 %copy-start.6 = (s32[128]{0:T(128)S(1)}, s32[128]{0:T(128)}, u32[]{:S(2)}) copy-start(s32[128]{0:T(128)} %parent.1) | copy-start | bytes 1540
  0.0 2.7 %copy-start.1 = (bf16[1,16,3,512]{3,1,2,0:T(8,128)(2,1)S(1)}, bf16[1,16,3,512]{3,1,2,0:T(8,128)(2,1)}, u32[]{:S(2)}) copy-start(bf16[1,16,3,512]{3,1,2,0:T(8,128)(2,1)} %param.22) | copy-start | bytes 147460
  0.0 2.7 %copy-start = (bf16[1,16,8,64,128]{4,3,2,1,0:T(8,128)(2,1)S(1)}, bf16[1,16,8,64,128]{4,3,2,1,0:T(8,128)(2,1)}, u32[]{:S(2)}) copy-start(bf16[1,16,8,64,128]{4,3,2,1,0:T(8,128)(2,1)} %param.21) | copy-start | bytes 6291460
  0.0 2.7 %copy-start.9 = (f32[1,8]{1,0:T(1,128)S(1)}, f32[1,8]{1,0:T(1,128)}, u32[]{:S(2)}) copy-start(f32[1,8]{1,0:T(1,128)} %skip_d.1) | copy-start | bytes 100
  0.0 2.7 %copy-start.8 = (f32[1,8]{1,0:T(1,128)S(1)}, f32[1,8]{1,0:T(1,128)}, u32[]{:S(2)}) copy-start(f32[1,8]{1,0:T(1,128)} %dt_bias.1) | copy-start | bytes 100
  0.0 2.7 %copy-start.7 = (f32[1,8]{1,0:T(1,128)S(1)}, f32[1,8]{1,0:T(1,128)}, u32[]{:S(2)}) copy-start(f32[1,8]{1,0:T(1,128)} %a_log.1) | copy-start | bytes 100
  0.0 2.7 %copy-start.11 = (bf16[1,4,512]{2,1,0:T(4,128)(2,1)S(1)}, bf16[1,4,512]{2,1,0:T(4,128)(2,1)}, u32[]{:S(2)}) copy-start(bf16[1,4,512]{2,1,0:T(4,128)(2,1)} %param.28) | copy-start | bytes 12292
  0.0 2.7 %copy-start.3 = (bf16[1,4,16,128]{3,2,1,0:T(8,128)(2,1)S(1)}, bf16[1,4,16,128]{3,2,1,0:T(8,128)(2,1)}, u32[]{:S(2)}) copy-start(bf16[1,4,16,128]{3,2,1,0:T(8,128)(2,1)} %param.27) | copy-start | bytes 49156
  0.1 2.7 %copy-start.4 = (bf16[1,4,16,128]{3,2,1,0:T(8,128)(2,1)S(1)}, bf16[1,4,16,128]{3,2,1,0:T(8,128)(2,1)}, u32[]{:S(2)}) copy-start(bf16[1,4,16,128]{3,2,1,0:T(8,128)(2,1)} %param.26) | copy-start | bytes 49156
  0.1 2.7 %copy-start.5 = (f32[1,4,16,8]{2,3,1,0:T(8,128)S(1)}, f32[1,4,16,8]{2,3,1,0:T(8,128)}, u32[]{:S(2)}) copy-start(f32[1,4,16,8]{2,3,1,0:T(8,128)} %param.25) | copy-start | bytes 6148
  0.1 2.7 %copy-start.2 = (bf16[1,4,16,512]{3,2,1,0:T(8,128)(2,1)S(1)}, bf16[1,4,16,512]{3,2,1,0:T(8,128)(2,1)}, u32[]{:S(2)}) copy-start(bf16[1,4,16,512]{3,2,1,0:T(8,128)(2,1)} %param.24) | copy-start | bytes 196612
  0.1 4.2 %copy-start.10 = (bf16[4,16,512]{2,1,0:T(8,128)(2,1)S(1)}, bf16[4,16,512]{2,1,0:T(8,128)(2,1)}, u32[]{:S(2)}) copy-start(bf16[4,16,512]{2,1,0:T(8,128)(2,1)} %param.23) | copy-start | bytes 196612
  0.1 4.2 %copy-start.12 = (f32[1,512]{1,0:T(1,128)S(1)}, f32[1,512]{1,0:T(1,128)}, u32[]{:S(2)}) copy-start(f32[1,512]{1,0:T(1,128)} %param.32) | copy-start | bytes 6148
  1.9 5.7 %collective-permute-start.2 = (bf16[528,128]{1,0:T(8,128)(2,1)S(1)}, bf16[528,128]{1,0:T(8,128)(2,1)S(1)}, u32[]{:S(2)}, u32[]{:S(2)}) collective-permute-start(bf16[528,128]{1,0:T(8,128)(2,1)S(1)} %crossing.1), channel_id=1, source_target_pairs={{0,32},{32,64},{64,96},{96,128},{128,160},{160,192},{192,224},{224... | collective-permute-start | bytes 405512 | tf_op jit(solution)/shard_map/ppermute | solution.py:297
  7.9 15.5 %collective-permute-start.1 = (f32[4,16,512]{2,1,0:T(8,128)S(1)}, f32[4,16,512]{2,1,0:T(8,128)S(1)}, u32[]{:S(2)}, u32[]{:S(2)}) collective-permute-start(f32[4,16,512]{2,1,0:T(8,128)S(1)} %get-tuple-element.139), channel_id=1, source_target_pairs={{0,16},{16,0},{1,17},{17,1},{2,18},{18,2},{3,19},{19,3},{4,20},{20... | collective-permute-start | bytes 393224 | tf_op jit(solution)/shard_map/cond/branch_0_fun/ppermute | solution.py:346

commit v6 on v4

--- a/solution.py
+++ b/solution.py
@@ -19,57 +19,72 @@
     return value / (1.0 + jnp.exp(-value))
 
 
+def tap_rows(conv):
+    rows = conv[...].astype(F32)
+    return [rows[k:k + 1] for k in range(rows.shape[0])]
+
+
 def pairs(steps):
     return [(t, r) for t in range(steps) for r in range(t + 1)]
+
+
+def crossing_row(parent, block, slots):
+    begin = block * slots
+    row = jnp.int32(0)
+    for s in range(slots):
+        found = parent[begin + s] - begin + slots
+        row = jnp.where(found < slots, found, row)
+    return jnp.clip(row, 0, slots - 1)
+
+
+def packed_window(window, row):
+    taps, slots, width = window.shape
+    groups = width // 128
+    pick = lax.broadcasted_iota(jnp.int32, (slots, 1), 0) == row
+    place = lax.broadcasted_iota(jnp.int32, (16, 128), 0)
+    packed = jnp.zeros(place.shape, F32)
+    for k in range(taps):
+        chosen = jnp.sum(jnp.where(pick, window[k].astype(F32), 0.0), axis=0, keepdims=True)
+        for j in range(groups):
+            packed = jnp.where(place == k * groups + j, chosen[:, j * 128:(j + 1) * 128], packed)
+    return packed.astype(BF16)
 
 
 def crossing_kernel(parent_hbm, state, window_hbm, out, parent, window, sems):
     slots = window.shape[1]
     nrows = state.shape[1]
-    taps, _, width = window.shape
-    groups = width // 128
     following = lax.axis_index("roll") + 1
-
-    @pl.when(following == lax.axis_size("roll"))
+    sends = (following < lax.axis_size("roll")) & (lax.axis_index("pipe") == 0)
+
+    @pl.when(jnp.logical_not(sends))
     def _():
         out[...] = jnp.zeros(out.shape, BF16)
 
-    @pl.when(following < lax.axis_size("roll"))
+    @pl.when(sends)
     def _():
         get_parent = pltpu.make_async_copy(parent_hbm, parent, sems.at[0])
         get_parent.start()
         get_window = pltpu.make_async_copy(window_hbm, window, sems.at[1])
         get_window.start()
-        begin = following * slots
         get_parent.wait()
-        row = jnp.int32(0)
-        for s in range(slots):
-            found = parent[begin + s] - begin + slots
-            row = jnp.where(found < slots, found, row)
-        row = jnp.clip(row, 0, slots - 1)
+        row = crossing_row(parent, following, slots)
         copy = pltpu.make_async_copy(state.at[row], out.at[pl.ds(0, nrows)], sems.at[2])
         copy.start()
-        pick = lax.broadcasted_iota(jnp.int32, (slots, 1), 0) == row
-        place = lax.broadcasted_iota(jnp.int32, (out.shape[0] - nrows, 128), 0)
-        packed = jnp.zeros(place.shape, F32)
         get_window.wait()
-        for k in range(taps):
-            chosen = jnp.sum(jnp.where(pick, window[k].astype(F32), 0.0), axis=0, keepdims=True)
-            for j in range(groups):
-                packed = jnp.where(place == k * groups + j, chosen[:, j * 128:(j + 1) * 128], packed)
-        out[pl.ds(nrows, place.shape[0])] = packed.astype(BF16)
+        out[pl.ds(nrows, 16)] = packed_window(window, row)
         copy.wait()
 
 
 def local_kernel(
-    parent, state, window, c_in, b_in, dt_raw, z_gate, conv, a_log, dt_bias, skip_d,
-    base_out, reach_out, mix_out, conv_out, cmask_out, wmask_out,
+    after, parent, state, window, c_in, b_in, dt_raw, z_gate, conv, a_log, dt_bias, skip_d,
+    base_out, reach_out, mix_out, conv_out, cmask_out, wmask_out, leaving_out,
 ):
     steps, slots, width = z_gate.shape
     heads = dt_raw.shape[1]
     taps = window.shape[0]
     nstate = c_in.shape[2]
-    first = lax.axis_index("roll") * slots
+    roll = lax.axis_index("roll")
+    first = roll * slots
     local = [parent[first + s] - first for s in range(slots)]
     held = [jnp.clip(row, 0, slots - 1) for row in local]
 
@@ -86,7 +101,7 @@
     choose = choose.astype(BF16)
 
     taken = [jnp.dot(choose, window[k], preferred_element_type=F32) for k in range(taps)]
-    weight = [conv[pl.ds(k, 1), :].astype(F32) for k in range(taps + 1)]
+    weight = tap_rows(conv)
     for t in range(taps):
         part = weight[0] * taken[t]
         for k in range(1, taps - t):
@@ -146,6 +161,11 @@
     for t in range(steps):
         base_out[t] = total[t * slots:(t + 1) * slots] * reach[t]
 
+    row = crossing_row(parent, lax.rem(roll + 1, lax.axis_size("roll")), slots)
+    nrows = state.shape[1]
+    leaving_out[pl.ds(0, nrows)] = state[row]
+    leaving_out[pl.ds(nrows, 16)] = packed_window(window, row)
+
 
 def gated_rows(pre, base, mix, steps):
     inner = [silu(value) for value in pre]
@@ -180,39 +200,6 @@
     )
 
 
-def first_kernel(arrived, base, reach, mix, conv_part, cmask, wmask, conv, x_in, gain,
-                 base_out, conv_out, send_out, sums_out):
-    steps, slots, width = x_in.shape
-    taps = conv_part.shape[0]
-    nrows = arrived.shape[0] - 16
-    groups = width // 128
-    extra = lax.dot_general(cmask[...], arrived[pl.ds(0, nrows)], NT, preferred_element_type=F32)
-    start = []
-    for t in range(steps):
-        start.append(base[t] + extra[t * slots:(t + 1) * slots] * reach[t])
-        base_out[t] = start[t]
-    packed = arrived[pl.ds(nrows, 16)].astype(F32)
-    rows = [
-        jnp.concatenate([packed[k * groups + j:k * groups + j + 1] for j in range(groups)], axis=1)
-        for k in range(taps)
-    ]
-    weight = [conv[pl.ds(k, 1), :].astype(F32) for k in range(taps + 1)]
-    mask = wmask[:, :1]
-    pre = []
-    for t in range(taps):
-        part = weight[0] * rows[t]
-        for k in range(1, taps - t):
-            part = part + weight[k] * rows[t + k]
-        pre.append(conv_part[t] + mask * part)
-        conv_out[t] = pre[t]
-    x_rows = [x_in[t].astype(F32) for t in range(steps)]
-    pre = with_inputs(pre, weight, x_rows)
-    gated = gated_rows(pre, start, [mix[i] for i in range(mix.shape[0])], steps)
-    for t in range(steps):
-        send_out[t] = gated[t] * gain[...]
-    sums_out[...] = jnp.broadcast_to(square_sums(gated)[None], sums_out.shape)
-
-
 def with_inputs(window_part, weight, x_rows):
     taps = len(window_part)
     pre = []
@@ -225,24 +212,112 @@
     return pre
 
 
+def arrived_rows(arrived, taps, groups):
+    nrows = arrived.shape[0] - 16
+    packed = arrived[pl.ds(nrows, 16)].astype(F32)
+    rows = [
+        jnp.concatenate([packed[k * groups + j:k * groups + j + 1] for j in range(groups)], axis=1)
+        for k in range(taps)
+    ]
+    return arrived[pl.ds(0, nrows)], rows
+
+
+def window_terms(weight, rows):
+    taps = len(rows)
+    parts = []
+    for t in range(taps):
+        part = weight[0] * rows[t]
+        for k in range(1, taps - t):
+            part = part + weight[k] * rows[t + k]
+        parts.append(part)
+    return parts
+
+
+def front_kernel(base, reach, mix, conv_part, cmask, wmask, conv, x_in, gain, pack_out, extra_out, row_out):
+    steps, slots, width = x_in.shape
+    taps = conv_part.shape[0]
+    outside = wmask[:, :1]
+    weight = tap_rows(conv)
+    pre = with_inputs([conv_part[t] for t in range(taps)], weight, [x_in[t].astype(F32) for t in range(steps)])
+    count = mix.shape[0]
+    mixes = [mix[i] for i in range(count)]
+    gated = gated_rows(pre, [base[t] for t in range(steps)], mixes, steps)
+    gated = [row * (1.0 - outside) for row in gated]
+    for t in range(steps):
+        pack_out[pl.ds(t * slots, slots)] = gated[t] * gain[...]
+
+    def crossing(value):
+        return jnp.sum(value * outside, axis=0, keepdims=True)
+
+    slot_c = [jnp.sum(cmask[pl.ds(t * slots, slots)].astype(F32), axis=0, keepdims=True) for t in range(steps)]
+    rows = [crossing(reach[t]) for t in range(steps)]
+    rows += [crossing(value) for value in mixes]
+    rows += [crossing(value) for value in pre]
+    rows += weight + [gain[...], jnp.concatenate(slot_c, axis=1)]
+    extra_out[...] = jnp.concatenate(rows + [jnp.zeros_like(gain)] * (extra_out.shape[0] - len(rows)), axis=0)
+    lane = lax.broadcasted_iota(jnp.int32, (slots, 128), 1)
+    slot = lax.broadcasted_iota(jnp.int32, (slots, 128), 0)
+    lanes = jnp.sum(jnp.where(lax.rem(lane, slots) == slot, wmask[...], 0.0), axis=0, keepdims=True)
+    row_out[...] = jnp.concatenate([square_sums(gated), lanes, jnp.zeros((6, 128), F32)], axis=0)
+
+
+def fill_kernel(arrived, pack, extra, row, wmask, taps, other_out, sums_out):
+    steps, slots, width = other_out.shape
+    number = len(pairs(steps))
+    nstate = arrived.shape[1]
+    extra = extra[...]
+
+    def take(begin, size):
+        return [extra[begin + i:begin + i + 1] for i in range(size)]
+
+    reach = take(0, steps)
+    mixes = take(steps, number)
+    pre = take(steps + number, steps)
+    weight = take(2 * steps + number, taps + 1)
+    gain, slot_c = take(2 * steps + number + taps + 1, 2)
+    state, rows = arrived_rows(arrived, taps, width // 128)
+    lhs = [slot_c[:, t * nstate:(t + 1) * nstate] for t in range(steps)]
+    lhs = jnp.concatenate(lhs + [jnp.zeros((16 - steps, nstate), F32)], axis=0).astype(BF16)
+    start = lax.dot_general(lhs, state, NT, preferred_element_type=F32)
+    for t, term in enumerate(window_terms(weight, rows)):
+        pre[t] = pre[t] + term
+    gated = gated_rows(pre, [start[t:t + 1] * reach[t] for t in range(steps)], mixes, steps)
+    mask = wmask[:, :1]
+    lane = lax.broadcasted_iota(jnp.int32, (1, 128), 1)
+    sums = jnp.zeros((1, 128), F32)
+    for t in range(steps):
+        other_out[t] = pack[pl.ds(t * slots, slots)] + mask * (gated[t] * gain)
+        square = jnp.sum(gated[t] * gated[t], axis=1, keepdims=True)
+        here = (lane >= t * slots) & (lane < (t + 1) * slots)
+        sums = jnp.where(here, square, sums)
+    sums = jnp.where(lax.axis_index("pipe") == 0, row[pl.ds(0, 1)], sums * row[pl.ds(1, 1)])
+    sums_out[...] = jnp.broadcast_to(sums[None], sums_out.shape)
+
+
 def finish_kernel(sums, own, channels, out):
-    steps, slots, _ = own.shape
+    steps, slots, _ = out.shape
     scale = row_scales(sums[...], channels, steps * slots)
     for t in range(steps):
         out[t] = scaled(own[t], scale[t * slots:(t + 1) * slots]).astype(BF16)
 
 
-def second_kernel(sums, other, base, mix, conv_part, conv, channels, gated_out, sums_out):
+def second_kernel(
+    sums, other, arrived, base, reach, mix, conv_part, cmask, wmask, conv, channels, gated_out, sums_out
+):
     steps, slots, width = other.shape
     taps = conv_part.shape[0]
+    weight = tap_rows(conv)
+    state, rows = arrived_rows(arrived, taps, width // 128)
+    extra = lax.dot_general(cmask[...], state, NT, preferred_element_type=F32)
+    start = [base[t] + extra[t * slots:(t + 1) * slots] * reach[t] for t in range(steps)]
+    mask = wmask[:, :1]
+    pre = [conv_part[t] + mask * term for t, term in enumerate(window_terms(weight, rows))]
     scale = row_scales(sums[...], channels, steps * slots)
-    rows = []
-    for t in range(steps):
-        row = scaled(other[t], scale[t * slots:(t + 1) * slots])
-        rows.append(row.astype(BF16).astype(F32))
-    weight = [conv[pl.ds(k, 1), :].astype(F32) for k in range(taps + 1)]
-    pre = with_inputs([conv_part[t] for t in range(taps)], weight, rows)
-    gated = gated_rows(pre, [base[t] for t in range(steps)], [mix[i] for i in range(mix.shape[0])], steps)
+    inputs = [
+        scaled(other[t], scale[t * slots:(t + 1) * slots]).astype(BF16).astype(F32) for t in range(steps)
+    ]
+    pre = with_inputs(pre, weight, inputs)
+    gated = gated_rows(pre, start, [mix[i] for i in range(mix.shape[0])], steps)
     for t in range(steps):
         gated_out[t] = gated[t]
     sums_out[...] = jnp.broadcast_to(square_sums(gated)[None], sums_out.shape)
@@ -268,11 +343,29 @@
     state = ssm_state.reshape(slots, rows, nstate)
     window = jnp.transpose(conv_window[0], (1, 0, 2))
     raw = jnp.transpose(dt_raw[0], (0, 2, 1))
+    conv = conv_weight[0]
     shape = jax.ShapeDtypeStruct
+    step_rows = shape((steps, slots, width), F32)
+    packed_slot = shape((rows + 16, nstate), BF16)
+    nextra = (2 * steps + npairs + taps + 3 + 7) // 8 * 8
+
+    def at(i, p, t):
+        return (i * pipes + p) * tp + t
+
+    end = count - 1
+    first_moves, second_moves = [], []
+    for t in range(tp):
+        first_moves += [(at(i, 0, t), at(i + 1, 1, t)) for i in range(end)]
+        first_moves += [(at(i + 1, 1, t), at(i, 0, t)) for i in range(end)]
+        first_moves += [(at(end, 0, t), at(end, 0, t ^ 1)), (at(0, 1, t), at(0, 1, t ^ 1))]
+        second_moves += [(at(i, 1, t), at(i + 1, 1, t)) for i in range(end)]
+        second_moves += [(at(i + 1, 0, t), at(i, 0, t)) for i in range(end)]
+        second_moves += [(at(end, 1, t), at(end, 0, t)), (at(0, 0, t), at(0, 1, t))]
+    swap = [(i, (i + 1) % pipes) for i in range(pipes)]
 
     leaving = pl.pallas_call(
         crossing_kernel,
-        out_shape=shape((rows + 16, nstate), BF16),
+        out_shape=packed_slot,
         in_specs=[HBM, HBM, HBM],
         out_specs=VMEM,
         scratch_shapes=[
@@ -283,63 +376,71 @@
         compiler_params=PARAMS,
         name="crossing",
     )(*[pltpu.with_memory_space_constraint(value, pltpu.HBM) for value in (parent, state, window)])
-    arrived = lax.ppermute(leaving, "roll", [(i, (i + 1) % count) for i in range(count)])
-
-    base, reach, mix, conv_part, cmask, wmask = pl.pallas_call(
+    arrived = lax.ppermute(leaving, ("roll", "pipe", "tp"), first_moves)
+
+    base, reach, mix, conv_part, cmask, wmask, leaving = pl.pallas_call(
         local_kernel,
         out_shape=(
-            shape((steps, slots, width), F32),
-            shape((steps, slots, width), F32),
+            step_rows,
+            step_rows,
             shape((npairs, slots, width), F32),
             shape((taps, slots, width), F32),
             shape((steps * slots, nstate), BF16),
             shape((slots, 128), F32),
+            packed_slot,
         ),
-        in_specs=[SMEM] + [VMEM] * 10,
-        out_specs=(VMEM,) * 6,
+        in_specs=[HBM, SMEM] + [VMEM] * 10,
+        out_specs=(VMEM,) * 7,
         compiler_params=PARAMS,
         cost_estimate=pl.CostEstimate(flops=20_000_000, bytes_accessed=4_000_000, transcendentals=0),
         name="local",
-    )(parent, state, window, c_in[0], b_in[0], raw, z_gate[0], conv_weight[0], a_log, dt_bias, skip_d)
-
-    base, conv_part, own, sums = pl.pallas_call(
-        first_kernel,
-        out_shape=(
-            shape((steps, slots, width), F32),
-            shape((taps, slots, width), F32),
-            shape((steps, slots, width), F32),
-            shape((pipes * tp, 1, 128), F32),
-        ),
-        in_specs=[VMEM] * 10,
-        out_specs=(VMEM,) * 4,
+    )(leaving, parent, state, window, c_in[0], b_in[0], raw, z_gate[0], conv, a_log, dt_bias, skip_d)
+
+    pack, extra, row = pl.pallas_call(
+        front_kernel,
+        out_shape=(shape((steps * slots, width), F32), shape((nextra, width), F32), shape((8, 128), F32)),
+        in_specs=[VMEM] * 9,
+        out_specs=(VMEM,) * 3,
         compiler_params=PARAMS,
-        name="first",
-    )(arrived, base, reach, mix, conv_part, cmask, wmask, conv_weight[0], x_in, norm_gain)
-    other = lax.ppermute(own, "pipe", [(i, (i + 1) % pipes) for i in range(pipes)])
+        name="front",
+    )(base, reach, mix, conv_part, cmask, wmask, conv, x_in, norm_gain)
+    other_extra = lax.ppermute(extra, "pipe", swap)
+    other_pack = lax.ppermute(pack, "pipe", swap)
+    later = lax.ppermute(leaving, ("roll", "pipe", "tp"), second_moves)
+
+    whole, sums = pl.pallas_call(
+        lambda *refs: fill_kernel(*refs[:5], taps, *refs[5:]),
+        out_shape=(step_rows, shape((pipes * tp, 1, 128), F32)),
+        in_specs=[VMEM] * 5,
+        out_specs=(VMEM,) * 2,
+        compiler_params=PARAMS,
+        name="fill",
+    )(arrived, other_pack, other_extra, row, wmask)
+    other_whole = lax.ppermute(whole, "pipe", swap)
     section = lax.axis_index("pipe")
     sums, section = lax.optimization_barrier((sums, section))
     sums = lax.all_to_all(sums, ("pipe", "tp"), 0, 0)
     sums, section = lax.optimization_barrier((sums, section))
 
-    def first_section(sums, own, other, base, mix, conv_part, conv, gain):
+    def first_section(sums, other_whole, whole, later, base, reach, mix, conv_part, cmask, wmask, conv, gain):
         return pl.pallas_call(
-            lambda sums, own, out: finish_kernel(sums.at[pl.ds(0, tp)], own, channels, out),
+            lambda sums, own, out: finish_kernel(sums, own, channels, out),
             out_shape=shape((steps, slots, width), BF16),
             in_specs=[VMEM] * 2,
             out_specs=VMEM,
             compiler_params=PARAMS,
             name="finish",
-        )(sums, own)
-
-    def second_section(sums, own, other, base, mix, conv_part, conv, gain):
+        )(sums, other_whole)
+
+    def second_section(sums, other_whole, whole, later, base, reach, mix, conv_part, cmask, wmask, conv, gain):
         gated, sums = pl.pallas_call(
-            lambda sums, *refs: second_kernel(sums.at[pl.ds(0, tp)], *refs[:5], channels, *refs[5:]),
-            out_shape=(shape((steps, slots, width), F32), shape((tp, 1, 128), F32)),
-            in_specs=[VMEM] * 6,
+            lambda *refs: second_kernel(*refs[:10], channels, *refs[10:]),
+            out_shape=(step_rows, shape((tp, 1, 128), F32)),
+            in_specs=[VMEM] * 10,
             out_specs=(VMEM,) * 2,
             compiler_params=PARAMS,
             name="second",
-        )(sums, other, base, mix, conv_part, conv)
+        )(sums, whole, later, base, reach, mix, conv_part, cmask, wmask, conv)
         sums = lax.all_to_all(sums, "tp", 0, 0)
         return pl.pallas_call(
             lambda sums, gated, gain, out: last_kernel(sums, gated, gain, channels, out),
@@ -352,7 +453,7 @@
 
     result = lax.cond(
         section == 0, first_section, second_section,
-        sums, own, other, base, mix, conv_part, conv_weight[0], norm_gain,
+        sums, other_whole, whole, later, base, reach, mix, conv_part, cmask, wmask, conv, norm_gain,
     )
     return result[None]
 

time: 35.8 us -> 32.9 us (0.919)
  waiting for transfers between devices: 3.05 us -> 0.01 us
  starting transfers between devices: 4.99 us -> 7.68 us
  blocking collectives: 22.8 us -> 21.3 us
  Pallas kernels: 3.96 us -> 2.53 us
    ppermute x2 -> x5, waiting for transfers between devices: 3.05 us -> 0.01 us  [the longest x1 0.01 us: body(): later = lax.ppermute(leaving, ('roll', 'pipe', 'tp'), second_moves)]
    ppermute x2 -> x5, starting transfers between devices: 4.99 us -> 7.68 us  [the longest x1 3.02 us: body(): other_pack = lax.ppermute(pack, 'pipe', swap)]
    all_to_all x1, blocking collectives: 13.6 us -> 12.1 us  [body(): sums = lax.all_to_all(sums, ('pipe', 'tp'), 0, 0)]
    pallas_call x4 -> x5, Pallas kernels: 3.85 us -> 2.42 us  [the longest x1 1.5 us: body(): pl.pallas_call(local_kernel, out_shape=(step_rows, step_rows, shape((npai...]
  transfers between devices with their start and end apart: 2 -> 5, of which waited for: 1 -> 0; matrix products, arithmetic and copies ran while one was open for 0% -> 0% of each run, Pallas kernels for 4% -> 6%
where the time goes in v6:
time: 32.9 us; the launch traced here: 32.4 us
  blocking collectives  21.3 us (65%)
  starting transfers between devices  7.68 us (23%)
  Pallas kernels  2.53 us (8%)
  local copies, waits for them, and re-layouts  0.68 us (2%)
    all_to_all x1, blocking collectives, body(): sums = lax.all_to_all(sums, ('pipe', 'tp'), 0, 0)  12.1 us
    all_to_all x1, blocking collectives, second_section(): sums = lax.all_to_all(sums, 'tp', 0, 0)  9.15 us
    ppermute x1, starting transfers between devices, body(): other_pack = lax.ppermute(pack, 'pipe', swap)  3.02 us
    ppermute x1, starting transfers between devices, body(): arrived = lax.ppermute(leaving, ('roll', 'pipe', 'tp'), first_moves)  2.13 us
    ppermute x1, starting transfers between devices, body(): later = lax.ppermute(leaving, ('roll', 'pipe', 'tp'), second_moves)  1.72 us
    pallas_call x1, Pallas kernels, body(): pl.pallas_call(local_kernel, out_shape=(step_rows, step_rows, shape((npai...  1.5 us
    ppermute x1, starting transfers between devices, body(): other_whole = lax.ppermute(whole, 'pipe', swap)  0.71 us
    unnamed x28, local copies, waits for them, and re-layouts  0.68 us
  transfers between devices with their start and end apart: 5, of which 0 were waited for; matrix products, arithmetic and copies ran while one was open for 0% of the time, Pallas kernels for 6%

profile of v6, /device:TPU:1, one launch (start us, length us, event | category | flops | bytes accessed | tf_op | source)
XLA Modules:
  0.0 32.4 jit_solution(1379798304295162390)
XLA Ops:
  0.1 0.1 crossing.1.after
  0.2 2.1 %collective-permute-start = (bf16[528,128]{1,0:T(8,128)(2,1)S(1)}, bf16[528,128]{1,0:T(8,128)(2,1)S(1)}, u32[]{:S(2)}, u32[]{:S(2)}) collective-permute-start(bf16[528,128]{1,0:T(8,128)(2,1)S(1)} %crossing.1.after), channel_id=1, source_target_pairs={{0,48},{32,80},{64,112},{96,144},{128,176},{160,208},{192,240},{48... | collective-permute-start | bytes 405512 | tf_op jit(solution)/shard_map/ppermute | solution.py:379
  2.3 0.0 copy-done.1
  2.4 1.5 %local.1 = (f32[4,16,512]{2,1,0:T(8,128)S(1)}, f32[4,16,512]{2,1,0:T(8,128)S(1)}, f32[10,16,512]{2,1,0:T(8,128)S(1)}, f32[3,16,512]{2,1,0:T(8,128)S(1)}, bf16[64...) custom-call(bf16[528,128]{1,0:T(8,128)(2,1)S(1)} %crossing.1.after, s32[128]{0:T(128)S(1)} %copy-done.7, ...), custom_call_target="tpu_custom_call" | custom-call | flops 20000000 | bytes 4000000 | tf_op jit(solution)/shard_map/local/pallas_call | solution.py:381
  3.9 0.0 copy-done.3
  3.9 0.0 copy-done.13
  3.9 0.2 front.1
  4.2 3.0 %collective-permute-start.1 = (f32[64,512]{1,0:T(8,128)S(1)}, f32[64,512]{1,0:T(8,128)S(1)}, u32[]{:S(2)}, u32[]{:S(2)}) collective-permute-start(f32[64,512]{1,0:T(8,128)S(1)} %get-tuple-element.72), channel_id=1, source_target_pairs={{0,16},{16,0},{1,17},{17,1},{2,18},{18,2},{3,19},{19,3},{4,20},{20... | collective-permute-start | bytes 393224 | tf_op jit(solution)/shard_map/ppermute | solution.py:408
  7.2 0.1 collective-permute-start.2
  7.3 1.7 %collective-permute-start.3 = (bf16[528,128]{1,0:T(8,128)(2,1)S(1)}, bf16[528,128]{1,0:T(8,128)(2,1)S(1)}, u32[]{:S(2)}, u32[]{:S(2)}) collective-permute-start(bf16[528,128]{1,0:T(8,128)(2,1)S(1)} %get-tuple-element.81), channel_id=1, source_target_pairs={{16,48},{48,80},{80,112},{112,144},{144,176},{176,208},{208,240},{... | collective-permute-start | bytes 405512 | tf_op jit(solution)/shard_map/ppermute | solution.py:409
  9.0 0.0 collective-permute-done.2.refs_2_
  9.0 0.0 collective-permute-done.1.refs_1_
  9.0 0.0 collective-permute-done.refs_0_
  9.0 0.3 fill.1
  9.3 0.7 %collective-permute-start.4 = (f32[4,16,512]{2,1,0:T(8,128)S(1)}, f32[4,16,512]{2,1,0:T(8,128)S(1)}, u32[]{:S(2)}, u32[]{:S(2)}) collective-permute-start(f32[4,16,512]{2,1,0:T(8,128)S(1)} %get-tuple-element.80), channel_id=1, source_target_pairs={{0,16},{16,0},{1,17},{17,1},{2,18},{18,2},{3,19},{19,3},{4,20},{20... | collective-permute-start | bytes 393224 | tf_op jit(solution)/shard_map/ppermute | solution.py:419
  10.0 12.1 %all_to_all.10 = f32[32,1,128]{2,1,0:T(1,128)S(1)} all-to-all(f32[32,1,128]{2,1,0:T(1,128)S(1)} %get-tuple-element.76), channel_id=1, replica_groups=mesh['roll'=8,'pipe'=2,'tp'=16] {'pipe','tp'}, dimensions={0} | all-to-all | bytes 32768 | tf_op jit(solution)/shard_map/all_to_all | solution.py:422
  22.1 0.0 collective-permute-done.3
  22.1 0.0 collective-permute-done.4
  22.1 9.6 %conditional.1 = (bf16[1,4,16,512]{3,2,1,0:T(8,128)(2,1)S(1)}) conditional(s32[]{:T(128)} %convert_element_type.3, (f32[32,1,128]{2,1,0:T(1,128)S(1)}, f32[4,16,512]{2,1,0:T(8,128)S(1)}, bf16[528,128]{1,0:T(8,128)(2,1)S(1)}, f32[4,16,512]{2,1,0:T(8,128)S(1)}, f32[4,16,512]{2,1,0:T(8,128)S(1)}, /*index=5*/f32[10,16,512]{2,1,0:T(8,128)S(1)}, ...), branch_computations={%region_0.0_spmd, %region_1.0_spmd} | conditional | bytes 16392 | solution.py:454
  22.1 0.4 %second.1 = (f32[4,16,512]{2,1,0:T(8,128)S(1)}, f32[16,1,128]{2,1,0:T(1,128)S(1)}) custom-call(f32[32,1,128]{2,1,0:T(1,128)S(1)} %get-tuple-element.35.refs_0_, f32[4,16,512]{2,1,0:T(8,128)S(1)} %get-tuple-element.36.refs_1_, bf16[528,128]{1,0:T(8,128)(2,1)S(1)} %get-tuple-element.37.refs_2_, f32[4,16,512]{2,1,0:T(8,128)S(1)} %get-tuple-element.38.refs_3_, ...), custom_call_target="tpu_custom_call" | custom-call | tf_op jit(solution)/shard_map/cond/branch_0_fun/second/pallas_call | solution.py:436
  22.5 9.2 %all_to_all.9.sums = f32[16,1,128]{2,1,0:T(1,128)S(1)} all-to-all(f32[16,1,128]{2,1,0:T(1,128)S(1)} %get-tuple-element.45), channel_id=1, replica_groups=mesh['roll'=8,'pipe'=2,'tp'=16] {'tp'}, dimensions={0} | all-to-all | bytes 16384 | tf_op jit(solution)/shard_map/cond/branch_0_fun/all_to_all | solution.py:444
  31.6 0.1 last.1
  31.8 0.0 copy-start.11
  31.8 0.6 %copy-done.11 = bf16[1,4,16,512]{3,2,1,0:T(8,128)(2,1)} copy-done((bf16[1,4,16,512]{3,2,1,0:T(8,128)(2,1)}, bf16[1,4,16,512]{3,2,1,0:T(8,128)(2,1)S(1)}, u32[]{:S(2)}) %copy-start.11) | copy-done | bytes 65560
  (23 shorter events, 0.0 us)
Async XLA Ops:
  0.0 2.3 %copy-start.7 = (s32[128]{0:T(128)S(1)}, s32[128]{0:T(128)}, u32[]{:S(2)}) copy-start(s32[128]{0:T(128)} %parent.1) | copy-start | bytes 1540
  0.0 2.3 %copy-start.1 = (bf16[1,16,3,512]{3,1,2,0:T(8,128)(2,1)S(1)}, bf16[1,16,3,512]{3,1,2,0:T(8,128)(2,1)}, u32[]{:S(2)}) copy-start(bf16[1,16,3,512]{3,1,2,0:T(8,128)(2,1)} %param.16) | copy-start | bytes 147460
  0.0 2.3 %copy-start = (bf16[1,16,8,64,128]{4,3,2,1,0:T(8,128)(2,1)S(1)}, bf16[1,16,8,64,128]{4,3,2,1,0:T(8,128)(2,1)}, u32[]{:S(2)}) copy-start(bf16[1,16,8,64,128]{4,3,2,1,0:T(8,128)(2,1)} %param.15) | copy-start | bytes 6291460
  0.0 2.3 %copy-start.10 = (f32[1,8]{1,0:T(1,128)S(1)}, f32[1,8]{1,0:T(1,128)}, u32[]{:S(2)}) copy-start(f32[1,8]{1,0:T(1,128)} %skip_d.1) | copy-start | bytes 100
  0.0 2.3 %copy-start.9 = (f32[1,8]{1,0:T(1,128)S(1)}, f32[1,8]{1,0:T(1,128)}, u32[]{:S(2)}) copy-start(f32[1,8]{1,0:T(1,128)} %dt_bias.1) | copy-start | bytes 100
  0.0 2.3 %copy-start.8 = (f32[1,8]{1,0:T(1,128)S(1)}, f32[1,8]{1,0:T(1,128)}, u32[]{:S(2)}) copy-start(f32[1,8]{1,0:T(1,128)} %a_log.1) | copy-start | bytes 100
  0.0 2.3 %copy-start.12 = (bf16[1,4,512]{2,1,0:T(4,128)(2,1)S(1)}, bf16[1,4,512]{2,1,0:T(4,128)(2,1)}, u32[]{:S(2)}) copy-start(bf16[1,4,512]{2,1,0:T(4,128)(2,1)} %param.22) | copy-start | bytes 12292
  0.0 2.3 %copy-start.4 = (bf16[1,4,16,128]{3,2,1,0:T(8,128)(2,1)S(1)}, bf16[1,4,16,128]{3,2,1,0:T(8,128)(2,1)}, u32[]{:S(2)}) copy-start(bf16[1,4,16,128]{3,2,1,0:T(8,128)(2,1)} %param.21) | copy-start | bytes 49156
  0.1 2.3 %copy-start.5 = (bf16[1,4,16,128]{3,2,1,0:T(8,128)(2,1)S(1)}, bf16[1,4,16,128]{3,2,1,0:T(8,128)(2,1)}, u32[]{:S(2)}) copy-start(bf16[1,4,16,128]{3,2,1,0:T(8,128)(2,1)} %param.20) | copy-start | bytes 49156
  0.1 2.3 %copy-start.6 = (f32[1,4,16,8]{2,3,1,0:T(8,128)S(1)}, f32[1,4,16,8]{2,3,1,0:T(8,128)}, u32[]{:S(2)}) copy-start(f32[1,4,16,8]{2,3,1,0:T(8,128)} %param.19) | copy-start | bytes 6148
  0.1 2.3 %copy-start.2 = (bf16[1,4,16,512]{3,2,1,0:T(8,128)(2,1)S(1)}, bf16[1,4,16,512]{3,2,1,0:T(8,128)(2,1)}, u32[]{:S(2)}) copy-start(bf16[1,4,16,512]{3,2,1,0:T(8,128)(2,1)} %param.18) | copy-start | bytes 196612
  0.1 3.8 %copy-start.3 = (bf16[4,16,512]{2,1,0:T(8,128)(2,1)S(1)}, bf16[4,16,512]{2,1,0:T(8,128)(2,1)}, u32[]{:S(2)}) copy-start(bf16[4,16,512]{2,1,0:T(8,128)(2,1)} %x_in.1) | copy-start | bytes 196612
  0.1 3.8 %copy-start.13 = (f32[1,512]{1,0:T(1,128)S(1)}, f32[1,512]{1,0:T(1,128)}, u32[]{:S(2)}) copy-start(f32[1,512]{1,0:T(1,128)} %gain.1) | copy-start | bytes 6148
  0.2 8.8 %collective-permute-start = (bf16[528,128]{1,0:T(8,128)(2,1)S(1)}, bf16[528,128]{1,0:T(8,128)(2,1)S(1)}, u32[]{:S(2)}, u32[]{:S(2)}) collective-permute-start(bf16[528,128]{1,0:T(8,128)(2,1)S(1)} %crossing.1.after), channel_id=1, source_target_pairs={{0,48},{32,80},{64,112},{96,144},{128,176},{160,208},{192,240},{48... | collective-permute-start | bytes 405512 | tf_op jit(solution)/shard_map/ppermute | solution.py:379
  4.2 4.9 %collective-permute-start.1 = (f32[64,512]{1,0:T(8,128)S(1)}, f32[64,512]{1,0:T(8,128)S(1)}, u32[]{:S(2)}, u32[]{:S(2)}) collective-permute-start(f32[64,512]{1,0:T(8,128)S(1)} %get-tuple-element.72), channel_id=1, source_target_pairs={{0,16},{16,0},{1,17},{17,1},{2,18},{18,2},{3,19},{19,3},{4,20},{20... | collective-permute-start | bytes 393224 | tf_op jit(solution)/shard_map/ppermute | solution.py:408
  7.2 1.8 %collective-permute-start.2 = (f32[24,512]{1,0:T(8,128)S(1)}, f32[24,512]{1,0:T(8,128)S(1)}, u32[]{:S(2)}, u32[]{:S(2)}) collective-permute-start(f32[24,512]{1,0:T(8,128)S(1)} %get-tuple-element.73), channel_id=1, source_target_pairs={{0,16},{16,0},{1,17},{17,1},{2,18},{18,2},{3,19},{19,3},{4,20},{20... | collective-permute-start | bytes 147464 | tf_op jit(solution)/shard_map/ppermute | solution.py:407
  7.3 14.8 %collective-permute-start.3 = (bf16[528,128]{1,0:T(8,128)(2,1)S(1)}, bf16[528,128]{1,0:T(8,128)(2,1)S(1)}, u32[]{:S(2)}, u32[]{:S(2)}) collective-permute-start(bf16[528,128]{1,0:T(8,128)(2,1)S(1)} %get-tuple-element.81), channel_id=1, source_target_pairs={{16,48},{48,80},{80,112},{112,144},{144,176},{176,208},{208,240},{... | collective-permute-start | bytes 405512 | tf_op jit(solution)/shard_map/ppermute | solution.py:409
  9.3 12.8 %collective-permute-start.4 = (f32[4,16,512]{2,1,0:T(8,128)S(1)}, f32[4,16,512]{2,1,0:T(8,128)S(1)}, u32[]{:S(2)}, u32[]{:S(2)}) collective-permute-start(f32[4,16,512]{2,1,0:T(8,128)S(1)} %get-tuple-element.80), channel_id=1, source_target_pairs={{0,16},{16,0},{1,17},{17,1},{2,18},{18,2},{3,19},{19,3},{4,20},{20... | collective-permute-start | bytes 393224 | tf_op jit(solution)/shard_map/ppermute | solution.py:419
  31.8 0.6 %copy-start.11 = (bf16[1,4,16,512]{3,2,1,0:T(8,128)(2,1)}, bf16[1,4,16,512]{3,2,1,0:T(8,128)(2,1)S(1)}, u32[]{:S(2)}) copy-start(bf16[1,4,16,512]{3,2,1,0:T(8,128)(2,1)S(1)} %get-tuple-element.95) | copy-start | bytes 196612

commit v7 on v6

--- a/solution.py
+++ b/solution.py
@@ -236,29 +236,39 @@
 def front_kernel(base, reach, mix, conv_part, cmask, wmask, conv, x_in, gain, pack_out, extra_out, row_out):
     steps, slots, width = x_in.shape
     taps = conv_part.shape[0]
-    outside = wmask[:, :1]
-    weight = tap_rows(conv)
-    pre = with_inputs([conv_part[t] for t in range(taps)], weight, [x_in[t].astype(F32) for t in range(steps)])
-    count = mix.shape[0]
-    mixes = [mix[i] for i in range(count)]
-    gated = gated_rows(pre, [base[t] for t in range(steps)], mixes, steps)
-    gated = [row * (1.0 - outside) for row in gated]
-    for t in range(steps):
-        pack_out[pl.ds(t * slots, slots)] = gated[t] * gain[...]
-
-    def crossing(value):
-        return jnp.sum(value * outside, axis=0, keepdims=True)
-
-    slot_c = [jnp.sum(cmask[pl.ds(t * slots, slots)].astype(F32), axis=0, keepdims=True) for t in range(steps)]
-    rows = [crossing(reach[t]) for t in range(steps)]
-    rows += [crossing(value) for value in mixes]
-    rows += [crossing(value) for value in pre]
-    rows += weight + [gain[...], jnp.concatenate(slot_c, axis=1)]
-    extra_out[...] = jnp.concatenate(rows + [jnp.zeros_like(gain)] * (extra_out.shape[0] - len(rows)), axis=0)
     lane = lax.broadcasted_iota(jnp.int32, (slots, 128), 1)
     slot = lax.broadcasted_iota(jnp.int32, (slots, 128), 0)
     lanes = jnp.sum(jnp.where(lax.rem(lane, slots) == slot, wmask[...], 0.0), axis=0, keepdims=True)
-    row_out[...] = jnp.concatenate([square_sums(gated), lanes, jnp.zeros((6, 128), F32)], axis=0)
+    row_out[...] = jnp.broadcast_to(lanes, row_out.shape)
+
+    @pl.when(lax.axis_index("pipe") > 0)
+    def _():
+        pack_out[...] = jnp.zeros(pack_out.shape, F32)
+        extra_out[...] = jnp.zeros(extra_out.shape, F32)
+
+    @pl.when(lax.axis_index("pipe") == 0)
+    def _():
+        outside = wmask[:, :1]
+        weight = tap_rows(conv)
+        pre = with_inputs([conv_part[t] for t in range(taps)], weight, [x_in[t].astype(F32) for t in range(steps)])
+        count = mix.shape[0]
+        mixes = [mix[i] for i in range(count)]
+        gated = gated_rows(pre, [base[t] for t in range(steps)], mixes, steps)
+        gated = [row * (1.0 - outside) for row in gated]
+        for t in range(steps):
+            pack_out[pl.ds(t * slots, slots)] = gated[t] * gain[...]
+
+        def crossing(value):
+            return jnp.sum(value * outside, axis=0, keepdims=True)
+
+        slot_c = [jnp.sum(cmask[pl.ds(t * slots, slots)].astype(F32), axis=0, keepdims=True) for t in range(steps)]
+        rows = [crossing(reach[t]) for t in range(steps)]
+        rows += [crossing(value) for value in mixes]
+        rows += [crossing(value) for value in pre]
+        rows += weight + [gain[...], jnp.concatenate(slot_c, axis=1)]
+        rows.append(jnp.concatenate([square_sums(gated), jnp.zeros((1, width - 128), F32)], axis=1))
+        blank = jnp.zeros((extra_out.shape[0] - len(rows), width), F32)
+        extra_out[...] = jnp.concatenate(rows + [blank], axis=0)
 
 
 def fill_kernel(arrived, pack, extra, row, wmask, taps, other_out, sums_out):
@@ -274,7 +284,7 @@
     mixes = take(steps, number)
     pre = take(steps + number, steps)
     weight = take(2 * steps + number, taps + 1)
-    gain, slot_c = take(2 * steps + number + taps + 1, 2)
+    gain, slot_c, local = take(2 * steps + number + taps + 1, 3)
     state, rows = arrived_rows(arrived, taps, width // 128)
     lhs = [slot_c[:, t * nstate:(t + 1) * nstate] for t in range(steps)]
     lhs = jnp.concatenate(lhs + [jnp.zeros((16 - steps, nstate), F32)], axis=0).astype(BF16)
@@ -290,19 +300,12 @@
         square = jnp.sum(gated[t] * gated[t], axis=1, keepdims=True)
         here = (lane >= t * slots) & (lane < (t + 1) * slots)
         sums = jnp.where(here, square, sums)
-    sums = jnp.where(lax.axis_index("pipe") == 0, row[pl.ds(0, 1)], sums * row[pl.ds(1, 1)])
+    sums = local[:, :128] + sums * row[pl.ds(0, 1)]
     sums_out[...] = jnp.broadcast_to(sums[None], sums_out.shape)
 
 
-def finish_kernel(sums, own, channels, out):
-    steps, slots, _ = out.shape
-    scale = row_scales(sums[...], channels, steps * slots)
-    for t in range(steps):
-        out[t] = scaled(own[t], scale[t * slots:(t + 1) * slots]).astype(BF16)
-
-
 def second_kernel(
-    sums, other, arrived, base, reach, mix, conv_part, cmask, wmask, conv, channels, gated_out, sums_out
+    sums, other, arrived, base, reach, mix, conv_part, cmask, wmask, conv, channels, norm_out, gated_out, sums_out
 ):
     steps, slots, width = other.shape
     taps = conv_part.shape[0]
@@ -313,9 +316,11 @@
     mask = wmask[:, :1]
     pre = [conv_part[t] + mask * term for t, term in enumerate(window_terms(weight, rows))]
     scale = row_scales(sums[...], channels, steps * slots)
-    inputs = [
-        scaled(other[t], scale[t * slots:(t + 1) * slots]).astype(BF16).astype(F32) for t in range(steps)
-    ]
+    inputs = []
+    for t in range(steps):
+        row = scaled(other[t], scale[t * slots:(t + 1) * slots]).astype(BF16)
+        norm_out[t] = row
+        inputs.append(row.astype(F32))
     pre = with_inputs(pre, weight, inputs)
     gated = gated_rows(pre, start, [mix[i] for i in range(mix.shape[0])], steps)
     for t in range(steps):
@@ -347,7 +352,7 @@
     shape = jax.ShapeDtypeStruct
     step_rows = shape((steps, slots, width), F32)
     packed_slot = shape((rows + 16, nstate), BF16)
-    nextra = (2 * steps + npairs + taps + 3 + 7) // 8 * 8
+    nextra = (2 * steps + npairs + taps + 4 + 7) // 8 * 8
 
     def at(i, p, t):
         return (i * pipes + p) * tp + t
@@ -410,51 +415,38 @@
 
     whole, sums = pl.pallas_call(
         lambda *refs: fill_kernel(*refs[:5], taps, *refs[5:]),
-        out_shape=(step_rows, shape((pipes * tp, 1, 128), F32)),
+        out_shape=(step_rows, shape((tp, 1, 128), F32)),
         in_specs=[VMEM] * 5,
         out_specs=(VMEM,) * 2,
         compiler_params=PARAMS,
         name="fill",
     )(arrived, other_pack, other_extra, row, wmask)
-    other_whole = lax.ppermute(whole, "pipe", swap)
     section = lax.axis_index("pipe")
-    sums, section = lax.optimization_barrier((sums, section))
-    sums = lax.all_to_all(sums, ("pipe", "tp"), 0, 0)
-    sums, section = lax.optimization_barrier((sums, section))
-
-    def first_section(sums, other_whole, whole, later, base, reach, mix, conv_part, cmask, wmask, conv, gain):
-        return pl.pallas_call(
-            lambda sums, own, out: finish_kernel(sums, own, channels, out),
-            out_shape=shape((steps, slots, width), BF16),
-            in_specs=[VMEM] * 2,
-            out_specs=VMEM,
-            compiler_params=PARAMS,
-            name="finish",
-        )(sums, other_whole)
-
-    def second_section(sums, other_whole, whole, later, base, reach, mix, conv_part, cmask, wmask, conv, gain):
-        gated, sums = pl.pallas_call(
-            lambda *refs: second_kernel(*refs[:10], channels, *refs[10:]),
-            out_shape=(step_rows, shape((tp, 1, 128), F32)),
-            in_specs=[VMEM] * 10,
-            out_specs=(VMEM,) * 2,
-            compiler_params=PARAMS,
-            name="second",
-        )(sums, whole, later, base, reach, mix, conv_part, cmask, wmask, conv)
+    sums = lax.cond(section == 0, lambda sums: sums, lambda sums: lax.all_to_all(sums, "tp", 0, 0), sums)
+    rows_out = shape((steps, slots, width), BF16)
+    norm, gated, sums = pl.pallas_call(
+        lambda *refs: second_kernel(*refs[:10], channels, *refs[10:]),
+        out_shape=(rows_out, step_rows, shape((tp, 1, 128), F32)),
+        in_specs=[VMEM] * 10,
+        out_specs=(VMEM,) * 3,
+        compiler_params=PARAMS,
+        name="second",
+    )(sums, whole, later, base, reach, mix, conv_part, cmask, wmask, conv)
+    other_norm = lax.ppermute(norm, "pipe", swap)
+
+    def second_section(idle, sums, gated, gain):
         sums = lax.all_to_all(sums, "tp", 0, 0)
         return pl.pallas_call(
             lambda sums, gated, gain, out: last_kernel(sums, gated, gain, channels, out),
-            out_shape=shape((steps, slots, width), BF16),
+            out_shape=rows_out,
             in_specs=[VMEM] * 3,
             out_specs=VMEM,
             compiler_params=PARAMS,
             name="last",
         )(sums, gated, gain)
 
-    result = lax.cond(
-        section == 0, first_section, second_section,
-        sums, other_whole, whole, later, base, reach, mix, conv_part, cmask, wmask, conv, norm_gain,
-    )
+    result = lax.cond(section == 0, lambda idle, *others: idle, second_section, x_in, sums, gated, norm_gain)
+    result = lax.cond(section == 0, lambda mine, sent: sent, lambda mine, sent: mine, result, other_norm)
     return result[None]
 
 

time: 32.9 us -> 32.2 us (0.979)
  waiting for transfers between devices: 0.01 us -> 0.94 us
  blocking collectives: 21.3 us -> 20.4 us
  starting transfers between devices: 7.68 us -> 7.07 us
    ppermute x1, starting transfers between devices: 3.02 us -> 0.09 us  [body(): other_pack = lax.ppermute(pack, 'pipe', swap)]
    ppermute x1, starting transfers between devices: 1.72 us -> 4.26 us  [body(): later = lax.ppermute(leaving, ('roll', 'pipe', 'tp'), second_moves)]
    ppermute x1, waiting for transfers between devices: 0.01 us -> 0.93 us  [body(): other_extra = lax.ppermute(extra, 'pipe', swap)]
    all_to_all x1, blocking collectives: 12.1 us -> 11.2 us  [body(): lax.all_to_all(sums, 'tp', 0, 0)]
    ppermute x1, starting transfers between devices: 0.71 us -> 0.09 us  [body(): other_norm = lax.ppermute(norm, 'pipe', swap)]
    ppermute x1, starting transfers between devices: 0.1 us -> 0.5 us  [body(): other_extra = lax.ppermute(extra, 'pipe', swap)]
  transfers between devices with their start and end apart: 5 -> 5, of which waited for: 0 -> 1; matrix products, arithmetic and copies ran while one was open for 0% -> 0% of each run, Pallas kernels for 6% -> 6%
where the time goes in v7:
time: 32.2 us; the launch traced here: 31.6 us
  blocking collectives  20.4 us (63%)
  starting transfers between devices  7.07 us (22%)
  Pallas kernels  2.28 us (7%)
  waiting for transfers between devices  0.94 us (3%)
  local copies, waits for them, and re-layouts  0.68 us (2%)
    all_to_all x1, blocking collectives, body(): lax.all_to_all(sums, 'tp', 0, 0)  11.2 us
    all_to_all x1, blocking collectives, second_section(): sums = lax.all_to_all(sums, 'tp', 0, 0)  9.11 us
    ppermute x1, starting transfers between devices, body(): later = lax.ppermute(leaving, ('roll', 'pipe', 'tp'), second_moves)  4.26 us
    ppermute x1, starting transfers between devices, body(): arrived = lax.ppermute(leaving, ('roll', 'pipe', 'tp'), first_moves)  2.13 us
    pallas_call x1, Pallas kernels, body(): pl.pallas_call(local_kernel, out_shape=(step_rows, step_rows, shape((npai...  1.5 us
    ppermute x1, waiting for transfers between devices, body(): other_extra = lax.ppermute(extra, 'pipe', swap)  0.93 us
    unnamed x28, local copies, waits for them, and re-layouts  0.68 us
  transfers between devices with their start and end apart: 5, of which 1 were waited for; matrix products, arithmetic and copies ran while one was open for 0% of the time, Pallas kernels for 6%

profile of v7, /device:TPU:1, one launch (start us, length us, event | category | flops | bytes accessed | tf_op | source)
XLA Modules:
  0.0 31.6 jit_solution(7780927705495577903)
XLA Ops:
  0.0 0.0 copy-start.10
  0.0 0.0 copy-start.9
  0.1 0.1 crossing.1.after
  0.2 2.1 %collective-permute-start = (bf16[528,128]{1,0:T(8,128)(2,1)S(1)}, bf16[528,128]{1,0:T(8,128)(2,1)S(1)}, u32[]{:S(2)}, u32[]{:S(2)}) collective-permute-start(bf16[528,128]{1,0:T(8,128)(2,1)S(1)} %crossing.1.after), channel_id=1, source_target_pairs={{0,48},{32,80},{64,112},{96,144},{128,176},{160,208},{192,240},{48... | collective-permute-start | bytes 405512 | tf_op jit(solution)/shard_map/ppermute | solution.py:384
  2.3 0.0 copy-done.1
  2.4 1.5 %local.1 = (f32[4,16,512]{2,1,0:T(8,128)S(1)}, f32[4,16,512]{2,1,0:T(8,128)S(1)}, f32[10,16,512]{2,1,0:T(8,128)S(1)}, f32[3,16,512]{2,1,0:T(8,128)S(1)}, bf16[64...) custom-call(bf16[528,128]{1,0:T(8,128)(2,1)S(1)} %crossing.1.after, s32[128]{0:T(128)S(1)} %copy-done.7, ...), custom_call_target="tpu_custom_call" | custom-call | flops 20000000 | bytes 4000000 | tf_op jit(solution)/shard_map/local/pallas_call | solution.py:386
  3.9 4.3 %collective-permute-start.3 = (bf16[528,128]{1,0:T(8,128)(2,1)S(1)}, bf16[528,128]{1,0:T(8,128)(2,1)S(1)}, u32[]{:S(2)}, u32[]{:S(2)}) collective-permute-start(bf16[528,128]{1,0:T(8,128)(2,1)S(1)} %get-tuple-element.57), channel_id=1, source_target_pairs={{16,48},{48,80},{80,112},{112,144},{144,176},{176,208},{208,240},{... | collective-permute-start | bytes 405512 | tf_op jit(solution)/shard_map/ppermute | solution.py:414
  8.2 0.1 collective-permute-start.1
  8.3 0.5 %collective-permute-start.2 = (f32[32,512]{1,0:T(8,128)S(1)}, f32[32,512]{1,0:T(8,128)S(1)}, u32[]{:S(2)}, u32[]{:S(2)}) collective-permute-start(f32[32,512]{1,0:T(8,128)S(1)} %get-tuple-element.53), channel_id=1, source_target_pairs={{0,16},{16,0},{1,17},{17,1},{2,18},{18,2},{3,19},{19,3},{4,20},{20... | collective-permute-start | bytes 196616 | tf_op jit(solution)/shard_map/ppermute | solution.py:412
  8.8 0.9 %collective-permute-done.2.refs_2_ = f32[32,512]{1,0:T(8,128)S(1)} collective-permute-done((f32[32,512]{1,0:T(8,128)S(1)}, f32[32,512]{1,0:T(8,128)S(1)}, u32[]{:S(2)}, u32[]{:S(2)}) %collective-permute-start.2) | collective-permute-done | bytes 65568 | tf_op jit(solution)/shard_map/ppermute | solution.py:412
  9.7 0.0 collective-permute-done.1.refs_1_
  9.7 0.0 collective-permute-done.refs_0_
  9.7 0.3 fill.1
  10.0 11.3 %conditional.3 = (f32[16,1,128]{2,1,0:T(1,128)S(1)}) conditional(s32[]{:T(128)} %convert_element_type.2, f32[16,1,128]{2,1,0:T(1,128)S(1)} %get-tuple-element.55, f32[16,1,128]{2,1,0:T(1,128)S(1)} %get-tuple-element.55), branch_computations={%region_0.0_spmd, %region_1.0_spmd} | conditional | bytes 32776 | solution.py:425
  10.0 11.2 %all_to_all.8 = f32[16,1,128]{2,1,0:T(1,128)S(1)} all-to-all(f32[16,1,128]{2,1,0:T(1,128)S(1)} %copy.23), channel_id=1, replica_groups=mesh['roll'=8,'pipe'=2,'tp'=16] {'tp'}, dimensions={0} | all-to-all | bytes 16384 | tf_op jit(solution)/shard_map/cond/branch_0_fun/all_to_all | solution.py:425
  21.3 0.0 collective-permute-done.3.refs_2_
  21.3 0.3 %second.1 = (bf16[4,16,512]{2,1,0:T(8,128)(2,1)S(1)}, f32[4,16,512]{2,1,0:T(8,128)S(1)}, f32[16,1,128]{2,1,0:T(1,128)S(1)}) custom-call(f32[16,1,128]{2,1,0:T(1,128)S(1)} %get-tuple-element.64.refs_0_, f32[4,16,512]{2,1,0:T(8,128)S(1)} %get-tuple-element.56.refs_1_, bf16[528,128]{1,0:T(8,128)(2,1)S(1)} %collective-permute-done.3.refs_2_, ...), custom_call_target="tpu_custom_call" | custom-call | tf_op jit(solution)/shard_map/second/pallas_call | solution.py:427
  21.6 0.1 collective-permute-start.4
  21.7 9.2 %conditional.4 = (bf16[4,16,512]{2,1,0:T(8,128)(2,1)S(1)}) conditional(s32[]{:T(128)} %convert_element_type.2, (f32[16,1,128]{2,1,0:T(1,128)S(1)}, f32[4,16,512]{2,1,0:T(8,128)S(1)}, f32[1,512]{1,0:T(1,128)S(1)}) %tuple.35, bf16[4,16,512]{2,1,0:T(8,128)(2,1)S(1)} %copy-done.11), branch_computations={%region_2.0_spmd, %region_3.0_spmd} | conditional | bytes 131080 | solution.py:448
  21.7 9.1 %all_to_all.9.sums = f32[16,1,128]{2,1,0:T(1,128)S(1)} all-to-all(f32[16,1,128]{2,1,0:T(1,128)S(1)} %get-tuple-element.28), channel_id=1, replica_groups=mesh['roll'=8,'pipe'=2,'tp'=16] {'tp'}, dimensions={0} | all-to-all | bytes 16384 | tf_op jit(solution)/shard_map/cond/branch_0_fun/all_to_all | solution.py:438
  30.8 0.1 last.1
  31.0 0.0 collective-permute-done.4
  31.0 0.0 copy-start.12
  31.0 0.6 %copy-done.12 = bf16[1,4,16,512]{3,2,1,0:T(8,128)(2,1)} copy-done((bf16[1,4,16,512]{3,2,1,0:T(8,128)(2,1)}, bf16[1,4,16,512]{3,2,1,0:T(8,128)(2,1)S(1)}, u32[]{:S(2)}) %copy-start.12) | copy-done | bytes 65560
  (26 shorter events, 0.1 us)
Async XLA Ops:
  0.0 2.3 %copy-start.7 = (s32[128]{0:T(128)S(1)}, s32[128]{0:T(128)}, u32[]{:S(2)}) copy-start(s32[128]{0:T(128)} %parent.1) | copy-start | bytes 1540
  0.0 2.3 %copy-start.1 = (bf16[1,16,3,512]{3,1,2,0:T(8,128)(2,1)S(1)}, bf16[1,16,3,512]{3,1,2,0:T(8,128)(2,1)}, u32[]{:S(2)}) copy-start(bf16[1,16,3,512]{3,1,2,0:T(8,128)(2,1)} %param.20) | copy-start | bytes 147460
  0.0 2.3 %copy-start = (bf16[1,16,8,64,128]{4,3,2,1,0:T(8,128)(2,1)S(1)}, bf16[1,16,8,64,128]{4,3,2,1,0:T(8,128)(2,1)}, u32[]{:S(2)}) copy-start(bf16[1,16,8,64,128]{4,3,2,1,0:T(8,128)(2,1)} %param.19) | copy-start | bytes 6291460
  0.0 2.3 %copy-start.10 = (f32[1,8]{1,0:T(1,128)S(1)}, f32[1,8]{1,0:T(1,128)}, u32[]{:S(2)}) copy-start(f32[1,8]{1,0:T(1,128)} %skip_d.1) | copy-start | bytes 100
  0.0 2.3 %copy-start.9 = (f32[1,8]{1,0:T(1,128)S(1)}, f32[1,8]{1,0:T(1,128)}, u32[]{:S(2)}) copy-start(f32[1,8]{1,0:T(1,128)} %dt_bias.1) | copy-start | bytes 100
  0.0 2.3 %copy-start.8 = (f32[1,8]{1,0:T(1,128)S(1)}, f32[1,8]{1,0:T(1,128)}, u32[]{:S(2)}) copy-start(f32[1,8]{1,0:T(1,128)} %a_log.1) | copy-start | bytes 100
  0.0 2.3 %copy-start.3 = (bf16[1,4,512]{2,1,0:T(4,128)(2,1)S(1)}, bf16[1,4,512]{2,1,0:T(4,128)(2,1)}, u32[]{:S(2)}) copy-start(bf16[1,4,512]{2,1,0:T(4,128)(2,1)} %param.26) | copy-start | bytes 12292
  0.0 2.3 %copy-start.4 = (bf16[1,4,16,128]{3,2,1,0:T(8,128)(2,1)S(1)}, bf16[1,4,16,128]{3,2,1,0:T(8,128)(2,1)}, u32[]{:S(2)}) copy-start(bf16[1,4,16,128]{3,2,1,0:T(8,128)(2,1)} %param.25) | copy-start | bytes 49156
  0.1 2.3 %copy-start.5 = (bf16[1,4,16,128]{3,2,1,0:T(8,128)(2,1)S(1)}, bf16[1,4,16,128]{3,2,1,0:T(8,128)(2,1)}, u32[]{:S(2)}) copy-start(bf16[1,4,16,128]{3,2,1,0:T(8,128)(2,1)} %param.24) | copy-start | bytes 49156
  0.1 2.3 %copy-start.6 = (f32[1,4,16,8]{2,3,1,0:T(8,128)S(1)}, f32[1,4,16,8]{2,3,1,0:T(8,128)}, u32[]{:S(2)}) copy-start(f32[1,4,16,8]{2,3,1,0:T(8,128)} %param.23) | copy-start | bytes 6148
  0.1 2.3 %copy-start.2 = (bf16[1,4,16,512]{3,2,1,0:T(8,128)(2,1)S(1)}, bf16[1,4,16,512]{3,2,1,0:T(8,128)(2,1)}, u32[]{:S(2)}) copy-start(bf16[1,4,16,512]{3,2,1,0:T(8,128)(2,1)} %param.22) | copy-start | bytes 196612
  0.1 8.1 %copy-start.11 = (bf16[4,16,512]{2,1,0:T(8,128)(2,1)S(1)}, bf16[4,16,512]{2,1,0:T(8,128)(2,1)}, u32[]{:S(2)}) copy-start(bf16[4,16,512]{2,1,0:T(8,128)(2,1)} %x_in.1) | copy-start | bytes 196612
  0.1 8.1 %copy-start.13 = (f32[1,512]{1,0:T(1,128)S(1)}, f32[1,512]{1,0:T(1,128)}, u32[]{:S(2)}) copy-start(f32[1,512]{1,0:T(1,128)} %gain.1) | copy-start | bytes 6148
  0.2 9.6 %collective-permute-start = (bf16[528,128]{1,0:T(8,128)(2,1)S(1)}, bf16[528,128]{1,0:T(8,128)(2,1)S(1)}, u32[]{:S(2)}, u32[]{:S(2)}) collective-permute-start(bf16[528,128]{1,0:T(8,128)(2,1)S(1)} %crossing.1.after), channel_id=1, source_target_pairs={{0,48},{32,80},{64,112},{96,144},{128,176},{160,208},{192,240},{48... | collective-permute-start | bytes 405512 | tf_op jit(solution)/shard_map/ppermute | solution.py:384
  3.9 17.4 %collective-permute-start.3 = (bf16[528,128]{1,0:T(8,128)(2,1)S(1)}, bf16[528,128]{1,0:T(8,128)(2,1)S(1)}, u32[]{:S(2)}, u32[]{:S(2)}) collective-permute-start(bf16[528,128]{1,0:T(8,128)(2,1)S(1)} %get-tuple-element.57), channel_id=1, source_target_pairs={{16,48},{48,80},{80,112},{112,144},{144,176},{176,208},{208,240},{... | collective-permute-start | bytes 405512 | tf_op jit(solution)/shard_map/ppermute | solution.py:414
  8.2 1.5 %collective-permute-start.1 = (f32[64,512]{1,0:T(8,128)S(1)}, f32[64,512]{1,0:T(8,128)S(1)}, u32[]{:S(2)}, u32[]{:S(2)}) collective-permute-start(f32[64,512]{1,0:T(8,128)S(1)} %get-tuple-element.52), channel_id=1, source_target_pairs={{0,16},{16,0},{1,17},{17,1},{2,18},{18,2},{3,19},{19,3},{4,20},{20... | collective-permute-start | bytes 393224 | tf_op jit(solution)/shard_map/ppermute | solution.py:413
  8.3 1.4 %collective-permute-start.2 = (f32[32,512]{1,0:T(8,128)S(1)}, f32[32,512]{1,0:T(8,128)S(1)}, u32[]{:S(2)}, u32[]{:S(2)}) collective-permute-start(f32[32,512]{1,0:T(8,128)S(1)} %get-tuple-element.53), channel_id=1, source_target_pairs={{0,16},{16,0},{1,17},{17,1},{2,18},{18,2},{3,19},{19,3},{4,20},{20... | collective-permute-start | bytes 196616 | tf_op jit(solution)/shard_map/ppermute | solution.py:412
  21.6 9.4 %collective-permute-start.4 = (bf16[4,16,512]{2,1,0:T(8,128)(2,1)S(1)}, bf16[4,16,512]{2,1,0:T(8,128)(2,1)S(1)}, u32[]{:S(2)}, u32[]{:S(2)}) collective-permute-start(bf16[4,16,512]{2,1,0:T(8,128)(2,1)S(1)} %get-tuple-element.60), channel_id=1, source_target_pairs={{0,16},{16,0},{1,17},{17,1},{2,18},{18,2},{3,19},{19,3},{4,20},{20... | collective-permute-start | bytes 196616 | tf_op jit(solution)/shard_map/ppermute | solution.py:435
  31.0 0.6 %copy-start.12 = (bf16[1,4,16,512]{3,2,1,0:T(8,128)(2,1)}, bf16[1,4,16,512]{3,2,1,0:T(8,128)(2,1)S(1)}, u32[]{:S(2)}) copy-start(bf16[1,4,16,512]{3,2,1,0:T(8,128)(2,1)S(1)} %get-tuple-element.75) | copy-start | bytes 196612

commit v8 on v7

--- a/solution.py
+++ b/solution.py
@@ -72,6 +72,8 @@
         copy.start()
         get_window.wait()
         out[pl.ds(nrows, 16)] = packed_window(window, row)
+        pad = out.shape[0] - nrows - 16
+        out[pl.ds(nrows + 16, pad)] = jnp.zeros((pad, out.shape[1]), BF16)
         copy.wait()
 
 
@@ -212,8 +214,7 @@
     return pre
 
 
-def arrived_rows(arrived, taps, groups):
-    nrows = arrived.shape[0] - 16
+def arrived_rows(arrived, nrows, taps, groups):
     packed = arrived[pl.ds(nrows, 16)].astype(F32)
     rows = [
         jnp.concatenate([packed[k * groups + j:k * groups + j + 1] for j in range(groups)], axis=1)
@@ -266,9 +267,9 @@
         rows += [crossing(value) for value in mixes]
         rows += [crossing(value) for value in pre]
         rows += weight + [gain[...], jnp.concatenate(slot_c, axis=1)]
-        rows.append(jnp.concatenate([square_sums(gated), jnp.zeros((1, width - 128), F32)], axis=1))
-        blank = jnp.zeros((extra_out.shape[0] - len(rows), width), F32)
-        extra_out[...] = jnp.concatenate(rows + [blank], axis=0)
+        sums = jnp.concatenate([square_sums(gated), jnp.zeros((1, width - 128), F32)], axis=1)
+        pack_out[pl.ds(steps * slots, 8)] = jnp.concatenate([sums, jnp.zeros((7, width), F32)], axis=0)
+        extra_out[...] = jnp.concatenate(rows + [jnp.zeros_like(gain)] * (extra_out.shape[0] - len(rows)), axis=0)
 
 
 def fill_kernel(arrived, pack, extra, row, wmask, taps, other_out, sums_out):
@@ -284,8 +285,8 @@
     mixes = take(steps, number)
     pre = take(steps + number, steps)
     weight = take(2 * steps + number, taps + 1)
-    gain, slot_c, local = take(2 * steps + number + taps + 1, 3)
-    state, rows = arrived_rows(arrived, taps, width // 128)
+    gain, slot_c = take(2 * steps + number + taps + 1, 2)
+    state, rows = arrived_rows(arrived, width, taps, width // 128)
     lhs = [slot_c[:, t * nstate:(t + 1) * nstate] for t in range(steps)]
     lhs = jnp.concatenate(lhs + [jnp.zeros((16 - steps, nstate), F32)], axis=0).astype(BF16)
     start = lax.dot_general(lhs, state, NT, preferred_element_type=F32)
@@ -300,7 +301,7 @@
         square = jnp.sum(gated[t] * gated[t], axis=1, keepdims=True)
         here = (lane >= t * slots) & (lane < (t + 1) * slots)
         sums = jnp.where(here, square, sums)
-    sums = local[:, :128] + sums * row[pl.ds(0, 1)]
+    sums = pack[pl.ds(steps * slots, 8)][:1, :128] + sums * row[pl.ds(0, 1)]
     sums_out[...] = jnp.broadcast_to(sums[None], sums_out.shape)
 
 
@@ -310,7 +311,7 @@
     steps, slots, width = other.shape
     taps = conv_part.shape[0]
     weight = tap_rows(conv)
-    state, rows = arrived_rows(arrived, taps, width // 128)
+    state, rows = arrived_rows(arrived, width, taps, width // 128)
     extra = lax.dot_general(cmask[...], state, NT, preferred_element_type=F32)
     start = [base[t] + extra[t * slots:(t + 1) * slots] * reach[t] for t in range(steps)]
     mask = wmask[:, :1]
@@ -352,7 +353,7 @@
     shape = jax.ShapeDtypeStruct
     step_rows = shape((steps, slots, width), F32)
     packed_slot = shape((rows + 16, nstate), BF16)
-    nextra = (2 * steps + npairs + taps + 4 + 7) // 8 * 8
+    nextra = steps * slots + 8
 
     def at(i, p, t):
         return (i * pipes + p) * tp + t
@@ -370,7 +371,7 @@
 
     leaving = pl.pallas_call(
         crossing_kernel,
-        out_shape=packed_slot,
+        out_shape=shape((rows + 80, nstate), BF16),
         in_specs=[HBM, HBM, HBM],
         out_specs=VMEM,
         scratch_shapes=[
@@ -403,7 +404,7 @@
 
     pack, extra, row = pl.pallas_call(
         front_kernel,
-        out_shape=(shape((steps * slots, width), F32), shape((nextra, width), F32), shape((8, 128), F32)),
+        out_shape=(shape((steps * slots + 8, width), F32), shape((nextra, width), F32), shape((8, 128), F32)),
         in_specs=[VMEM] * 9,
         out_specs=(VMEM,) * 3,
         compiler_params=PARAMS,

time: 32.2 us -> 31.4 us (0.975)
  waiting for transfers between devices: 0.94 us -> 0.01 us
    ppermute x1, starting transfers between devices: 0.09 us -> 3.24 us  [body(): other_pack = lax.ppermute(pack, 'pipe', swap)]
    ppermute x1, starting transfers between devices: 4.26 us -> 1.5 us  [body(): later = lax.ppermute(leaving, ('roll', 'pipe', 'tp'), second_moves)]
    ppermute x1, waiting for transfers between devices: 0.93 us -> 0.01 us  [body(): other_extra = lax.ppermute(extra, 'pipe', swap)]
    ppermute x1, starting transfers between devices: 0.5 us -> 0.1 us  [body(): other_extra = lax.ppermute(extra, 'pipe', swap)]
  transfers between devices with their start and end apart: 5 -> 5, of which waited for: 1 -> 0; matrix products, arithmetic and copies ran while one was open for 0% -> 0% of each run, Pallas kernels for 6% -> 6%
where the time goes in v8:
time: 31.4 us; the launch traced here: 30.8 us
  blocking collectives  20.5 us (65%)
  starting transfers between devices  7.06 us (22%)
  Pallas kernels  2.3 us (7%)
  local copies, waits for them, and re-layouts  0.68 us (2%)
    all_to_all x1, blocking collectives, body(): lax.all_to_all(sums, 'tp', 0, 0)  11.4 us
    all_to_all x1, blocking collectives, second_section(): sums = lax.all_to_all(sums, 'tp', 0, 0)  9.11 us
    ppermute x1, starting transfers between devices, body(): other_pack = lax.ppermute(pack, 'pipe', swap)  3.24 us
    ppermute x1, starting transfers between devices, body(): arrived = lax.ppermute(leaving, ('roll', 'pipe', 'tp'), first_moves)  2.13 us
    ppermute x1, starting transfers between devices, body(): later = lax.ppermute(leaving, ('roll', 'pipe', 'tp'), second_moves)  1.5 us
    pallas_call x1, Pallas kernels, body(): pl.pallas_call(local_kernel, out_shape=(step_rows, step_rows, shape((npai...  1.5 us
    unnamed x28, local copies, waits for them, and re-layouts  0.68 us
  transfers between devices with their start and end apart: 5, of which 0 were waited for; matrix products, arithmetic and copies ran while one was open for 0% of the time, Pallas kernels for 6%

profile of v8, /device:TPU:1, one launch (start us, length us, event | category | flops | bytes accessed | tf_op | source)
XLA Modules:
  0.0 30.8 jit_solution(6171046788076838723)
XLA Ops:
  0.1 0.1 crossing.1.after
  0.2 2.1 %collective-permute-start = (bf16[592,128]{1,0:T(8,128)(2,1)S(1)}, bf16[592,128]{1,0:T(8,128)(2,1)S(1)}, u32[]{:S(2)}, u32[]{:S(2)}) collective-permute-start(bf16[592,128]{1,0:T(8,128)(2,1)S(1)} %crossing.1.after), channel_id=1, source_target_pairs={{0,48},{32,80},{64,112},{96,144},{128,176},{160,208},{192,240},{48... | collective-permute-start | bytes 454664 | tf_op jit(solution)/shard_map/ppermute | solution.py:385
  2.3 0.0 copy-done.7
  2.3 0.0 copy-done
  2.4 1.5 %local.1 = (f32[4,16,512]{2,1,0:T(8,128)S(1)}, f32[4,16,512]{2,1,0:T(8,128)S(1)}, f32[10,16,512]{2,1,0:T(8,128)S(1)}, f32[3,16,512]{2,1,0:T(8,128)S(1)}, bf16[64...) custom-call(bf16[592,128]{1,0:T(8,128)(2,1)S(1)} %crossing.1.after, s32[128]{0:T(128)S(1)} %copy-done.7, ...), custom_call_target="tpu_custom_call" | custom-call | flops 20000000 | bytes 4000000 | tf_op jit(solution)/shard_map/local/pallas_call | solution.py:387
  3.9 0.0 copy-done.11
  4.0 3.2 %collective-permute-start.1 = (f32[72,512]{1,0:T(8,128)S(1)}, f32[72,512]{1,0:T(8,128)S(1)}, u32[]{:S(2)}, u32[]{:S(2)}) collective-permute-start(f32[72,512]{1,0:T(8,128)S(1)} %get-tuple-element.52), channel_id=1, source_target_pairs={{0,16},{16,0},{1,17},{17,1},{2,18},{18,2},{3,19},{19,3},{4,20},{20... | collective-permute-start | bytes 442376 | tf_op jit(solution)/shard_map/ppermute | solution.py:414
  7.2 0.1 collective-permute-start.2
  7.3 1.5 %collective-permute-start.3 = (bf16[528,128]{1,0:T(8,128)(2,1)S(1)}, bf16[528,128]{1,0:T(8,128)(2,1)S(1)}, u32[]{:S(2)}, u32[]{:S(2)}) collective-permute-start(bf16[528,128]{1,0:T(8,128)(2,1)S(1)} %get-tuple-element.57), channel_id=1, source_target_pairs={{16,48},{48,80},{80,112},{112,144},{144,176},{176,208},{208,240},{... | collective-permute-start | bytes 405512 | tf_op jit(solution)/shard_map/ppermute | solution.py:415
  8.8 0.0 collective-permute-done.1.refs_1_
  8.8 0.0 collective-permute-done.2.refs_2_
  8.8 0.0 collective-permute-done.refs_0_
  8.8 0.3 fill.1
  9.1 11.4 %conditional.3 = (f32[16,1,128]{2,1,0:T(1,128)S(1)}) conditional(s32[]{:T(128)} %convert_element_type.2, f32[16,1,128]{2,1,0:T(1,128)S(1)} %get-tuple-element.55, f32[16,1,128]{2,1,0:T(1,128)S(1)} %get-tuple-element.55), branch_computations={%region_0.0_spmd, %region_1.0_spmd} | conditional | bytes 32776 | solution.py:426
  9.1 11.4 %all_to_all.8 = f32[16,1,128]{2,1,0:T(1,128)S(1)} all-to-all(f32[16,1,128]{2,1,0:T(1,128)S(1)} %copy.23), channel_id=1, replica_groups=mesh['roll'=8,'pipe'=2,'tp'=16] {'tp'}, dimensions={0} | all-to-all | bytes 16384 | tf_op jit(solution)/shard_map/cond/branch_0_fun/all_to_all | solution.py:426
  20.5 0.0 collective-permute-done.3.refs_2_
  20.5 0.3 %second.1 = (bf16[4,16,512]{2,1,0:T(8,128)(2,1)S(1)}, f32[4,16,512]{2,1,0:T(8,128)S(1)}, f32[16,1,128]{2,1,0:T(1,128)S(1)}) custom-call(f32[16,1,128]{2,1,0:T(1,128)S(1)} %get-tuple-element.64.refs_0_, f32[4,16,512]{2,1,0:T(8,128)S(1)} %get-tuple-element.56.refs_1_, bf16[528,128]{1,0:T(8,128)(2,1)S(1)} %collective-permute-done.3.refs_2_, ...), custom_call_target="tpu_custom_call" | custom-call | tf_op jit(solution)/shard_map/second/pallas_call | solution.py:428
  20.8 0.1 collective-permute-start.4
  20.9 9.2 %conditional.4 = (bf16[4,16,512]{2,1,0:T(8,128)(2,1)S(1)}) conditional(s32[]{:T(128)} %convert_element_type.2, (f32[16,1,128]{2,1,0:T(1,128)S(1)}, f32[4,16,512]{2,1,0:T(8,128)S(1)}, f32[1,512]{1,0:T(1,128)S(1)}) %tuple.35, bf16[4,16,512]{2,1,0:T(8,128)(2,1)S(1)} %copy-done.11), branch_computations={%region_2.0_spmd, %region_3.0_spmd} | conditional | bytes 131080 | solution.py:449
  20.9 9.1 %all_to_all.9.sums = f32[16,1,128]{2,1,0:T(1,128)S(1)} all-to-all(f32[16,1,128]{2,1,0:T(1,128)S(1)} %get-tuple-element.28), channel_id=1, replica_groups=mesh['roll'=8,'pipe'=2,'tp'=16] {'tp'}, dimensions={0} | all-to-all | bytes 16384 | tf_op jit(solution)/shard_map/cond/branch_0_fun/all_to_all | solution.py:439
  30.1 0.1 last.1
  30.2 0.0 collective-permute-done.4
  30.2 0.0 copy-start.12
  30.2 0.6 %copy-done.12 = bf16[1,4,16,512]{3,2,1,0:T(8,128)(2,1)} copy-done((bf16[1,4,16,512]{3,2,1,0:T(8,128)(2,1)}, bf16[1,4,16,512]{3,2,1,0:T(8,128)(2,1)S(1)}, u32[]{:S(2)}) %copy-start.12) | copy-done | bytes 65560
  (26 shorter events, 0.1 us)
Async XLA Ops:
  0.0 2.3 %copy-start.7 = (s32[128]{0:T(128)S(1)}, s32[128]{0:T(128)}, u32[]{:S(2)}) copy-start(s32[128]{0:T(128)} %parent.1) | copy-start | bytes 1540
  0.0 2.3 %copy-start.1 = (bf16[1,16,3,512]{3,1,2,0:T(8,128)(2,1)S(1)}, bf16[1,16,3,512]{3,1,2,0:T(8,128)(2,1)}, u32[]{:S(2)}) copy-start(bf16[1,16,3,512]{3,1,2,0:T(8,128)(2,1)} %param.20) | copy-start | bytes 147460
  0.0 2.3 %copy-start = (bf16[1,16,8,64,128]{4,3,2,1,0:T(8,128)(2,1)S(1)}, bf16[1,16,8,64,128]{4,3,2,1,0:T(8,128)(2,1)}, u32[]{:S(2)}) copy-start(bf16[1,16,8,64,128]{4,3,2,1,0:T(8,128)(2,1)} %param.19) | copy-start | bytes 6291460
  0.0 2.3 %copy-start.10 = (f32[1,8]{1,0:T(1,128)S(1)}, f32[1,8]{1,0:T(1,128)}, u32[]{:S(2)}) copy-start(f32[1,8]{1,0:T(1,128)} %skip_d.1) | copy-start | bytes 100
  0.0 2.3 %copy-start.9 = (f32[1,8]{1,0:T(1,128)S(1)}, f32[1,8]{1,0:T(1,128)}, u32[]{:S(2)}) copy-start(f32[1,8]{1,0:T(1,128)} %dt_bias.1) | copy-start | bytes 100
  0.0 2.3 %copy-start.8 = (f32[1,8]{1,0:T(1,128)S(1)}, f32[1,8]{1,0:T(1,128)}, u32[]{:S(2)}) copy-start(f32[1,8]{1,0:T(1,128)} %a_log.1) | copy-start | bytes 100
  0.0 2.3 %copy-start.3 = (bf16[1,4,512]{2,1,0:T(4,128)(2,1)S(1)}, bf16[1,4,512]{2,1,0:T(4,128)(2,1)}, u32[]{:S(2)}) copy-start(bf16[1,4,512]{2,1,0:T(4,128)(2,1)} %param.26) | copy-start | bytes 12292
  0.0 2.3 %copy-start.4 = (bf16[1,4,16,128]{3,2,1,0:T(8,128)(2,1)S(1)}, bf16[1,4,16,128]{3,2,1,0:T(8,128)(2,1)}, u32[]{:S(2)}) copy-start(bf16[1,4,16,128]{3,2,1,0:T(8,128)(2,1)} %param.25) | copy-start | bytes 49156
  0.1 2.3 %copy-start.5 = (bf16[1,4,16,128]{3,2,1,0:T(8,128)(2,1)S(1)}, bf16[1,4,16,128]{3,2,1,0:T(8,128)(2,1)}, u32[]{:S(2)}) copy-start(bf16[1,4,16,128]{3,2,1,0:T(8,128)(2,1)} %param.24) | copy-start | bytes 49156
  0.1 2.3 %copy-start.6 = (f32[1,4,16,8]{2,3,1,0:T(8,128)S(1)}, f32[1,4,16,8]{2,3,1,0:T(8,128)}, u32[]{:S(2)}) copy-start(f32[1,4,16,8]{2,3,1,0:T(8,128)} %param.23) | copy-start | bytes 6148
  0.1 2.3 %copy-start.2 = (bf16[1,4,16,512]{3,2,1,0:T(8,128)(2,1)S(1)}, bf16[1,4,16,512]{3,2,1,0:T(8,128)(2,1)}, u32[]{:S(2)}) copy-start(bf16[1,4,16,512]{3,2,1,0:T(8,128)(2,1)} %param.22) | copy-start | bytes 196612
  0.1 3.8 %copy-start.11 = (bf16[4,16,512]{2,1,0:T(8,128)(2,1)S(1)}, bf16[4,16,512]{2,1,0:T(8,128)(2,1)}, u32[]{:S(2)}) copy-start(bf16[4,16,512]{2,1,0:T(8,128)(2,1)} %x_in.1) | copy-start | bytes 196612
  0.1 3.8 %copy-start.13 = (f32[1,512]{1,0:T(1,128)S(1)}, f32[1,512]{1,0:T(1,128)}, u32[]{:S(2)}) copy-start(f32[1,512]{1,0:T(1,128)} %gain.1) | copy-start | bytes 6148
  0.2 8.6 %collective-permute-start = (bf16[592,128]{1,0:T(8,128)(2,1)S(1)}, bf16[592,128]{1,0:T(8,128)(2,1)S(1)}, u32[]{:S(2)}, u32[]{:S(2)}) collective-permute-start(bf16[592,128]{1,0:T(8,128)(2,1)S(1)} %crossing.1.after), channel_id=1, source_target_pairs={{0,48},{32,80},{64,112},{96,144},{128,176},{160,208},{192,240},{48... | collective-permute-start | bytes 454664 | tf_op jit(solution)/shard_map/ppermute | solution.py:385
  4.0 4.8 %collective-permute-start.1 = (f32[72,512]{1,0:T(8,128)S(1)}, f32[72,512]{1,0:T(8,128)S(1)}, u32[]{:S(2)}, u32[]{:S(2)}) collective-permute-start(f32[72,512]{1,0:T(8,128)S(1)} %get-tuple-element.52), channel_id=1, source_target_pairs={{0,16},{16,0},{1,17},{17,1},{2,18},{18,2},{3,19},{19,3},{4,20},{20... | collective-permute-start | bytes 442376 | tf_op jit(solution)/shard_map/ppermute | solution.py:414
  7.2 1.6 %collective-permute-start.2 = (f32[72,512]{1,0:T(8,128)S(1)}, f32[72,512]{1,0:T(8,128)S(1)}, u32[]{:S(2)}, u32[]{:S(2)}) collective-permute-start(f32[72,512]{1,0:T(8,128)S(1)} %get-tuple-element.53), channel_id=1, source_target_pairs={{0,16},{16,0},{1,17},{17,1},{2,18},{18,2},{3,19},{19,3},{4,20},{20... | collective-permute-start | bytes 442376 | tf_op jit(solution)/shard_map/ppermute | solution.py:413
  7.3 13.2 %collective-permute-start.3 = (bf16[528,128]{1,0:T(8,128)(2,1)S(1)}, bf16[528,128]{1,0:T(8,128)(2,1)S(1)}, u32[]{:S(2)}, u32[]{:S(2)}) collective-permute-start(bf16[528,128]{1,0:T(8,128)(2,1)S(1)} %get-tuple-element.57), channel_id=1, source_target_pairs={{16,48},{48,80},{80,112},{112,144},{144,176},{176,208},{208,240},{... | collective-permute-start | bytes 405512 | tf_op jit(solution)/shard_map/ppermute | solution.py:415
  20.8 9.4 %collective-permute-start.4 = (bf16[4,16,512]{2,1,0:T(8,128)(2,1)S(1)}, bf16[4,16,512]{2,1,0:T(8,128)(2,1)S(1)}, u32[]{:S(2)}, u32[]{:S(2)}) collective-permute-start(bf16[4,16,512]{2,1,0:T(8,128)(2,1)S(1)} %get-tuple-element.60), channel_id=1, source_target_pairs={{0,16},{16,0},{1,17},{17,1},{2,18},{18,2},{3,19},{19,3},{4,20},{20... | collective-permute-start | bytes 196616 | tf_op jit(solution)/shard_map/ppermute | solution.py:436
  30.2 0.6 %copy-start.12 = (bf16[1,4,16,512]{3,2,1,0:T(8,128)(2,1)}, bf16[1,4,16,512]{3,2,1,0:T(8,128)(2,1)S(1)}, u32[]{:S(2)}) copy-start(bf16[1,4,16,512]{3,2,1,0:T(8,128)(2,1)S(1)} %get-tuple-element.75) | copy-start | bytes 196612

commit v9 on v8

--- a/solution.py
+++ b/solution.py
@@ -153,11 +153,11 @@
     cmask_out[...] = (c_all * all_outside).astype(BF16)
     c_inside = c_all * all_inside
     total = None
-    for s in range(0, slots, 2):
+    for s in range(0, slots, 4):
         lhs = jnp.concatenate(
-            [jnp.where(slot_of == s + i, c_inside, 0.0).astype(BF16) for i in range(2)], axis=1
+            [jnp.where(slot_of == s + i, c_inside, 0.0).astype(BF16) for i in range(4)], axis=1
         )
-        rhs = jnp.concatenate([state[held[s]], state[held[s + 1]]], axis=1)
+        rhs = jnp.concatenate([state[held[s + i]] for i in range(4)], axis=1)
         part = lax.dot_general(lhs, rhs, NT, preferred_element_type=F32)
         total = part if total is None else total + part
     for t in range(steps):

time: 31.4 us -> 31.4 us (level)
  no operation moved by 1% of the time
where the time goes in v9:
time: 31.4 us; the launch traced here: 30.8 us
  blocking collectives  20.5 us (65%)
  starting transfers between devices  7.06 us (22%)
  Pallas kernels  2.3 us (7%)
  local copies, waits for them, and re-layouts  0.68 us (2%)
    all_to_all x1, blocking collectives, body(): lax.all_to_all(sums, 'tp', 0, 0)  11.4 us
    all_to_all x1, blocking collectives, second_section(): sums = lax.all_to_all(sums, 'tp', 0, 0)  9.11 us
    ppermute x1, starting transfers between devices, body(): other_pack = lax.ppermute(pack, 'pipe', swap)  3.24 us
    ppermute x1, starting transfers between devices, body(): arrived = lax.ppermute(leaving, ('roll', 'pipe', 'tp'), first_moves)  2.13 us
    ppermute x1, starting transfers between devices, body(): later = lax.ppermute(leaving, ('roll', 'pipe', 'tp'), second_moves)  1.5 us
    pallas_call x1, Pallas kernels, body(): pl.pallas_call(local_kernel, out_shape=(step_rows, step_rows, shape((npai...  1.5 us
    unnamed x28, local copies, waits for them, and re-layouts  0.68 us
  transfers between devices with their start and end apart: 5, of which 0 were waited for; matrix products, arithmetic and copies ran while one was open for 0% of the time, Pallas kernels for 6%

profile of v9, /device:TPU:1, one launch (start us, length us, event | category | flops | bytes accessed | tf_op | source)
XLA Modules:
  0.0 30.8 jit_solution(15245931833823147878)
XLA Ops:
  0.0 0.0 copy-start.10
  0.0 0.0 copy-start.9
  0.0 0.0 copy-start.8
  0.1 0.1 crossing.1.after
  0.2 2.1 %collective-permute-start = (bf16[592,128]{1,0:T(8,128)(2,1)S(1)}, bf16[592,128]{1,0:T(8,128)(2,1)S(1)}, u32[]{:S(2)}, u32[]{:S(2)}) collective-permute-start(bf16[592,128]{1,0:T(8,128)(2,1)S(1)} %crossing.1.after), channel_id=1, source_target_pairs={{0,48},{32,80},{64,112},{96,144},{128,176},{160,208},{192,240},{48... | collective-permute-start | bytes 454664 | tf_op jit(solution)/shard_map/ppermute | solution.py:385
  2.4 1.5 %local.1 = (f32[4,16,512]{2,1,0:T(8,128)S(1)}, f32[4,16,512]{2,1,0:T(8,128)S(1)}, f32[10,16,512]{2,1,0:T(8,128)S(1)}, f32[3,16,512]{2,1,0:T(8,128)S(1)}, bf16[64...) custom-call(bf16[592,128]{1,0:T(8,128)(2,1)S(1)} %crossing.1.after, s32[128]{0:T(128)S(1)} %copy-done.7, ...), custom_call_target="tpu_custom_call" | custom-call | flops 20000000 | bytes 4000000 | tf_op jit(solution)/shard_map/local/pallas_call | solution.py:387
  4.0 3.2 %collective-permute-start.1 = (f32[72,512]{1,0:T(8,128)S(1)}, f32[72,512]{1,0:T(8,128)S(1)}, u32[]{:S(2)}, u32[]{:S(2)}) collective-permute-start(f32[72,512]{1,0:T(8,128)S(1)} %get-tuple-element.52), channel_id=1, source_target_pairs={{0,16},{16,0},{1,17},{17,1},{2,18},{18,2},{3,19},{19,3},{4,20},{20... | collective-permute-start | bytes 442376 | tf_op jit(solution)/shard_map/ppermute | solution.py:414
  7.2 0.1 collective-permute-start.2
  7.3 1.5 %collective-permute-start.3 = (bf16[528,128]{1,0:T(8,128)(2,1)S(1)}, bf16[528,128]{1,0:T(8,128)(2,1)S(1)}, u32[]{:S(2)}, u32[]{:S(2)}) collective-permute-start(bf16[528,128]{1,0:T(8,128)(2,1)S(1)} %get-tuple-element.57), channel_id=1, source_target_pairs={{16,48},{48,80},{80,112},{112,144},{144,176},{176,208},{208,240},{... | collective-permute-start | bytes 405512 | tf_op jit(solution)/shard_map/ppermute | solution.py:415
  8.8 0.0 collective-permute-done.1.refs_1_
  8.8 0.0 collective-permute-done.2.refs_2_
  8.8 0.0 collective-permute-done.refs_0_
  8.8 0.3 fill.1
  9.1 11.4 %conditional.3 = (f32[16,1,128]{2,1,0:T(1,128)S(1)}) conditional(s32[]{:T(128)} %convert_element_type.2, f32[16,1,128]{2,1,0:T(1,128)S(1)} %get-tuple-element.55, f32[16,1,128]{2,1,0:T(1,128)S(1)} %get-tuple-element.55), branch_computations={%region_0.0_spmd, %region_1.0_spmd} | conditional | bytes 32776 | solution.py:426
  9.1 11.4 %all_to_all.8 = f32[16,1,128]{2,1,0:T(1,128)S(1)} all-to-all(f32[16,1,128]{2,1,0:T(1,128)S(1)} %copy.23), channel_id=1, replica_groups=mesh['roll'=8,'pipe'=2,'tp'=16] {'tp'}, dimensions={0} | all-to-all | bytes 16384 | tf_op jit(solution)/shard_map/cond/branch_0_fun/all_to_all | solution.py:426
  20.5 0.0 collective-permute-done.3.refs_2_
  20.5 0.3 %second.1 = (bf16[4,16,512]{2,1,0:T(8,128)(2,1)S(1)}, f32[4,16,512]{2,1,0:T(8,128)S(1)}, f32[16,1,128]{2,1,0:T(1,128)S(1)}) custom-call(f32[16,1,128]{2,1,0:T(1,128)S(1)} %get-tuple-element.64.refs_0_, f32[4,16,512]{2,1,0:T(8,128)S(1)} %get-tuple-element.56.refs_1_, bf16[528,128]{1,0:T(8,128)(2,1)S(1)} %collective-permute-done.3.refs_2_, ...), custom_call_target="tpu_custom_call" | custom-call | tf_op jit(solution)/shard_map/second/pallas_call | solution.py:428
  20.8 0.1 collective-permute-start.4
  20.9 9.2 %conditional.4 = (bf16[4,16,512]{2,1,0:T(8,128)(2,1)S(1)}) conditional(s32[]{:T(128)} %convert_element_type.2, (f32[16,1,128]{2,1,0:T(1,128)S(1)}, f32[4,16,512]{2,1,0:T(8,128)S(1)}, f32[1,512]{1,0:T(1,128)S(1)}) %tuple.35, bf16[4,16,512]{2,1,0:T(8,128)(2,1)S(1)} %copy-done.11), branch_computations={%region_2.0_spmd, %region_3.0_spmd} | conditional | bytes 131080 | solution.py:449
  20.9 9.1 %all_to_all.9.sums = f32[16,1,128]{2,1,0:T(1,128)S(1)} all-to-all(f32[16,1,128]{2,1,0:T(1,128)S(1)} %get-tuple-element.28), channel_id=1, replica_groups=mesh['roll'=8,'pipe'=2,'tp'=16] {'tp'}, dimensions={0} | all-to-all | bytes 16384 | tf_op jit(solution)/shard_map/cond/branch_0_fun/all_to_all | solution.py:439
  30.1 0.1 last.1
  30.2 0.0 collective-permute-done.4
  30.2 0.0 copy-start.12
  30.2 0.6 %copy-done.12 = bf16[1,4,16,512]{3,2,1,0:T(8,128)(2,1)} copy-done((bf16[1,4,16,512]{3,2,1,0:T(8,128)(2,1)}, bf16[1,4,16,512]{3,2,1,0:T(8,128)(2,1)S(1)}, u32[]{:S(2)}) %copy-start.12) | copy-done | bytes 65560
  (26 shorter events, 0.1 us)
Async XLA Ops:
  0.0 2.3 %copy-start.7 = (s32[128]{0:T(128)S(1)}, s32[128]{0:T(128)}, u32[]{:S(2)}) copy-start(s32[128]{0:T(128)} %parent.1) | copy-start | bytes 1540
  0.0 2.3 %copy-start.1 = (bf16[1,16,3,512]{3,1,2,0:T(8,128)(2,1)S(1)}, bf16[1,16,3,512]{3,1,2,0:T(8,128)(2,1)}, u32[]{:S(2)}) copy-start(bf16[1,16,3,512]{3,1,2,0:T(8,128)(2,1)} %param.20) | copy-start | bytes 147460
  0.0 2.3 %copy-start = (bf16[1,16,8,64,128]{4,3,2,1,0:T(8,128)(2,1)S(1)}, bf16[1,16,8,64,128]{4,3,2,1,0:T(8,128)(2,1)}, u32[]{:S(2)}) copy-start(bf16[1,16,8,64,128]{4,3,2,1,0:T(8,128)(2,1)} %param.19) | copy-start | bytes 6291460
  0.0 2.3 %copy-start.10 = (f32[1,8]{1,0:T(1,128)S(1)}, f32[1,8]{1,0:T(1,128)}, u32[]{:S(2)}) copy-start(f32[1,8]{1,0:T(1,128)} %skip_d.1) | copy-start | bytes 100
  0.0 2.3 %copy-start.9 = (f32[1,8]{1,0:T(1,128)S(1)}, f32[1,8]{1,0:T(1,128)}, u32[]{:S(2)}) copy-start(f32[1,8]{1,0:T(1,128)} %dt_bias.1) | copy-start | bytes 100
  0.0 2.3 %copy-start.8 = (f32[1,8]{1,0:T(1,128)S(1)}, f32[1,8]{1,0:T(1,128)}, u32[]{:S(2)}) copy-start(f32[1,8]{1,0:T(1,128)} %a_log.1) | copy-start | bytes 100
  0.0 2.3 %copy-start.3 = (bf16[1,4,512]{2,1,0:T(4,128)(2,1)S(1)}, bf16[1,4,512]{2,1,0:T(4,128)(2,1)}, u32[]{:S(2)}) copy-start(bf16[1,4,512]{2,1,0:T(4,128)(2,1)} %param.26) | copy-start | bytes 12292
  0.0 2.3 %copy-start.4 = (bf16[1,4,16,128]{3,2,1,0:T(8,128)(2,1)S(1)}, bf16[1,4,16,128]{3,2,1,0:T(8,128)(2,1)}, u32[]{:S(2)}) copy-start(bf16[1,4,16,128]{3,2,1,0:T(8,128)(2,1)} %param.25) | copy-start | bytes 49156
  0.1 2.3 %copy-start.5 = (bf16[1,4,16,128]{3,2,1,0:T(8,128)(2,1)S(1)}, bf16[1,4,16,128]{3,2,1,0:T(8,128)(2,1)}, u32[]{:S(2)}) copy-start(bf16[1,4,16,128]{3,2,1,0:T(8,128)(2,1)} %param.24) | copy-start | bytes 49156
  0.1 2.3 %copy-start.6 = (f32[1,4,16,8]{2,3,1,0:T(8,128)S(1)}, f32[1,4,16,8]{2,3,1,0:T(8,128)}, u32[]{:S(2)}) copy-start(f32[1,4,16,8]{2,3,1,0:T(8,128)} %param.23) | copy-start | bytes 6148
  0.1 2.3 %copy-start.2 = (bf16[1,4,16,512]{3,2,1,0:T(8,128)(2,1)S(1)}, bf16[1,4,16,512]{3,2,1,0:T(8,128)(2,1)}, u32[]{:S(2)}) copy-start(bf16[1,4,16,512]{3,2,1,0:T(8,128)(2,1)} %param.22) | copy-start | bytes 196612
  0.1 3.8 %copy-start.11 = (bf16[4,16,512]{2,1,0:T(8,128)(2,1)S(1)}, bf16[4,16,512]{2,1,0:T(8,128)(2,1)}, u32[]{:S(2)}) copy-start(bf16[4,16,512]{2,1,0:T(8,128)(2,1)} %x_in.1) | copy-start | bytes 196612
  0.1 3.8 %copy-start.13 = (f32[1,512]{1,0:T(1,128)S(1)}, f32[1,512]{1,0:T(1,128)}, u32[]{:S(2)}) copy-start(f32[1,512]{1,0:T(1,128)} %gain.1) | copy-start | bytes 6148
  0.2 8.6 %collective-permute-start = (bf16[592,128]{1,0:T(8,128)(2,1)S(1)}, bf16[592,128]{1,0:T(8,128)(2,1)S(1)}, u32[]{:S(2)}, u32[]{:S(2)}) collective-permute-start(bf16[592,128]{1,0:T(8,128)(2,1)S(1)} %crossing.1.after), channel_id=1, source_target_pairs={{0,48},{32,80},{64,112},{96,144},{128,176},{160,208},{192,240},{48... | collective-permute-start | bytes 454664 | tf_op jit(solution)/shard_map/ppermute | solution.py:385
  4.0 4.8 %collective-permute-start.1 = (f32[72,512]{1,0:T(8,128)S(1)}, f32[72,512]{1,0:T(8,128)S(1)}, u32[]{:S(2)}, u32[]{:S(2)}) collective-permute-start(f32[72,512]{1,0:T(8,128)S(1)} %get-tuple-element.52), channel_id=1, source_target_pairs={{0,16},{16,0},{1,17},{17,1},{2,18},{18,2},{3,19},{19,3},{4,20},{20... | collective-permute-start | bytes 442376 | tf_op jit(solution)/shard_map/ppermute | solution.py:414
  7.2 1.6 %collective-permute-start.2 = (f32[72,512]{1,0:T(8,128)S(1)}, f32[72,512]{1,0:T(8,128)S(1)}, u32[]{:S(2)}, u32[]{:S(2)}) collective-permute-start(f32[72,512]{1,0:T(8,128)S(1)} %get-tuple-element.53), channel_id=1, source_target_pairs={{0,16},{16,0},{1,17},{17,1},{2,18},{18,2},{3,19},{19,3},{4,20},{20... | collective-permute-start | bytes 442376 | tf_op jit(solution)/shard_map/ppermute | solution.py:413
  7.3 13.2 %collective-permute-start.3 = (bf16[528,128]{1,0:T(8,128)(2,1)S(1)}, bf16[528,128]{1,0:T(8,128)(2,1)S(1)}, u32[]{:S(2)}, u32[]{:S(2)}) collective-permute-start(bf16[528,128]{1,0:T(8,128)(2,1)S(1)} %get-tuple-element.57), channel_id=1, source_target_pairs={{16,48},{48,80},{80,112},{112,144},{144,176},{176,208},{208,240},{... | collective-permute-start | bytes 405512 | tf_op jit(solution)/shard_map/ppermute | solution.py:415
  20.8 9.4 %collective-permute-start.4 = (bf16[4,16,512]{2,1,0:T(8,128)(2,1)S(1)}, bf16[4,16,512]{2,1,0:T(8,128)(2,1)S(1)}, u32[]{:S(2)}, u32[]{:S(2)}) collective-permute-start(bf16[4,16,512]{2,1,0:T(8,128)(2,1)S(1)} %get-tuple-element.60), channel_id=1, source_target_pairs={{0,16},{16,0},{1,17},{17,1},{2,18},{18,2},{3,19},{19,3},{4,20},{20... | collective-permute-start | bytes 196616 | tf_op jit(solution)/shard_map/ppermute | solution.py:436
  30.2 0.6 %copy-start.12 = (bf16[1,4,16,512]{3,2,1,0:T(8,128)(2,1)}, bf16[1,4,16,512]{3,2,1,0:T(8,128)(2,1)S(1)}, u32[]{:S(2)}) copy-start(bf16[1,4,16,512]{3,2,1,0:T(8,128)(2,1)S(1)} %get-tuple-element.75) | copy-start | bytes 196612

commit v10 on v9

--- a/solution.py
+++ b/solution.py
@@ -16,7 +16,8 @@
 
 
 def silu(value):
-    return value / (1.0 + jnp.exp(-value))
+    half = 0.5 * value
+    return half + half * jnp.tanh(half)
 
 
 def tap_rows(conv):

time: 31.4 us -> 31.4 us (level)
  no operation moved by 1% of the time
where the time goes in v10:
time: 31.4 us; the launch traced here: 30.8 us
  blocking collectives  20.5 us (65%)
  starting transfers between devices  7.06 us (22%)
  Pallas kernels  2.3 us (7%)
  local copies, waits for them, and re-layouts  0.68 us (2%)
    all_to_all x1, blocking collectives, body(): lax.all_to_all(sums, 'tp', 0, 0)  11.4 us
    all_to_all x1, blocking collectives, second_section(): sums = lax.all_to_all(sums, 'tp', 0, 0)  9.11 us
    ppermute x1, starting transfers between devices, body(): other_pack = lax.ppermute(pack, 'pipe', swap)  3.23 us
    ppermute x1, starting transfers between devices, body(): arrived = lax.ppermute(leaving, ('roll', 'pipe', 'tp'), first_moves)  2.13 us
    ppermute x1, starting transfers between devices, body(): later = lax.ppermute(leaving, ('roll', 'pipe', 'tp'), second_moves)  1.51 us
    pallas_call x1, Pallas kernels, body(): pl.pallas_call(local_kernel, out_shape=(step_rows, step_rows, shape((npai...  1.5 us
    unnamed x28, local copies, waits for them, and re-layouts  0.68 us
  transfers between devices with their start and end apart: 5, of which 0 were waited for; matrix products, arithmetic and copies ran while one was open for 0% of the time, Pallas kernels for 6%

profile of v10, /device:TPU:1, one launch (start us, length us, event | category | flops | bytes accessed | tf_op | source)
XLA Modules:
  0.0 30.8 jit_solution(1278129539647640176)
XLA Ops:
  0.1 0.1 crossing.1.after
  0.2 2.1 %collective-permute-start = (bf16[592,128]{1,0:T(8,128)(2,1)S(1)}, bf16[592,128]{1,0:T(8,128)(2,1)S(1)}, u32[]{:S(2)}, u32[]{:S(2)}) collective-permute-start(bf16[592,128]{1,0:T(8,128)(2,1)S(1)} %crossing.1.after), channel_id=1, source_target_pairs={{0,48},{32,80},{64,112},{96,144},{128,176},{160,208},{192,240},{48... | collective-permute-start | bytes 454664 | tf_op jit(solution)/shard_map/ppermute | solution.py:386
  2.3 0.0 copy-done.1
  2.4 1.5 %local.1 = (f32[4,16,512]{2,1,0:T(8,128)S(1)}, f32[4,16,512]{2,1,0:T(8,128)S(1)}, f32[10,16,512]{2,1,0:T(8,128)S(1)}, f32[3,16,512]{2,1,0:T(8,128)S(1)}, bf16[64...) custom-call(bf16[592,128]{1,0:T(8,128)(2,1)S(1)} %crossing.1.after, s32[128]{0:T(128)S(1)} %copy-done.7, ...), custom_call_target="tpu_custom_call" | custom-call | flops 20000000 | bytes 4000000 | tf_op jit(solution)/shard_map/local/pallas_call | solution.py:388
  3.9 0.0 copy-done.11
  3.9 0.0 copy-done.13
  4.0 3.2 %collective-permute-start.1 = (f32[72,512]{1,0:T(8,128)S(1)}, f32[72,512]{1,0:T(8,128)S(1)}, u32[]{:S(2)}, u32[]{:S(2)}) collective-permute-start(f32[72,512]{1,0:T(8,128)S(1)} %get-tuple-element.52), channel_id=1, source_target_pairs={{0,16},{16,0},{1,17},{17,1},{2,18},{18,2},{3,19},{19,3},{4,20},{20... | collective-permute-start | bytes 442376 | tf_op jit(solution)/shard_map/ppermute | solution.py:415
  7.2 0.1 collective-permute-start.2
  7.3 1.5 %collective-permute-start.3 = (bf16[528,128]{1,0:T(8,128)(2,1)S(1)}, bf16[528,128]{1,0:T(8,128)(2,1)S(1)}, u32[]{:S(2)}, u32[]{:S(2)}) collective-permute-start(bf16[528,128]{1,0:T(8,128)(2,1)S(1)} %get-tuple-element.57), channel_id=1, source_target_pairs={{16,48},{48,80},{80,112},{112,144},{144,176},{176,208},{208,240},{... | collective-permute-start | bytes 405512 | tf_op jit(solution)/shard_map/ppermute | solution.py:416
  8.8 0.0 collective-permute-done.1.refs_1_
  8.8 0.0 collective-permute-done.2.refs_2_
  8.8 0.0 collective-permute-done.refs_0_
  8.8 0.3 fill.1
  9.1 11.4 %conditional.3 = (f32[16,1,128]{2,1,0:T(1,128)S(1)}) conditional(s32[]{:T(128)} %convert_element_type.2, f32[16,1,128]{2,1,0:T(1,128)S(1)} %get-tuple-element.55, f32[16,1,128]{2,1,0:T(1,128)S(1)} %get-tuple-element.55), branch_computations={%region_0.0_spmd, %region_1.0_spmd} | conditional | bytes 32776 | solution.py:427
  9.1 11.4 %all_to_all.8 = f32[16,1,128]{2,1,0:T(1,128)S(1)} all-to-all(f32[16,1,128]{2,1,0:T(1,128)S(1)} %copy.23), channel_id=1, replica_groups=mesh['roll'=8,'pipe'=2,'tp'=16] {'tp'}, dimensions={0} | all-to-all | bytes 16384 | tf_op jit(solution)/shard_map/cond/branch_0_fun/all_to_all | solution.py:427
  20.5 0.0 collective-permute-done.3.refs_2_
  20.5 0.3 %second.1 = (bf16[4,16,512]{2,1,0:T(8,128)(2,1)S(1)}, f32[4,16,512]{2,1,0:T(8,128)S(1)}, f32[16,1,128]{2,1,0:T(1,128)S(1)}) custom-call(f32[16,1,128]{2,1,0:T(1,128)S(1)} %get-tuple-element.64.refs_0_, f32[4,16,512]{2,1,0:T(8,128)S(1)} %get-tuple-element.56.refs_1_, bf16[528,128]{1,0:T(8,128)(2,1)S(1)} %collective-permute-done.3.refs_2_, ...), custom_call_target="tpu_custom_call" | custom-call | tf_op jit(solution)/shard_map/second/pallas_call | solution.py:429
  20.8 0.1 collective-permute-start.4
  20.9 9.2 %conditional.4 = (bf16[4,16,512]{2,1,0:T(8,128)(2,1)S(1)}) conditional(s32[]{:T(128)} %convert_element_type.2, (f32[16,1,128]{2,1,0:T(1,128)S(1)}, f32[4,16,512]{2,1,0:T(8,128)S(1)}, f32[1,512]{1,0:T(1,128)S(1)}) %tuple.35, bf16[4,16,512]{2,1,0:T(8,128)(2,1)S(1)} %copy-done.11), branch_computations={%region_2.0_spmd, %region_3.0_spmd} | conditional | bytes 131080 | solution.py:450
  20.9 9.1 %all_to_all.9.sums = f32[16,1,128]{2,1,0:T(1,128)S(1)} all-to-all(f32[16,1,128]{2,1,0:T(1,128)S(1)} %get-tuple-element.28), channel_id=1, replica_groups=mesh['roll'=8,'pipe'=2,'tp'=16] {'tp'}, dimensions={0} | all-to-all | bytes 16384 | tf_op jit(solution)/shard_map/cond/branch_0_fun/all_to_all | solution.py:440
  30.0 0.1 last.1
  30.2 0.0 collective-permute-done.4
  30.2 0.0 copy-start.12
  30.2 0.6 %copy-done.12 = bf16[1,4,16,512]{3,2,1,0:T(8,128)(2,1)} copy-done((bf16[1,4,16,512]{3,2,1,0:T(8,128)(2,1)}, bf16[1,4,16,512]{3,2,1,0:T(8,128)(2,1)S(1)}, u32[]{:S(2)}) %copy-start.12) | copy-done | bytes 65560
  (26 shorter events, 0.1 us)
Async XLA Ops:
  0.0 2.3 %copy-start.7 = (s32[128]{0:T(128)S(1)}, s32[128]{0:T(128)}, u32[]{:S(2)}) copy-start(s32[128]{0:T(128)} %parent.1) | copy-start | bytes 1540
  0.0 2.3 %copy-start.1 = (bf16[1,16,3,512]{3,1,2,0:T(8,128)(2,1)S(1)}, bf16[1,16,3,512]{3,1,2,0:T(8,128)(2,1)}, u32[]{:S(2)}) copy-start(bf16[1,16,3,512]{3,1,2,0:T(8,128)(2,1)} %param.20) | copy-start | bytes 147460
  0.0 2.3 %copy-start = (bf16[1,16,8,64,128]{4,3,2,1,0:T(8,128)(2,1)S(1)}, bf16[1,16,8,64,128]{4,3,2,1,0:T(8,128)(2,1)}, u32[]{:S(2)}) copy-start(bf16[1,16,8,64,128]{4,3,2,1,0:T(8,128)(2,1)} %param.19) | copy-start | bytes 6291460
  0.0 2.3 %copy-start.10 = (f32[1,8]{1,0:T(1,128)S(1)}, f32[1,8]{1,0:T(1,128)}, u32[]{:S(2)}) copy-start(f32[1,8]{1,0:T(1,128)} %skip_d.1) | copy-start | bytes 100
  0.0 2.3 %copy-start.9 = (f32[1,8]{1,0:T(1,128)S(1)}, f32[1,8]{1,0:T(1,128)}, u32[]{:S(2)}) copy-start(f32[1,8]{1,0:T(1,128)} %dt_bias.1) | copy-start | bytes 100
  0.0 2.3 %copy-start.8 = (f32[1,8]{1,0:T(1,128)S(1)}, f32[1,8]{1,0:T(1,128)}, u32[]{:S(2)}) copy-start(f32[1,8]{1,0:T(1,128)} %a_log.1) | copy-start | bytes 100
  0.0 2.3 %copy-start.3 = (bf16[1,4,512]{2,1,0:T(4,128)(2,1)S(1)}, bf16[1,4,512]{2,1,0:T(4,128)(2,1)}, u32[]{:S(2)}) copy-start(bf16[1,4,512]{2,1,0:T(4,128)(2,1)} %param.26) | copy-start | bytes 12292
  0.0 2.3 %copy-start.4 = (bf16[1,4,16,128]{3,2,1,0:T(8,128)(2,1)S(1)}, bf16[1,4,16,128]{3,2,1,0:T(8,128)(2,1)}, u32[]{:S(2)}) copy-start(bf16[1,4,16,128]{3,2,1,0:T(8,128)(2,1)} %param.25) | copy-start | bytes 49156
  0.1 2.3 %copy-start.5 = (bf16[1,4,16,128]{3,2,1,0:T(8,128)(2,1)S(1)}, bf16[1,4,16,128]{3,2,1,0:T(8,128)(2,1)}, u32[]{:S(2)}) copy-start(bf16[1,4,16,128]{3,2,1,0:T(8,128)(2,1)} %param.24) | copy-start | bytes 49156
  0.1 2.3 %copy-start.6 = (f32[1,4,16,8]{2,3,1,0:T(8,128)S(1)}, f32[1,4,16,8]{2,3,1,0:T(8,128)}, u32[]{:S(2)}) copy-start(f32[1,4,16,8]{2,3,1,0:T(8,128)} %param.23) | copy-start | bytes 6148
  0.1 2.3 %copy-start.2 = (bf16[1,4,16,512]{3,2,1,0:T(8,128)(2,1)S(1)}, bf16[1,4,16,512]{3,2,1,0:T(8,128)(2,1)}, u32[]{:S(2)}) copy-start(bf16[1,4,16,512]{3,2,1,0:T(8,128)(2,1)} %param.22) | copy-start | bytes 196612
  0.1 3.8 %copy-start.11 = (bf16[4,16,512]{2,1,0:T(8,128)(2,1)S(1)}, bf16[4,16,512]{2,1,0:T(8,128)(2,1)}, u32[]{:S(2)}) copy-start(bf16[4,16,512]{2,1,0:T(8,128)(2,1)} %x_in.1) | copy-start | bytes 196612
  0.1 3.8 %copy-start.13 = (f32[1,512]{1,0:T(1,128)S(1)}, f32[1,512]{1,0:T(1,128)}, u32[]{:S(2)}) copy-start(f32[1,512]{1,0:T(1,128)} %gain.1) | copy-start | bytes 6148
  0.2 8.6 %collective-permute-start = (bf16[592,128]{1,0:T(8,128)(2,1)S(1)}, bf16[592,128]{1,0:T(8,128)(2,1)S(1)}, u32[]{:S(2)}, u32[]{:S(2)}) collective-permute-start(bf16[592,128]{1,0:T(8,128)(2,1)S(1)} %crossing.1.after), channel_id=1, source_target_pairs={{0,48},{32,80},{64,112},{96,144},{128,176},{160,208},{192,240},{48... | collective-permute-start | bytes 454664 | tf_op jit(solution)/shard_map/ppermute | solution.py:386
  4.0 4.8 %collective-permute-start.1 = (f32[72,512]{1,0:T(8,128)S(1)}, f32[72,512]{1,0:T(8,128)S(1)}, u32[]{:S(2)}, u32[]{:S(2)}) collective-permute-start(f32[72,512]{1,0:T(8,128)S(1)} %get-tuple-element.52), channel_id=1, source_target_pairs={{0,16},{16,0},{1,17},{17,1},{2,18},{18,2},{3,19},{19,3},{4,20},{20... | collective-permute-start | bytes 442376 | tf_op jit(solution)/shard_map/ppermute | solution.py:415
  7.2 1.6 %collective-permute-start.2 = (f32[72,512]{1,0:T(8,128)S(1)}, f32[72,512]{1,0:T(8,128)S(1)}, u32[]{:S(2)}, u32[]{:S(2)}) collective-permute-start(f32[72,512]{1,0:T(8,128)S(1)} %get-tuple-element.53), channel_id=1, source_target_pairs={{0,16},{16,0},{1,17},{17,1},{2,18},{18,2},{3,19},{19,3},{4,20},{20... | collective-permute-start | bytes 442376 | tf_op jit(solution)/shard_map/ppermute | solution.py:414
  7.3 13.2 %collective-permute-start.3 = (bf16[528,128]{1,0:T(8,128)(2,1)S(1)}, bf16[528,128]{1,0:T(8,128)(2,1)S(1)}, u32[]{:S(2)}, u32[]{:S(2)}) collective-permute-start(bf16[528,128]{1,0:T(8,128)(2,1)S(1)} %get-tuple-element.57), channel_id=1, source_target_pairs={{16,48},{48,80},{80,112},{112,144},{144,176},{176,208},{208,240},{... | collective-permute-start | bytes 405512 | tf_op jit(solution)/shard_map/ppermute | solution.py:416
  20.8 9.4 %collective-permute-start.4 = (bf16[4,16,512]{2,1,0:T(8,128)(2,1)S(1)}, bf16[4,16,512]{2,1,0:T(8,128)(2,1)S(1)}, u32[]{:S(2)}, u32[]{:S(2)}) collective-permute-start(bf16[4,16,512]{2,1,0:T(8,128)(2,1)S(1)} %get-tuple-element.60), channel_id=1, source_target_pairs={{0,16},{16,0},{1,17},{17,1},{2,18},{18,2},{3,19},{19,3},{4,20},{20... | collective-permute-start | bytes 196616 | tf_op jit(solution)/shard_map/ppermute | solution.py:437
  30.2 0.6 %copy-start.12 = (bf16[1,4,16,512]{3,2,1,0:T(8,128)(2,1)}, bf16[1,4,16,512]{3,2,1,0:T(8,128)(2,1)S(1)}, u32[]{:S(2)}) copy-start(bf16[1,4,16,512]{3,2,1,0:T(8,128)(2,1)S(1)} %get-tuple-element.75) | copy-start | bytes 196612
